TPU v7x, 32 devices: a whole 2x2x4 slice. The times are simulated.
32 devices in a mesh: grp: 4 (over y, core), tp: 8 (over z, x).
Axes of the slice: x: 2, y: 2, z: 4, core: 2. Of those that a mesh axis runs over, the one named last changes fastest.
Arguments:
- queries: bfloat16 [4, 130, 8192], P('grp', None, 'tp'), may hold values from -24 to 24
- new_kv: bfloat16 [4, 128, 2048], P('grp', 'tp'), may hold values from -6 to 6
- decode_kv: bfloat16 [4, 2, 2048], P('grp'), may hold values from -6 to 6
- pool: bfloat16 [768, 16, 2048], P(('grp', 'tp')), may hold values from -12 to 12
- hist_pages: int32 [4], replicated, may hold values from 1 to 192, 384 in all
- owner: int32 [4], replicated, may hold values from 0 to 3, as said below
- block_table: int32 [4, 192], replicated, may hold values from 0 to 23, as said below
Outputs:
- attended: bfloat16 [4, 130, 8192], P('grp', None, 'tp')
- returned: bfloat16 [4, 128, 2048], P('grp', None, 'tp')
Inputs may be any that keep to these rules, and one draw needn't show every extreme that they name: `hist_pages`: in every draw one session has exactly 192 pages, and the counts add up to 384. `owner`: each group owns exactly one session; in every draw some session s is owned by group (s + 2) mod 4. block_table[s, p] lies in [s * 6, (s + 1) * 6); the pages of one session on one device take distinct slots.
All inputs are finite; a program needn't handle non-finite values.
Results may differ from a plain program's by a relative error of at most 0.001.
Values may be sent and summed in bfloat16 or wider, within the bound.
No kernel may reach another device: no remote copies, remote signals or barrier semaphores. Data moves between devices by JAX's collectives and lax.ppermute only.
A program may use at most 320 MiB of HBM per device.

v0:
```python
import jax
import jax.numpy as jnp
import numpy as np
from jax import lax
from jax.sharding import PartitionSpec as P

H = 64
KVH = 8
HD = 128


NEG_FLOOR = -1e30


def page_index(source_group, session_owner, span_number, tp_rank, groups, ways):
    return ((source_group - session_owner) % groups + span_number * groups) * ways + tp_rank


def init_carry(rows, heads_here, head_dim):
    return (
        jnp.zeros((rows, heads_here, head_dim), jnp.float32),
        jnp.full((rows, heads_here), NEG_FLOOR, jnp.float32),
        jnp.zeros((rows, heads_here), jnp.float32),
    )


def online_block(carry, query, keys, values, visible, scale):
    running, maximum, totals = carry
    score = jnp.einsum("rnd,kd->rnk", query, keys, preferred_element_type=jnp.float32) * scale
    score = jnp.where(visible[:, None, :], score, NEG_FLOOR)
    new_max = jnp.maximum(maximum, jnp.max(score, axis=2))
    weight = jnp.where(visible[:, None, :], jnp.exp(score - new_max[:, :, None]), 0.0)
    shrink = jnp.exp(maximum - new_max)
    totals = totals * shrink + jnp.sum(weight, axis=2)
    running = running * shrink[:, :, None] + jnp.einsum(
        "rnk,kd->rnd", weight, values.astype(jnp.float32), precision=lax.Precision.HIGHEST
    )
    return (running, new_max, totals)


def on_device(queries, new_kv, decode_kv, pool, hist_pages, owner, block_table):
    groups = lax.axis_size("grp")
    ways = lax.axis_size("tp")
    my_group = lax.axis_index("grp")
    tp_rank = lax.axis_index("tp")
    head_dim = HD
    kv_heads = KVH
    heads_here = H // ways
    capacity = pool.shape[0] // groups
    page_rows = pool.shape[1]
    query_rows = queries.shape[1]
    local_new = new_kv.shape[1]
    fresh_count = local_new * ways
    decode_count = decode_kv.shape[1]
    scale = head_dim ** (-0.5)
    session_owner = owner[my_group]
    pages_used = hist_pages[my_group]
    span_ids = jnp.arange(capacity, dtype=jnp.int32)
    group_ids = jnp.arange(groups, dtype=jnp.int32)
    query_pos = jnp.arange(query_rows, dtype=jnp.int32)
    wanted = page_index(my_group, owner[:, None], span_ids[None, :], tp_rank, groups, ways)
    slots = jnp.take_along_axis(block_table, wanted, axis=1)
    outgoing = pool[slots]
    repeat_by = ways // kv_heads
    head_pick = np.arange(ways) // repeat_by
    spread = outgoing.reshape(groups, capacity, page_rows, 2, kv_heads, head_dim)[
        :, :, :, :, head_pick, :
    ]
    spread = jnp.transpose(spread, (0, 1, 2, 4, 3, 5)).reshape(
        groups, capacity, page_rows, ways * 2 * head_dim
    )
    arrived = lax.all_to_all(
        lax.all_to_all(spread, "grp", split_axis=0, concat_axis=0, tiled=True),
        "tp",
        split_axis=3,
        concat_axis=1,
        tiled=True,
    )
    source_rank = jnp.arange(ways * capacity, dtype=jnp.int32) // capacity
    source_span = jnp.arange(ways * capacity, dtype=jnp.int32) % capacity
    page_of = page_index(
        group_ids[:, None], session_owner, source_span[None, :], source_rank[None, :], groups, ways
    )
    page_live = page_of < pages_used
    own_q = queries[0].reshape(query_rows, heads_here, head_dim)

    def scan_step(carry, inputs):
        block, live = inputs
        rows = block.reshape(-1, 2 * head_dim)
        seen = jnp.broadcast_to(
            jnp.broadcast_to(live[:, None], (live.shape[0], page_rows)).reshape(-1)[None, :],
            (query_rows, rows.shape[0]),
        )
        return (
            online_block(carry, own_q, rows[:, :head_dim], rows[:, head_dim:], seen, scale),
            None,
        )

    carry, unused = lax.scan(
        scan_step, init_carry(query_rows, heads_here, head_dim), (arrived, page_live)
    )
    fresh_all = lax.all_gather(new_kv, "tp", axis=1, tiled=True)[0]
    fresh_block = jnp.concatenate([fresh_all, decode_kv[0]], axis=0)
    my_head = tp_rank // repeat_by
    key_cols = lax.dynamic_slice_in_dim(fresh_block, my_head * head_dim, head_dim, 1)
    value_cols = lax.dynamic_slice_in_dim(fresh_block, (kv_heads + my_head) * head_dim, head_dim, 1)
    fresh_pos = jnp.arange(fresh_count + decode_count, dtype=jnp.int32)
    carry = online_block(
        carry, own_q, key_cols, value_cols, fresh_pos[None, :] <= query_pos[:, None], scale
    )
    attended = (
        (carry[0] / carry[2][:, :, None])
        .reshape(1, query_rows, heads_here * head_dim)
        .astype(jnp.bfloat16)
    )
    homeward = jnp.where(
        (group_ids == session_owner)[:, None, None], new_kv, jnp.zeros((), new_kv.dtype)
    )
    split_rows = lax.all_to_all(homeward, "tp", split_axis=2, concat_axis=1, tiled=True)
    landed = lax.all_to_all(split_rows, "grp", split_axis=0, concat_axis=0, tiled=True)
    sender = (owner == my_group)[:, None, None]
    returned = jnp.sum(
        jnp.where(sender, landed.astype(jnp.float32), 0.0), axis=0, keepdims=True
    ).astype(jnp.bfloat16)
    return (attended, returned)


def solution(mesh):
    return jax.shard_map(
        on_device,
        mesh=mesh,
        in_specs=(
            P("grp", None, "tp"),
            P("grp", "tp", None),
            P("grp", None, None),
            P(("grp", "tp"), None, None),
            P(),
            P(),
            P(),
        ),
        out_specs=(P("grp", None, "tp"), P("grp", None, "tp")),
        check_vma=False,
    )
```

profile of v0, /device:TPU:0, one launch (start us, length us, event | category | flops | bytes accessed | tf_op | source)
XLA Modules:
  0.0 227.5 jit_solution(15997347059966600801)
XLA Ops:
  3.8 2.2 fusion.43
  6.0 4.1 %reshape.294 = bf16[8,2,8192]{2,1,0:T(2,128)(2,1)} reshape(bf16[2048,4,16]{2,1,0:T(4,128)(2,1)} %fusion.43) | data formatting | bytes 524288
  10.0 7.3 %all-to-all-start.2 = ((bf16[8,2,8192]{2,1,0:T(2,128)(2,1)}), bf16[8,2,8192]{2,1,0:T(2,128)(2,1)S(1)}, u32[]{:S(2)}, u32[]{:S(2)}) async-start(bf16[8,2,8192]{2,1,0:T(2,128)(2,1)} %reshape.294), calls=%async_computation.2 | async-start | bytes 524288 | tf_op jit(solution)/shard_map/all_to_all | solution.py:119
  20.8 2.0 gather_fusion.1
  22.8 3.1 %copy.52 = bf16[4,6,16,8,2,128]{5,4,3,2,1,0:T(2,128)(2,1)S(1)} copy(bf16[4,6,16,8,2,128]{5,2,4,1,0,3:T(8,128)(2,1)} %bitcast.95) | data formatting | bytes 3145728 | tf_op jit(solution)/shard_map/transpose | solution.py:69
  25.9 2.4 %reshape.260 = bf16[4,6,16,2048]{3,2,1,0:T(8,128)(2,1)} reshape(bf16[4,6,16,8,2,128]{5,4,3,2,1,0:T(2,128)(2,1)S(1)} %copy.52) | data formatting | bytes 3145728 | tf_op jit(solution)/shard_map/reshape | solution.py:69
  28.3 3.6 %all-to-all-start = ((bf16[4,6,16,2048]{3,2,1,0:T(8,128)(2,1)}), bf16[4,6,16,2048]{3,2,1,0:T(8,128)(2,1)S(1)}, u32[]{:S(2)}, u32[]{:S(2)}) async-start(bf16[4,6,16,2048]{3,2,1,0:T(8,128)(2,1)} %reshape.260), calls=%async_computation | async-start | bytes 3145728 | tf_op jit(solution)/shard_map/all_to_all | solution.py:73
  31.8 2.4 %reshape.295 = bf16[2048,4,16]{2,1,0:T(4,128)(2,1)} reshape(bf16[8,2,8192]{2,1,0:T(2,128)(2,1)S(1)} %all-to-all-done.2) | data formatting | bytes 524288
  34.3 3.9 %copy.67 = bf16[4,16,8,256]{3,1,2,0:T(8,128)(2,1)} copy(bf16[4,16,8,256]{1,0,3,2:T(4,128)(2,1)} %bitcast.92) | data formatting | bytes 524288 | tf_op jit(solution)/shard_map/all_to_all | solution.py:119
  38.1 13.8 %all-to-all-done = bf16[4,6,16,2048]{3,2,1,0:T(8,128)(2,1)S(1)} async-done(((bf16[4,6,16,2048]{3,2,1,0:T(8,128)(2,1)}), bf16[4,6,16,2048]{3,2,1,0:T(8,128)(2,1)S(1)}, u32[]{:S(2)}, u32[]{:S(2)}) %all-to-all-start) | async-done | bytes 1572896 | tf_op jit(solution)/shard_map/all_to_all | solution.py:73
  51.9 3.4 %all-to-all-start.3 = ((bf16[4,128,256]{2,1,0:T(8,128)(2,1)}), bf16[4,128,256]{2,1,0:T(8,128)(2,1)S(1)}, u32[]{:S(2)}, u32[]{:S(2)}) async-start(bf16[4,128,256]{2,1,0:T(8,128)(2,1)} %bitcast.16), calls=%async_computation.3 | async-start | bytes 524288 | tf_op jit(solution)/shard_map/all_to_all | solution.py:120
  55.3 14.0 %copy.53 = bf16[4,6,16,2048]{2,0,1,3:T(4,128)(2,1)} copy(bf16[4,6,16,2048]{3,2,1,0:T(8,128)(2,1)S(1)} %all-to-all-done) | data formatting | bytes 3145728 | tf_op jit(solution)/shard_map/all_to_all | solution.py:73
  69.3 14.9 %reshape.292 = bf16[8,2,49152]{2,1,0:T(2,128)(2,1)} reshape(bf16[2048,6,4,16]{3,2,1,0:T(4,128)(2,1)} %bitcast.88) | data formatting | bytes 3145728
  84.9 6.0 %all-to-all-start.1 = ((bf16[8,2,49152]{2,1,0:T(2,128)(2,1)}), bf16[8,2,49152]{2,1,0:T(2,128)(2,1)S(1)}, u32[]{:S(2)}, u32[]{:S(2)}) async-start(bf16[8,2,49152]{2,1,0:T(2,128)(2,1)} %reshape.292), calls=%async_computation.1 | async-start | bytes 3145728 | tf_op jit(solution)/shard_map/all_to_all | solution.py:72
  94.5 55.4 %all_gather.3 = bf16[1,128,2048]{2,1,0:T(8,128)(2,1)S(1)} all-gather(bf16[1,16,2048]{2,1,0:T(8,128)(2,1)S(1)} %copy-done.9), channel_id=1, replica_groups=mesh['grp'=4,'tp'=8] {'tp'}, dimensions={1}, use_global_device_ids=true | all-gather | bytes 589824 | tf_op jit(solution)/shard_map/all_gather | solution.py:102
  149.9 2.4 %fusion.42 = (f32[130,8]{0,1:T(8,128)S(1)}, f32[130,8,130]{0,2,1:T(8,128)}) fusion(bf16[130,8,128]{2,1,0:T(8,128)(2,1)} %copy-done.4, s32[]{:T(128)S(6)} %select_n.123, bf16[2,2048]{1,0:T(2,128)(2,1)S(1)} %bitcast.103, bf16[128,2048]{1,0:T(8,128)(2,1)S(1)} %bitcast.97, pred[130,130]{0,1:T(8,128)(4,1)S(1)} %iota_compare_fusion), kind=kOutput, calls=%fused_computation.84 | convolution fusion | flops 35082320 | bytes 1360584 | tf_op jit(solution)/shard_map/rnd,kd->rnk/dot_general | solution.py:29
  153.1 10.3 %reshape.293 = bf16[2048,6,4,16]{3,2,1,0:T(4,128)(2,1)} reshape(bf16[8,2,49152]{2,1,0:T(2,128)(2,1)S(1)} %all-to-all-done.1) | data formatting | bytes 3145728
  163.4 17.7 %copy.65 = bf16[4,6,16,8,256]{4,2,1,3,0:T(8,128)(2,1)} copy(bf16[4,6,16,8,256]{2,0,1,4,3:T(4,128)(2,1)} %bitcast.89) | data formatting | bytes 3145728 | tf_op jit(solution)/shard_map/all_to_all | solution.py:72
  181.1 42.5 %while.15 = (s32[]{:T(128)}, f32[130,8,128]{2,0,1:T(8,128)}, f32[130,8]{0,1:T(8,128)S(1)}, f32[130,8]{0,1:T(8,128)S(1)}, pred[4,48]{1,0:T(4,128)(4,1)S(1)}, /*in...) while((s32[]{:T(128)}, f32[130,8,128]{2,0,1:T(8,128)}, ...), condition=%wide.region_3.4_spmd.clone, body=%wide.region_0.0_spmd.clone.sunk | while | flops 1441295488 | bytes 25115800 | solution.py:99
  182.4 2.3 %bitcast_reduce_fusion.2 = (f32[130,8]{0,1:T(8,128)S(1)}, f32[768,130,8]{0,1,2:T(8,128)}) fusion(pred[768]{0:T(1024)(128)(4,1)S(1)} %reshape.297, bf16[130,8,128]{2,0,1:T(8,128)(2,1)S(1)} %get-tuple-element.204, bf16[768,256]{1,0:T(8,128)(2,1)S(1)} %bitcast.90), kind=kOutput, calls=%fused_computation.4.clone.1 | convolution fusion | flops 206867440 | bytes 3675200 | tf_op jit(solution)/shard_map/while/body/eval_jaxpr/rnd,kd->rnk/dot_general | solution.py:29
  184.8 3.1 %fusion.52 = f32[130,8]{0,1:T(8,128)S(1)} fusion(f32[768,130,8]{0,1,2:T(8,128)} %get-tuple-element.176, f32[130,8]{0,1:T(8,128)S(1)} %select_maximum_fusion.2, pred[768]{0:T(1024)(128)(4,1)S(1)} %reshape.297), kind=kLoop, calls=%fused_computation.8.clone.1 | loop fusion | flops 3992560 | bytes 3203968 | tf_op jit(solution)/shard_map/while/body/eval_jaxpr/reduce_sum | solution.py:34
  187.9 3.1 %fusion.54 = f32[130,8,128]{2,0,1:T(8,128)} fusion(f32[768,130,8]{0,1,2:T(8,128)S(1)} %copy-done.2, f32[130,8]{0,1:T(8,128)S(1)} %select_maximum_fusion.2, pred[768]{0:T(1024)(128)(4,1)S(1)} %reshape.297, f32[130,8,128]{2,0,1:T(8,128)} %get-tuple-element.190, f32[130,8]{0,1:T(8,128)S(1)} %get-tuple-element.178, pred[]{:T(512)S(6)} %compare.9, ...), kind=kOutput, calls=%fused_computation.16.clone.1 | convolution fusion | flops 1230428160 | bytes 4622337 | tf_op jit(solution)/shard_map/while/body/eval_jaxpr/rnk,kd->rnd/dot_general | solution.py:35
  192.2 2.3 %bitcast_reduce_fusion.2 = (f32[130,8]{0,1:T(8,128)S(1)}, f32[768,130,8]{0,1,2:T(8,128)}) fusion(pred[768]{0:T(1024)(128)(4,1)S(1)} %reshape.297, bf16[130,8,128]{2,0,1:T(8,128)(2,1)S(1)} %get-tuple-element.204, bf16[768,256]{1,0:T(8,128)(2,1)S(1)} %bitcast.90), kind=kOutput, calls=%fused_computation.4.clone.1 | convolution fusion | flops 206867440 | bytes 3675200 | tf_op jit(solution)/shard_map/while/body/eval_jaxpr/rnd,kd->rnk/dot_general | solution.py:29
  194.6 3.1 %fusion.52 = f32[130,8]{0,1:T(8,128)S(1)} fusion(f32[768,130,8]{0,1,2:T(8,128)} %get-tuple-element.176, f32[130,8]{0,1:T(8,128)S(1)} %select_maximum_fusion.2, pred[768]{0:T(1024)(128)(4,1)S(1)} %reshape.297), kind=kLoop, calls=%fused_computation.8.clone.1 | loop fusion | flops 3992560 | bytes 3203968 | tf_op jit(solution)/shard_map/while/body/eval_jaxpr/reduce_sum | solution.py:34
  197.7 4.2 %fusion.54 = f32[130,8,128]{2,0,1:T(8,128)} fusion(f32[768,130,8]{0,1,2:T(8,128)S(1)} %copy-done.2, f32[130,8]{0,1:T(8,128)S(1)} %select_maximum_fusion.2, pred[768]{0:T(1024)(128)(4,1)S(1)} %reshape.297, f32[130,8,128]{2,0,1:T(8,128)} %get-tuple-element.190, f32[130,8]{0,1:T(8,128)S(1)} %get-tuple-element.178, pred[]{:T(512)S(6)} %compare.9, ...), kind=kOutput, calls=%fused_computation.16.clone.1 | convolution fusion | flops 1230428160 | bytes 4622337 | tf_op jit(solution)/shard_map/while/body/eval_jaxpr/rnk,kd->rnd/dot_general | solution.py:35
  203.1 2.3 %bitcast_reduce_fusion.2 = (f32[130,8]{0,1:T(8,128)S(1)}, f32[768,130,8]{0,1,2:T(8,128)}) fusion(pred[768]{0:T(1024)(128)(4,1)S(1)} %reshape.297, bf16[130,8,128]{2,0,1:T(8,128)(2,1)S(1)} %get-tuple-element.204, bf16[768,256]{1,0:T(8,128)(2,1)S(1)} %bitcast.90), kind=kOutput, calls=%fused_computation.4.clone.1 | convolution fusion | flops 206867440 | bytes 3675200 | tf_op jit(solution)/shard_map/while/body/eval_jaxpr/rnd,kd->rnk/dot_general | solution.py:29
  205.5 3.1 %fusion.52 = f32[130,8]{0,1:T(8,128)S(1)} fusion(f32[768,130,8]{0,1,2:T(8,128)} %get-tuple-element.176, f32[130,8]{0,1:T(8,128)S(1)} %select_maximum_fusion.2, pred[768]{0:T(1024)(128)(4,1)S(1)} %reshape.297), kind=kLoop, calls=%fused_computation.8.clone.1 | loop fusion | flops 3992560 | bytes 3203968 | tf_op jit(solution)/shard_map/while/body/eval_jaxpr/reduce_sum | solution.py:34
  208.6 4.2 %fusion.54 = f32[130,8,128]{2,0,1:T(8,128)} fusion(f32[768,130,8]{0,1,2:T(8,128)S(1)} %copy-done.2, f32[130,8]{0,1:T(8,128)S(1)} %select_maximum_fusion.2, pred[768]{0:T(1024)(128)(4,1)S(1)} %reshape.297, f32[130,8,128]{2,0,1:T(8,128)} %get-tuple-element.190, f32[130,8]{0,1:T(8,128)S(1)} %get-tuple-element.178, pred[]{:T(512)S(6)} %compare.9, ...), kind=kOutput, calls=%fused_computation.16.clone.1 | convolution fusion | flops 1230428160 | bytes 4622337 | tf_op jit(solution)/shard_map/while/body/eval_jaxpr/rnk,kd->rnd/dot_general | solution.py:35
  214.0 2.3 %bitcast_reduce_fusion.2 = (f32[130,8]{0,1:T(8,128)S(1)}, f32[768,130,8]{0,1,2:T(8,128)}) fusion(pred[768]{0:T(1024)(128)(4,1)S(1)} %reshape.297, bf16[130,8,128]{2,0,1:T(8,128)(2,1)S(1)} %get-tuple-element.204, bf16[768,256]{1,0:T(8,128)(2,1)S(1)} %bitcast.90), kind=kOutput, calls=%fused_computation.4.clone.1 | convolution fusion | flops 206867440 | bytes 3675200 | tf_op jit(solution)/shard_map/while/body/eval_jaxpr/rnd,kd->rnk/dot_general | solution.py:29
  216.3 3.1 %fusion.52 = f32[130,8]{0,1:T(8,128)S(1)} fusion(f32[768,130,8]{0,1,2:T(8,128)} %get-tuple-element.176, f32[130,8]{0,1:T(8,128)S(1)} %select_maximum_fusion.2, pred[768]{0:T(1024)(128)(4,1)S(1)} %reshape.297), kind=kLoop, calls=%fused_computation.8.clone.1 | loop fusion | flops 3992560 | bytes 3203968 | tf_op jit(solution)/shard_map/while/body/eval_jaxpr/reduce_sum | solution.py:34
  219.5 4.2 %fusion.54 = f32[130,8,128]{2,0,1:T(8,128)} fusion(f32[768,130,8]{0,1,2:T(8,128)S(1)} %copy-done.2, f32[130,8]{0,1:T(8,128)S(1)} %select_maximum_fusion.2, pred[768]{0:T(1024)(128)(4,1)S(1)} %reshape.297, f32[130,8,128]{2,0,1:T(8,128)} %get-tuple-element.190, f32[130,8]{0,1:T(8,128)S(1)} %get-tuple-element.178, pred[]{:T(512)S(6)} %compare.9, ...), kind=kOutput, calls=%fused_computation.16.clone.1 | convolution fusion | flops 1230428160 | bytes 4622337 | tf_op jit(solution)/shard_map/while/body/eval_jaxpr/rnk,kd->rnd/dot_general | solution.py:35
  223.9 2.7 %fusion.22 = bf16[130,8,128]{2,0,1:T(8,128)(2,1)S(1)} fusion(f32[130,8,130]{0,2,1:T(8,128)S(1)} %copy-done.3, f32[130,8]{0,1:T(8,128)S(1)} %max.6, f32[130,8,128]{2,0,1:T(8,128)} %get-tuple-element.41, pred[130,130]{0,1:T(8,128)(4,1)S(1)} %iota_compare_fusion, f32[130,8]{0,1:T(8,128)S(1)} %get-tuple-element.119, f32[130,8]{0,1:T(8,128)S(1)} %get-tuple-element.120, ...), kind=kOutput, calls=%fused_computation.36 | convolution fusion | flops 208536640 | bytes 1901384 | tf_op jit(solution)/shard_map/rnk,kd->rnd/dot_general | solution.py:35
  (99 shorter events, 17.6 us)
Async XLA Ops:
  0.6 18.6 %copy-start = (bf16[24,16,2048]{2,1,0:T(8,128)(2,1)S(1)}, bf16[24,16,2048]{2,1,0:T(8,128)(2,1)}, u32[]{:S(2)}) copy-start(bf16[24,16,2048]{2,1,0:T(8,128)(2,1)} %param.14) | copy-start | bytes 4718596
  6.0 11.3 %copy-start.11 = (s32[4]{0:T(128)S(1)}, s32[4]{0:T(128)}, u32[]{:S(2)}) copy-start(s32[4]{0:T(128)} %param.16) | copy-start | bytes 52
  6.0 12.2 %copy-start.1 = (s32[4,192]{1,0:T(4,128)S(1)}, s32[4,192]{1,0:T(4,128)}, u32[]{:S(2)}) copy-start(s32[4,192]{1,0:T(4,128)} %param.17) | copy-start | bytes 9220
  10.0 18.3 %all-to-all-start.2 = ((bf16[8,2,8192]{2,1,0:T(2,128)(2,1)}), bf16[8,2,8192]{2,1,0:T(2,128)(2,1)S(1)}, u32[]{:S(2)}, u32[]{:S(2)}) async-start(bf16[8,2,8192]{2,1,0:T(2,128)(2,1)} %reshape.294), calls=%async_computation.2 | async-start | bytes 524288 | tf_op jit(solution)/shard_map/all_to_all | solution.py:119
  28.3 23.6 %all-to-all-start = ((bf16[4,6,16,2048]{3,2,1,0:T(8,128)(2,1)}), bf16[4,6,16,2048]{3,2,1,0:T(8,128)(2,1)S(1)}, u32[]{:S(2)}, u32[]{:S(2)}) async-start(bf16[4,6,16,2048]{3,2,1,0:T(8,128)(2,1)} %reshape.260), calls=%async_computation | async-start | bytes 3145728 | tf_op jit(solution)/shard_map/all_to_all | solution.py:73
  51.9 32.3 %all-to-all-start.3 = ((bf16[4,128,256]{2,1,0:T(8,128)(2,1)}), bf16[4,128,256]{2,1,0:T(8,128)(2,1)S(1)}, u32[]{:S(2)}, u32[]{:S(2)}) async-start(bf16[4,128,256]{2,1,0:T(8,128)(2,1)} %bitcast.16), calls=%async_computation.3 | async-start | bytes 524288 | tf_op jit(solution)/shard_map/all_to_all | solution.py:120
  84.2 6.8 %copy-start.13 = (s32[4]{0:T(128)S(1)}, s32[4]{0:T(128)}, u32[]{:S(2)}) copy-start(s32[4]{0:T(128)} %param.15) | copy-start | bytes 52
  84.2 7.4 %copy-start.8 = (bf16[1,130,1024]{2,1,0:T(8,128)(2,1)S(1)}, bf16[1,130,1024]{2,1,0:T(8,128)(2,1)}, u32[]{:S(2)}) copy-start(bf16[1,130,1024]{2,1,0:T(8,128)(2,1)} %param.11) | copy-start | bytes 798724
  84.2 0.7 copy-start.6
  84.9 68.1 %all-to-all-start.1 = ((bf16[8,2,49152]{2,1,0:T(2,128)(2,1)}), bf16[8,2,49152]{2,1,0:T(2,128)(2,1)S(1)}, u32[]{:S(2)}, u32[]{:S(2)}) async-start(bf16[8,2,49152]{2,1,0:T(2,128)(2,1)} %reshape.292), calls=%async_computation.1 | async-start | bytes 3145728 | tf_op jit(solution)/shard_map/all_to_all | solution.py:72
  90.9 3.5 %copy-start.9 = (bf16[1,16,2048]{2,1,0:T(8,128)(2,1)S(1)}, bf16[1,16,2048]{2,1,0:T(8,128)(2,1)}, u32[]{:S(2)}) copy-start(bf16[1,16,2048]{2,1,0:T(8,128)(2,1)} %param.12) | copy-start | bytes 196612
  90.9 58.9 %copy-start.10 = (bf16[1,2,2048]{2,1,0:T(2,128)(2,1)S(1)}, bf16[1,2,2048]{2,1,0:T(2,128)(2,1)}, u32[]{:S(2)}) copy-start(bf16[1,2,2048]{2,1,0:T(2,128)(2,1)} %param.13) | copy-start | bytes 24580
  91.7 0.7 copy-start.4
  92.4 59.9 %copy-start.7 = (bf16[4,128,256]{2,1,0:T(8,128)(2,1)S(1)}, bf16[4,128,256]{2,1,0:T(8,128)(2,1)}, u32[]{:S(2)}) copy-start(bf16[4,128,256]{2,1,0:T(8,128)(2,1)} %copy-done.6) | copy-start | bytes 786436
  149.9 2.5 %copy-start.5 = (bf16[1,128,2048]{2,1,0:T(8,128)(2,1)}, bf16[1,128,2048]{2,1,0:T(8,128)(2,1)S(1)}, u32[]{:S(2)}) copy-start(bf16[1,128,2048]{2,1,0:T(8,128)(2,1)S(1)} %all_gather.3) | copy-start | bytes 1572868
  163.4 17.7 %copy-start.12 = (pred[4,48]{1,0:T(4,128)(4,1)S(1)}, pred[4,48]{1,0:T(4,128)(4,1)}, u32[]{:S(2)}) copy-start(pred[4,48]{1,0:T(4,128)(4,1)} %add_compare_fusion) | copy-start | bytes 580
  181.1 42.5 %copy-start.3 = (f32[130,8,130]{0,2,1:T(8,128)S(1)}, f32[130,8,130]{0,2,1:T(8,128)}, u32[]{:S(2)}) copy-start(f32[130,8,130]{0,2,1:T(8,128)} %get-tuple-element.124) | copy-start | bytes 1622404
  184.8 3.1 %copy-start.2 = (f32[768,130,8]{0,1,2:T(8,128)S(1)}, f32[768,130,8]{0,1,2:T(8,128)}, u32[]{:S(2)}) copy-start(f32[768,130,8]{0,1,2:T(8,128)} %get-tuple-element.176) | copy-start | bytes 9584644 | tf_op jit(solution)/shard_map/while
  194.6 3.1 %copy-start.2 = (f32[768,130,8]{0,1,2:T(8,128)S(1)}, f32[768,130,8]{0,1,2:T(8,128)}, u32[]{:S(2)}) copy-start(f32[768,130,8]{0,1,2:T(8,128)} %get-tuple-element.176) | copy-start | bytes 9584644 | tf_op jit(solution)/shard_map/while
  205.5 3.1 %copy-start.2 = (f32[768,130,8]{0,1,2:T(8,128)S(1)}, f32[768,130,8]{0,1,2:T(8,128)}, u32[]{:S(2)}) copy-start(f32[768,130,8]{0,1,2:T(8,128)} %get-tuple-element.176) | copy-start | bytes 9584644 | tf_op jit(solution)/shard_map/while
  216.3 3.1 %copy-start.2 = (f32[768,130,8]{0,1,2:T(8,128)S(1)}, f32[768,130,8]{0,1,2:T(8,128)}, u32[]{:S(2)}) copy-start(f32[768,130,8]{0,1,2:T(8,128)} %get-tuple-element.176) | copy-start | bytes 9584644 | tf_op jit(solution)/shard_map/while
where the time goes:
time: 229 us; the launch traced here: 228 us
  local copies, waits for them, and re-layouts  87.8 us (38%)
  blocking collectives  55.4 us (24%)
  matrix products  30.3 us (13%)
  starting transfers between devices  20.2 us (9%)
  other arithmetic  19.1 us (8%)
  waiting for transfers between devices  13.8 us (6%)
    all_gather x1, blocking collectives, on_device(): fresh_all = lax.all_gather(new_kv, 'tp', axis=1, tiled=True)[0]  55.4 us
    unnamed x33, local copies, waits for them, and re-layouts  33.7 us
    dot_general x5, matrix products, online_block(): jnp.einsum('rnk,kd->rnd', weight, values.astype(jnp.float32), precision=l...  18.4 us
    all_to_all x1, local copies, waits for them, and re-layouts, on_device(): lax.all_to_all(lax.all_to_all(spread, 'grp', split_axis=0, concat_axis=0,...  17.7 us
    all_to_all x1, local copies, waits for them, and re-layouts, on_device(): lax.all_to_all(spread, 'grp', split_axis=0, concat_axis=0, tiled=True)  14 us
    all_to_all x1, waiting for transfers between devices, on_device(): lax.all_to_all(spread, 'grp', split_axis=0, concat_axis=0, tiled=True)  13.8 us
    reduce_sum x5, other arithmetic, online_block(): totals = totals * shrink + jnp.sum(weight, axis=2)  12.6 us
    dot_general x5, matrix products, online_block(): jnp.einsum('rnd,kd->rnk', query, keys, preferred_element_type=jnp.float32)  11.8 us
  transfers between devices with their start and end apart: 4, of which 1 were waited for; matrix products, arithmetic and copies ran while one was open for 23% of the time, Pallas kernels for 0%

commit v1 on v0

v1 whole, which is shorter than its diff:
```python
import functools
import math

import jax
import jax.numpy as jnp
from jax import lax
from jax.experimental import pallas as pl
from jax.experimental.pallas import tpu as pltpu
from jax.sharding import PartitionSpec as P

H = 64
KVH = 8
HD = 128
FLOOR = -1e30
ANY = pl.BlockSpec(memory_space=pl.ANY)
SMEM = pl.BlockSpec(memory_space=pltpu.SMEM)
VMEM = pl.BlockSpec(memory_space=pltpu.VMEM)
LIMIT = 56 * 1024 * 1024


def live_pages(session, group, rank, hist_ref, owner_ref, groups, ways):
    step = groups * ways
    first = lax.rem(group - owner_ref[session] + groups, groups) * ways + rank
    return lax.div(hist_ref[session] - first + step - 1, step)


def place(session, group, rank, hist_ref, owner_ref, groups, ways):
    def add(s, total):
        n = live_pages(s, group, rank, hist_ref, owner_ref, groups, ways)
        return total + jnp.where(s < session, n, 0)

    offset = lax.fori_loop(0, groups, add, jnp.int32(0), unroll=groups <= 4)
    return offset, live_pages(session, group, rank, hist_ref, owner_ref, groups, ways)


def pack_kernel(dims, hist_ref, owner_ref, table_ref, pool_ref, new_ref, *refs):
    groups, ways, capacity, packed, page, width = dims
    outs, stage, sem = refs[:ways], refs[ways], refs[ways + 1]
    group, rank = lax.axis_index("grp"), lax.axis_index("tp")
    stage[...] = jnp.zeros_like(stage)

    def each_session(s, at):
        first = lax.rem(group - owner_ref[s] + groups, groups) * ways + rank
        count = live_pages(s, group, rank, hist_ref, owner_ref, groups, ways)

        def each_page(j, at):
            slot = table_ref[s, j * groups * ways + first]
            pltpu.make_async_copy(pool_ref.at[slot], stage.at[at], sem.at[at]).start()
            return at + 1

        return lax.fori_loop(0, count, each_page, at)

    total = lax.fori_loop(0, groups, each_session, jnp.int32(0))
    repeat = ways // KVH

    def halves(shift):
        to = rank ^ shift
        key = pl.multiple_of(lax.div(to, repeat) * HD, HD)
        value = pl.multiple_of((KVH + lax.div(to, repeat)) * HD, HD)
        return to, key, value

    for shift in range(ways):
        to, key, value = halves(shift)
        outs[shift][packed, :, 0:HD] = new_ref[:, pl.ds(key, HD)]
        outs[shift][packed, :, HD:] = new_ref[:, pl.ds(value, HD)]
        columns = pl.multiple_of(to * width, width)
        outs[shift][packed + 1, :, 0:width] = new_ref[:, pl.ds(columns, width)]

    def drain(i, unused):
        pltpu.make_async_copy(pool_ref.at[0], stage.at[i], sem.at[i]).wait()
        return unused

    lax.fori_loop(0, total, drain, 0)

    for shift in range(ways):
        to, key, value = halves(shift)
        outs[shift][0:packed, :, 0:HD] = stage[:, :, pl.ds(key, HD)]
        outs[shift][0:packed, :, HD:] = stage[:, :, pl.ds(value, HD)]


def regroup_kernel(dims, shifts, hist_ref, owner_ref, *refs):
    groups, ways, capacity, packed = dims
    count = len(shifts)
    ins, outs = refs[:count], refs[count:]
    group, rank = lax.axis_index("grp"), lax.axis_index("tp")
    for i, shift in enumerate(shifts):
        for far in range(groups):
            offset, unused = place(group ^ far, group, rank ^ shift, hist_ref, owner_ref, groups, ways)
            start = jnp.minimum(offset, packed + 2 - capacity)
            outs[far][i, 0:capacity] = ins[i][pl.ds(start, capacity)]
            outs[far][i, capacity] = ins[i][packed + 1]


def attend_kernel(dims, refs, shifts, rounds):
    groups, ways, capacity, packed, page, rows, heads, local_new, decode = dims
    first, last = shifts == rounds[0], shifts == rounds[-1]
    hist_ref, owner_ref, query_ref = refs["hist"], refs["owner"], refs["query"]
    padded = -(-rows // 16) * 16
    group, rank = lax.axis_index("grp"), lax.axis_index("tp")
    stacked = refs["stacked"]

    copies, homeward = [], []
    if last:
        fresh = refs["fresh"]
        fresh[...] = jnp.zeros_like(fresh)
        for shift in range(ways):
            copies.append(pltpu.make_async_copy(
                refs["arrived"][shift].at[packed], fresh.at[rank ^ shift], refs["sems"].at[shift]))
        sender = jnp.int32(0)
        for s in range(groups):
            sender = sender + jnp.where(owner_ref[s] == group, s, 0)
        for far in range(groups):
            homeward.append((sender ^ group) == far)
            for part, sources in zip(refs["parts"], rounds):
                for i, shift in enumerate(sources):
                    copies.append((far, pltpu.make_async_copy(
                        part[far].at[i, capacity], refs["returned"].at[rank ^ shift],
                        refs["sems"].at[ways + shift])))
        for copy in copies[:ways]:
            copy.start()
        for far in range(groups):
            @pl.when(homeward[far])
            def start():
                for other, copy in copies[ways:]:
                    if other == far:
                        copy.start()

    for head in range(heads):
        stacked[head * padded:head * padded + rows, :] = query_ref[:, head * HD:(head + 1) * HD]
        stacked[head * padded + rows:(head + 1) * padded, :] = jnp.zeros((padded - rows, HD), jnp.bfloat16)

    keys = len(shifts) * capacity * page
    lane = lax.broadcasted_iota(jnp.int32, (1, keys), 1)
    masks = []
    for far in range(groups):
        seen = lane < 0
        for i, shift in enumerate(shifts):
            offset, live = place(group, group ^ far, rank ^ shift, hist_ref, owner_ref, groups, ways)
            low = (i * capacity + offset - jnp.minimum(offset, packed + 2 - capacity)) * page
            seen = seen | ((lane >= low) & (lane < low + live * page))
        masks.append(jnp.where(seen, 0.0, FLOOR).astype(jnp.float32))

    if last:
        for copy in copies[:ways]:
            copy.wait()
        fresh[ways, 0:page, 0:HD] = refs["decode"][:, pl.ds(pl.multiple_of(lax.div(rank, ways // KVH) * HD, HD), HD)]
        fresh[ways, 0:page, HD:] = refs["decode"][
            :, pl.ds(pl.multiple_of((KVH + lax.div(rank, ways // KVH)) * HD, HD), HD)]

    slope = HD ** -0.5 * math.log2(math.e)
    block_heads = min(heads, 4)
    tall = block_heads * padded

    def fold(state, query, key, value, bias):
        total, top, mixed = state
        score = lax.dot_general(query, key, (((1,), (1,)), ((), ())), preferred_element_type=jnp.float32) + bias
        new_top = jnp.maximum(top, jnp.max(score, axis=1, keepdims=True))
        weight = jnp.exp2((score - new_top) * slope)
        upper = weight.astype(jnp.bfloat16)
        lower = (weight - upper.astype(jnp.float32)).astype(jnp.bfloat16)
        wide = jnp.concatenate([value, jnp.ones_like(value)], axis=1)
        product = jnp.dot(upper, wide, preferred_element_type=jnp.float32)
        product = product + jnp.dot(lower, wide, preferred_element_type=jnp.float32)
        shrink = jnp.exp2((top - new_top) * slope)
        return total * shrink + product[:, HD:], new_top, mixed * shrink + product[:, :HD]

    for b in range(heads // block_heads):
        at = pl.ds(b * tall, tall)
        query = stacked[at, :]
        if first:
            state = (jnp.zeros((tall, HD), jnp.float32), jnp.full((tall, 1), FLOOR, jnp.float32),
                     jnp.zeros((tall, HD), jnp.float32))
        else:
            state = (refs["carry"][0][at, :], refs["carry"][1][at, :][:, :1], refs["carry"][2][at, :])
        for far in range(groups):
            block = refs["blocks"][far]
            rows_of = lambda low: jnp.concatenate(
                [block[i, 0:capacity, :, low:low + HD].reshape(capacity * page, HD) for i in range(len(shifts))], axis=0)
            state = fold(state, query, rows_of(0), rows_of(HD), masks[far])
        if last:
            units = fresh.shape[0]
            place_of = lax.broadcasted_iota(jnp.int32, (padded, units * page), 1)
            asker = lax.broadcasted_iota(jnp.int32, (padded, units * page), 0)
            unit, inside = lax.div(place_of, page), lax.rem(place_of, page)
            token = jnp.minimum(unit, ways) * local_new + inside
            real = ((unit < ways) & (inside < local_new)) | ((unit == ways) & (inside < decode))
            bias = jnp.where(real & (token <= asker), 0.0, FLOOR).astype(jnp.float32)
            bias = jnp.concatenate([bias] * block_heads, axis=0)
            state = fold(state, query, fresh[:, :, :HD].reshape(units * page, HD),
                         fresh[:, :, HD:].reshape(units * page, HD), bias)
            result = (state[2] / state[0]).astype(jnp.bfloat16)
            for h in range(block_heads):
                head = b * block_heads + h
                refs["out"][:, head * HD:(head + 1) * HD] = result[h * padded:h * padded + rows, :]
        else:
            refs["next"][0][at, :] = state[0]
            refs["next"][1][at, :] = jnp.broadcast_to(state[1], (tall, HD))
            refs["next"][2][at, :] = state[2]

    if last:
        for far in range(groups):
            @pl.when(homeward[far])
            def finish():
                for other, copy in copies[ways:]:
                    if other == far:
                        copy.wait()


def on_device(queries, new_kv, decode_kv, pool, hist_pages, owner, block_table):
    groups, ways = lax.axis_size("grp"), lax.axis_size("tp")
    slots, page, features = pool.shape
    capacity = slots // groups
    span = groups * ways
    rows = queries.shape[1]
    heads = H // ways
    local_new = new_kv.shape[1]
    decode = decode_kv.shape[1]
    width = features // ways
    pages_in_all = groups * block_table.shape[1] // 2
    packed = min(slots, (pages_in_all + groups * (span - 1) - ways * groups * (groups - 1) // 2) // span)
    rounds = [list(range(ways))]
    params = pltpu.CompilerParams(vmem_limit_bytes=LIMIT)

    new_rows = new_kv[0]
    if local_new < page:
        new_rows = jnp.pad(new_rows, ((0, page - local_new), (0, 0)))
    decode_rows = jnp.pad(decode_kv[0], ((0, page - decode), (0, 0)))

    unit = (page, 2 * HD)
    cut = pl.pallas_call(
        functools.partial(pack_kernel, (groups, ways, capacity, packed, page, width)),
        out_shape=[jax.ShapeDtypeStruct((packed + 2,) + unit, jnp.bfloat16)] * ways,
        in_specs=[SMEM, SMEM, SMEM, ANY, VMEM],
        out_specs=[VMEM] * ways,
        scratch_shapes=[pltpu.VMEM((packed, page, features), jnp.bfloat16), pltpu.SemaphoreType.DMA((packed,))],
        compiler_params=params,
    )(hist_pages, owner, block_table, pool, new_rows)
    arrived = [cut[0]] + [
        lax.ppermute(cut[shift], "tp", [(i, i ^ shift) for i in range(ways)]) for shift in range(1, ways)]

    parts, carry = [], None
    for shifts in rounds:
        sent = pl.pallas_call(
            functools.partial(regroup_kernel, (groups, ways, capacity, packed), shifts),
            out_shape=[jax.ShapeDtypeStruct((len(shifts), capacity + 1) + unit, jnp.bfloat16)] * groups,
            in_specs=[SMEM, SMEM] + [VMEM] * len(shifts),
            out_specs=[VMEM] * groups,
            compiler_params=params,
        )(hist_pages, owner, *[arrived[shift] for shift in shifts])
        parts.append([sent[0]] + [
            lax.ppermute(sent[far], "grp", [(i, i ^ far) for i in range(groups)]) for far in range(1, groups)])

    tall = heads * (-(-rows // 16) * 16)
    for shifts, blocks in zip(rounds, parts):
        last = shifts == rounds[-1]
        args = dict(hist=hist_pages, owner=owner, query=queries[0], blocks=blocks)
        specs = dict(hist=SMEM, owner=SMEM, query=VMEM, blocks=[VMEM] * groups)
        if carry is not None:
            args["carry"], specs["carry"] = list(carry), [VMEM] * 3
        scratch = dict(stacked=pltpu.VMEM((tall, HD), jnp.bfloat16))
        if last:
            args.update(arrived=arrived, decode=decode_rows, parts=parts)
            specs.update(arrived=[ANY] * ways, decode=VMEM, parts=[[ANY] * groups for unused in rounds])
            outs = dict(out=jax.ShapeDtypeStruct((rows, heads * HD), jnp.bfloat16),
                        returned=jax.ShapeDtypeStruct((ways,) + unit, jnp.bfloat16))
            out_specs = dict(out=VMEM, returned=ANY)
            scratch["fresh"] = pltpu.VMEM((-(-(ways + 1) // 8) * 8,) + unit, jnp.bfloat16)
            scratch["sems"] = pltpu.SemaphoreType.DMA((2 * ways,))
        else:
            outs = dict(next=[jax.ShapeDtypeStruct((tall, HD), jnp.float32)] * 3)
            out_specs = dict(next=[VMEM] * 3)
        flat_args, in_tree = jax.tree.flatten(args)
        flat_outs, out_tree = jax.tree.flatten(outs)
        flat_scratch, scratch_tree = jax.tree.flatten(scratch)

        def kernel(*flat, in_tree=in_tree, out_tree=out_tree, scratch_tree=scratch_tree, shifts=shifts):
            n, m = in_tree.num_leaves, out_tree.num_leaves
            refs = dict(jax.tree.unflatten(in_tree, flat[:n]))
            refs.update(jax.tree.unflatten(out_tree, flat[n:n + m]))
            refs.update(jax.tree.unflatten(scratch_tree, flat[n + m:]))
            dims = (groups, ways, capacity, packed, page, rows, heads, local_new, decode)
            attend_kernel(dims, refs, shifts, rounds)

        flat = pl.pallas_call(
            kernel,
            out_shape=flat_outs,
            in_specs=jax.tree.leaves(specs),
            out_specs=jax.tree.leaves(out_specs),
            scratch_shapes=flat_scratch,
            compiler_params=params,
        )(*flat_args)
        result = jax.tree.unflatten(out_tree, flat)
        carry = None if last else result["next"]
    returned = result["returned"][:, :local_new, :width].reshape(1, ways * local_new, width)
    return result["out"][None], returned


def solution(mesh):
    return jax.shard_map(
        on_device,
        mesh=mesh,
        in_specs=(
            P("grp", None, "tp"),
            P("grp", "tp", None),
            P("grp", None, None),
            P(("grp", "tp"), None, None),
            P(),
            P(),
            P(),
        ),
        out_specs=(P("grp", None, "tp"), P("grp", None, "tp")),
        check_vma=False,
    )
```

time: 229 us -> 71.9 us (0.31)
  the two profiles are of different devices: /device:TPU:0 before, /device:TPU:17 now
where the time goes in v1:
time: 71.9 us; the launch traced here: 71.5 us
  waiting for transfers between devices  41.2 us (57%)
  Pallas kernels  16.7 us (23%)
  starting transfers between devices  10.9 us (15%)
  local copies, waits for them, and re-layouts  2.03 us (3%)
    ppermute x7, waiting for transfers between devices, on_device(): lax.ppermute(cut[shift], 'tp', [(i, i ^ shift) for i in range(ways)])  21.2 us
    ppermute x3, waiting for transfers between devices, on_device(): lax.ppermute(sent[far], 'grp', [(i, i ^ far) for i in range(groups)])  20 us
    pallas_call x1, Pallas kernels, on_device(): pl.pallas_call(kernel, out_shape=flat_outs, in_specs=jax.tree.leaves(spec...  10.4 us
    ppermute x7, starting transfers between devices, on_device(): lax.ppermute(cut[shift], 'tp', [(i, i ^ shift) for i in range(ways)])  7.44 us
    pallas_call x1, Pallas kernels, on_device(): pl.pallas_call(functools.partial(pack_kernel, (groups, ways, capacity, pa...  3.44 us
    ppermute x3, starting transfers between devices, on_device(): lax.ppermute(sent[far], 'grp', [(i, i ^ far) for i in range(groups)])  3.44 us
    pallas_call x1, Pallas kernels, on_device(): pl.pallas_call(functools.partial(regroup_kernel, (groups, ways, capacity,...  2.93 us
  transfers between devices with their start and end apart: 10, of which 7 were waited for; matrix products, arithmetic and copies ran while one was open for 1% of the time, Pallas kernels for 0%

profile of v1, /device:TPU:17, one launch (start us, length us, event | category | flops | bytes accessed | tf_op | source)
XLA Modules:
  0.0 71.5 jit_solution(15274597964749938465)
XLA Ops:
  0.6 0.0 copy-start.10
  0.6 3.4 %shard_map.86 = (bf16[16,16,256]{2,1,0:T(8,128)(2,1)}, bf16[16,16,256]{2,1,0:T(8,128)(2,1)}, bf16[16,16,256]{2,1,0:T(8,128)(2,1)}, bf16[16,16,256]{2,1,0:T(8,128...) custom-call(s32[4]{0:T(128)} %flat_13_.1, ...), custom_call_target="tpu_custom_call" | custom-call | tf_op jit(solution)/shard_map/pallas_call | solution.py:230
  4.1 1.3 %collective-permute-start = (bf16[16,16,256]{2,1,0:T(8,128)(2,1)}, bf16[16,16,256]{2,1,0:T(8,128)(2,1)S(1)}, u32[]{:S(2)}, u32[]{:S(2)}) collective-permute-start(bf16[16,16,256]{2,1,0:T(8,128)(2,1)} %get-tuple-element.17), channel_id=1, source_target_pairs={{0,1},{1,0},{2,3},{3,2},{4,5},{5,4},{6,7},{7,6},{8,9},{9,8},{10,11... | collective-permute-start | bytes 393224 | tf_op jit(solution)/shard_map/ppermute | solution.py:239
  5.4 1.3 %collective-permute-start.1 = (bf16[16,16,256]{2,1,0:T(8,128)(2,1)}, bf16[16,16,256]{2,1,0:T(8,128)(2,1)S(1)}, u32[]{:S(2)}, u32[]{:S(2)}) collective-permute-start(bf16[16,16,256]{2,1,0:T(8,128)(2,1)} %get-tuple-element.18), channel_id=1, source_target_pairs={{0,2},{1,3},{2,0},{3,1},{4,6},{5,7},{6,4},{7,5},{8,10},{9,11},{10,... | collective-permute-start | bytes 393224 | tf_op jit(solution)/shard_map/ppermute | solution.py:239
  6.7 0.1 collective-permute-start.2
  6.8 0.0 collective-permute-start.3
  6.8 3.3 %collective-permute-start.4 = (bf16[16,16,256]{2,1,0:T(8,128)(2,1)}, bf16[16,16,256]{2,1,0:T(8,128)(2,1)S(1)}, u32[]{:S(2)}, u32[]{:S(2)}) collective-permute-start(bf16[16,16,256]{2,1,0:T(8,128)(2,1)} %get-tuple-element.21), channel_id=1, source_target_pairs={{0,5},{1,4},{2,7},{3,6},{4,1},{5,0},{6,3},{7,2},{8,13},{9,12},{10,... | collective-permute-start | bytes 393224 | tf_op jit(solution)/shard_map/ppermute | solution.py:239
  10.1 0.0 collective-permute-done.refs_1_.flat_1_
  10.1 0.2 collective-permute-start.5
  10.3 0.0 collective-permute-done.1.refs_2_.flat_2_
  10.3 1.3 %collective-permute-start.6 = (bf16[16,16,256]{2,1,0:T(8,128)(2,1)}, bf16[16,16,256]{2,1,0:T(8,128)(2,1)S(1)}, u32[]{:S(2)}, u32[]{:S(2)}) collective-permute-start(bf16[16,16,256]{2,1,0:T(8,128)(2,1)} %get-tuple-element.23), channel_id=1, source_target_pairs={{0,7},{1,6},{2,5},{3,4},{4,3},{5,2},{6,1},{7,0},{8,15},{9,14},{10,... | collective-permute-start | bytes 393224 | tf_op jit(solution)/shard_map/ppermute | solution.py:239
  11.5 2.9 %collective-permute-done.2.refs_3_.flat_3_ = bf16[16,16,256]{2,1,0:T(8,128)(2,1)S(1)} collective-permute-done((bf16[16,16,256]{2,1,0:T(8,128)(2,1)}, bf16[16,16,256]{2,1,0:T(8,128)(2,1)S(1)}, u32[]{:S(2)}, u32[]{:S(2)}) %collective-permute-start.2) | collective-permute-done | bytes 131104 | tf_op jit(solution)/shard_map/ppermute | solution.py:239
  14.5 0.6 collective-permute-done.3.refs_4_.flat_4_
  15.0 2.7 %collective-permute-done.4.refs_5_.flat_5_ = bf16[16,16,256]{2,1,0:T(8,128)(2,1)S(1)} collective-permute-done((bf16[16,16,256]{2,1,0:T(8,128)(2,1)}, bf16[16,16,256]{2,1,0:T(8,128)(2,1)S(1)}, u32[]{:S(2)}, u32[]{:S(2)}) %collective-permute-start.4) | collective-permute-done | bytes 131104 | tf_op jit(solution)/shard_map/ppermute | solution.py:239
  17.7 10.7 %collective-permute-done.5.refs_6_.flat_6_ = bf16[16,16,256]{2,1,0:T(8,128)(2,1)S(1)} collective-permute-done((bf16[16,16,256]{2,1,0:T(8,128)(2,1)}, bf16[16,16,256]{2,1,0:T(8,128)(2,1)S(1)}, u32[]{:S(2)}, u32[]{:S(2)}) %collective-permute-start.5) | collective-permute-done | bytes 131104 | tf_op jit(solution)/shard_map/ppermute | solution.py:239
  28.4 4.4 %collective-permute-done.6.refs_7_.flat_7_ = bf16[16,16,256]{2,1,0:T(8,128)(2,1)S(1)} collective-permute-done((bf16[16,16,256]{2,1,0:T(8,128)(2,1)}, bf16[16,16,256]{2,1,0:T(8,128)(2,1)S(1)}, u32[]{:S(2)}, u32[]{:S(2)}) %collective-permute-start.6) | collective-permute-done | bytes 131104 | tf_op jit(solution)/shard_map/ppermute | solution.py:239
  32.8 0.0 copy-done.3
  32.8 0.0 copy-done.4
  32.8 0.0 copy-done.5
  32.8 0.0 copy-done.6
  32.8 0.6 copy-done.9
  33.4 2.9 %shard_map.87 = (bf16[8,7,16,256]{3,2,1,0:T(8,128)(2,1)}, bf16[8,7,16,256]{3,2,1,0:T(8,128)(2,1)}, bf16[8,7,16,256]{3,2,1,0:T(8,128)(2,1)}, bf16[8,7,16,256]{3,2,1,0:T(8,128)(2,1)}) custom-call(s32[4]{0:T(128)} %flat_13_.1, s32[4]{0:T(128)} %flat_14_.1, bf16[16,16,256]{2,1,0:T(8,128)(2,1)} %get-tuple-element.16.refs_0_.flat_0_, ...), custom_call_target="tpu_custom_call" | custom-call | tf_op jit(solution)/shard_map/pallas_call | solution.py:243
  36.4 1.7 %collective-permute-start.7 = (bf16[8,7,16,256]{3,2,1,0:T(8,128)(2,1)}, bf16[8,7,16,256]{3,2,1,0:T(8,128)(2,1)S(1)}, u32[]{:S(2)}, u32[]{:S(2)}) collective-permute-start(bf16[8,7,16,256]{3,2,1,0:T(8,128)(2,1)} %get-tuple-element.25), channel_id=1, source_target_pairs={{0,8},{8,0},{16,24},{24,16},{1,9},{9,1},{17,25},{25,17},{2,10},{10... | collective-permute-start | bytes 1376264 | tf_op jit(solution)/shard_map/ppermute | solution.py:251
  38.1 1.2 %collective-permute-start.8 = (bf16[8,7,16,256]{3,2,1,0:T(8,128)(2,1)}, bf16[8,7,16,256]{3,2,1,0:T(8,128)(2,1)S(1)}, u32[]{:S(2)}, u32[]{:S(2)}) collective-permute-start(bf16[8,7,16,256]{3,2,1,0:T(8,128)(2,1)} %get-tuple-element.26), channel_id=1, source_target_pairs={{0,16},{8,24},{16,0},{24,8},{1,17},{9,25},{17,1},{25,9},{2,18},{10... | collective-permute-start | bytes 1376264 | tf_op jit(solution)/shard_map/ppermute | solution.py:251
  39.3 0.5 collective-permute-start.9
  39.8 0.0 copy-done.10
  39.8 0.6 pad.4.flat_12_
  40.4 0.0 collective-permute-done.7.flat_9_.flat_16_
  40.4 10.0 %collective-permute-done.8.flat_10_.flat_17_ = bf16[8,7,16,256]{3,2,1,0:T(8,128)(2,1)S(1)} collective-permute-done((bf16[8,7,16,256]{3,2,1,0:T(8,128)(2,1)}, bf16[8,7,16,256]{3,2,1,0:T(8,128)(2,1)S(1)}, u32[]{:S(2)}, u32[]{:S(2)}) %collective-permute-start.8) | collective-permute-done | bytes 458784 | tf_op jit(solution)/shard_map/ppermute | solution.py:251
  50.4 10.0 %collective-permute-done.9.flat_11_.flat_18_ = bf16[8,7,16,256]{3,2,1,0:T(8,128)(2,1)S(1)} collective-permute-done((bf16[8,7,16,256]{3,2,1,0:T(8,128)(2,1)}, bf16[8,7,16,256]{3,2,1,0:T(8,128)(2,1)S(1)}, u32[]{:S(2)}, u32[]{:S(2)}) %collective-permute-start.9) | collective-permute-done | bytes 458784 | tf_op jit(solution)/shard_map/ppermute | solution.py:251
  60.4 0.8 %copy-done.2 = bf16[8,7,16,256]{3,2,1,0:T(8,128)(2,1)} copy-done((bf16[8,7,16,256]{3,2,1,0:T(8,128)(2,1)}, bf16[8,7,16,256]{3,2,1,0:T(8,128)(2,1)S(1)}, u32[]{:S(2)}) %copy-start.2) | copy-done | bytes 458776
  61.2 10.4 %shard_map.88 = (bf16[130,1024]{1,0:T(8,128)(2,1)}, bf16[8,16,256]{2,1,0:T(8,128)(2,1)}) custom-call(bf16[16,16,256]{2,1,0:T(8,128)(2,1)} %get-tuple-element.16.refs_0_.flat_0_, bf16[16,16,256]{2,1,0:T(8,128)(2,1)} %copy-done.3, bf16[16,16,256]{2,1,0:T(8,128)(2,1)} %copy-done.4, bf16[16,16,256]{2,1,0:T(8,128)(2,1)} %copy-done.5, ...), custom_call_target="tpu_custom_call" | custom-call | tf_op jit(solution)/shard_map/pallas_call | solution.py:284
  (14 shorter events, 0.0 us)
Async XLA Ops:
  0.6 39.2 %copy-start.10 = (bf16[1,2,2048]{2,1,0:T(2,128)(2,1)S(1)}, bf16[1,2,2048]{2,1,0:T(2,128)(2,1)}, u32[]{:S(2)}) copy-start(bf16[1,2,2048]{2,1,0:T(2,128)(2,1)} %param.9) | copy-start | bytes 24580
  4.1 6.0 %collective-permute-start = (bf16[16,16,256]{2,1,0:T(8,128)(2,1)}, bf16[16,16,256]{2,1,0:T(8,128)(2,1)S(1)}, u32[]{:S(2)}, u32[]{:S(2)}) collective-permute-start(bf16[16,16,256]{2,1,0:T(8,128)(2,1)} %get-tuple-element.17), channel_id=1, source_target_pairs={{0,1},{1,0},{2,3},{3,2},{4,5},{5,4},{6,7},{7,6},{8,9},{9,8},{10,11... | collective-permute-start | bytes 393224 | tf_op jit(solution)/shard_map/ppermute | solution.py:239
  5.4 4.9 %collective-permute-start.1 = (bf16[16,16,256]{2,1,0:T(8,128)(2,1)}, bf16[16,16,256]{2,1,0:T(8,128)(2,1)S(1)}, u32[]{:S(2)}, u32[]{:S(2)}) collective-permute-start(bf16[16,16,256]{2,1,0:T(8,128)(2,1)} %get-tuple-element.18), channel_id=1, source_target_pairs={{0,2},{1,3},{2,0},{3,1},{4,6},{5,7},{6,4},{7,5},{8,10},{9,11},{10,... | collective-permute-start | bytes 393224 | tf_op jit(solution)/shard_map/ppermute | solution.py:239
  6.7 7.8 %collective-permute-start.2 = (bf16[16,16,256]{2,1,0:T(8,128)(2,1)}, bf16[16,16,256]{2,1,0:T(8,128)(2,1)S(1)}, u32[]{:S(2)}, u32[]{:S(2)}) collective-permute-start(bf16[16,16,256]{2,1,0:T(8,128)(2,1)} %get-tuple-element.19), channel_id=1, source_target_pairs={{0,3},{1,2},{2,1},{3,0},{4,7},{5,6},{6,5},{7,4},{8,11},{9,10},{10,... | collective-permute-start | bytes 393224 | tf_op jit(solution)/shard_map/ppermute | solution.py:239
  6.8 8.2 %collective-permute-start.3 = (bf16[16,16,256]{2,1,0:T(8,128)(2,1)}, bf16[16,16,256]{2,1,0:T(8,128)(2,1)S(1)}, u32[]{:S(2)}, u32[]{:S(2)}) collective-permute-start(bf16[16,16,256]{2,1,0:T(8,128)(2,1)} %get-tuple-element.20), channel_id=1, source_target_pairs={{0,4},{1,5},{2,6},{3,7},{4,0},{5,1},{6,2},{7,3},{8,12},{9,13},{10,... | collective-permute-start | bytes 393224 | tf_op jit(solution)/shard_map/ppermute | solution.py:239
  6.8 10.9 %collective-permute-start.4 = (bf16[16,16,256]{2,1,0:T(8,128)(2,1)}, bf16[16,16,256]{2,1,0:T(8,128)(2,1)S(1)}, u32[]{:S(2)}, u32[]{:S(2)}) collective-permute-start(bf16[16,16,256]{2,1,0:T(8,128)(2,1)} %get-tuple-element.21), channel_id=1, source_target_pairs={{0,5},{1,4},{2,7},{3,6},{4,1},{5,0},{6,3},{7,2},{8,13},{9,12},{10,... | collective-permute-start | bytes 393224 | tf_op jit(solution)/shard_map/ppermute | solution.py:239
  10.1 22.7 %copy-start.3 = (bf16[16,16,256]{2,1,0:T(8,128)(2,1)}, bf16[16,16,256]{2,1,0:T(8,128)(2,1)S(1)}, u32[]{:S(2)}) copy-start(bf16[16,16,256]{2,1,0:T(8,128)(2,1)S(1)} %collective-permute-done.refs_1_.flat_1_) | copy-start | bytes 393220
  10.1 18.3 %collective-permute-start.5 = (bf16[16,16,256]{2,1,0:T(8,128)(2,1)}, bf16[16,16,256]{2,1,0:T(8,128)(2,1)S(1)}, u32[]{:S(2)}, u32[]{:S(2)}) collective-permute-start(bf16[16,16,256]{2,1,0:T(8,128)(2,1)} %get-tuple-element.22), channel_id=1, source_target_pairs={{0,6},{1,7},{2,4},{3,5},{4,2},{5,3},{6,0},{7,1},{8,14},{9,15},{10,... | collective-permute-start | bytes 393224 | tf_op jit(solution)/shard_map/ppermute | solution.py:239
  10.3 22.5 %copy-start.4 = (bf16[16,16,256]{2,1,0:T(8,128)(2,1)}, bf16[16,16,256]{2,1,0:T(8,128)(2,1)S(1)}, u32[]{:S(2)}) copy-start(bf16[16,16,256]{2,1,0:T(8,128)(2,1)S(1)} %collective-permute-done.1.refs_2_.flat_2_) | copy-start | bytes 393220
  10.3 22.5 %collective-permute-start.6 = (bf16[16,16,256]{2,1,0:T(8,128)(2,1)}, bf16[16,16,256]{2,1,0:T(8,128)(2,1)S(1)}, u32[]{:S(2)}, u32[]{:S(2)}) collective-permute-start(bf16[16,16,256]{2,1,0:T(8,128)(2,1)} %get-tuple-element.23), channel_id=1, source_target_pairs={{0,7},{1,6},{2,5},{3,4},{4,3},{5,2},{6,1},{7,0},{8,15},{9,14},{10,... | collective-permute-start | bytes 393224 | tf_op jit(solution)/shard_map/ppermute | solution.py:239
  14.5 18.3 %copy-start.5 = (bf16[16,16,256]{2,1,0:T(8,128)(2,1)}, bf16[16,16,256]{2,1,0:T(8,128)(2,1)S(1)}, u32[]{:S(2)}) copy-start(bf16[16,16,256]{2,1,0:T(8,128)(2,1)S(1)} %collective-permute-done.2.refs_3_.flat_3_) | copy-start | bytes 393220
  15.0 17.8 %copy-start.6 = (bf16[16,16,256]{2,1,0:T(8,128)(2,1)}, bf16[16,16,256]{2,1,0:T(8,128)(2,1)S(1)}, u32[]{:S(2)}) copy-start(bf16[16,16,256]{2,1,0:T(8,128)(2,1)S(1)} %collective-permute-done.3.refs_4_.flat_4_) | copy-start | bytes 393220
  17.7 15.1 %copy-start.7 = (bf16[16,16,256]{2,1,0:T(8,128)(2,1)}, bf16[16,16,256]{2,1,0:T(8,128)(2,1)S(1)}, u32[]{:S(2)}) copy-start(bf16[16,16,256]{2,1,0:T(8,128)(2,1)S(1)} %collective-permute-done.4.refs_5_.flat_5_) | copy-start | bytes 393220
  28.4 4.5 %copy-start.8 = (bf16[16,16,256]{2,1,0:T(8,128)(2,1)}, bf16[16,16,256]{2,1,0:T(8,128)(2,1)S(1)}, u32[]{:S(2)}) copy-start(bf16[16,16,256]{2,1,0:T(8,128)(2,1)S(1)} %collective-permute-done.5.refs_6_.flat_6_) | copy-start | bytes 393220
  32.8 0.6 copy-start.9
  36.4 4.1 %collective-permute-start.7 = (bf16[8,7,16,256]{3,2,1,0:T(8,128)(2,1)}, bf16[8,7,16,256]{3,2,1,0:T(8,128)(2,1)S(1)}, u32[]{:S(2)}, u32[]{:S(2)}) collective-permute-start(bf16[8,7,16,256]{3,2,1,0:T(8,128)(2,1)} %get-tuple-element.25), channel_id=1, source_target_pairs={{0,8},{8,0},{16,24},{24,16},{1,9},{9,1},{17,25},{25,17},{2,10},{10... | collective-permute-start | bytes 1376264 | tf_op jit(solution)/shard_map/ppermute | solution.py:251
  38.1 12.3 %collective-permute-start.8 = (bf16[8,7,16,256]{3,2,1,0:T(8,128)(2,1)}, bf16[8,7,16,256]{3,2,1,0:T(8,128)(2,1)S(1)}, u32[]{:S(2)}, u32[]{:S(2)}) collective-permute-start(bf16[8,7,16,256]{3,2,1,0:T(8,128)(2,1)} %get-tuple-element.26), channel_id=1, source_target_pairs={{0,16},{8,24},{16,0},{24,8},{1,17},{9,25},{17,1},{25,9},{2,18},{10... | collective-permute-start | bytes 1376264 | tf_op jit(solution)/shard_map/ppermute | solution.py:251
  39.3 21.0 %collective-permute-start.9 = (bf16[8,7,16,256]{3,2,1,0:T(8,128)(2,1)}, bf16[8,7,16,256]{3,2,1,0:T(8,128)(2,1)S(1)}, u32[]{:S(2)}, u32[]{:S(2)}) collective-permute-start(bf16[8,7,16,256]{3,2,1,0:T(8,128)(2,1)} %get-tuple-element.27), channel_id=1, source_target_pairs={{0,24},{8,16},{16,8},{24,0},{1,25},{9,17},{17,9},{25,1},{2,26},{10... | collective-permute-start | bytes 1376264 | tf_op jit(solution)/shard_map/ppermute | solution.py:251
  40.4 20.0 %copy-start = (bf16[8,7,16,256]{3,2,1,0:T(8,128)(2,1)}, bf16[8,7,16,256]{3,2,1,0:T(8,128)(2,1)S(1)}, u32[]{:S(2)}) copy-start(bf16[8,7,16,256]{3,2,1,0:T(8,128)(2,1)S(1)} %collective-permute-done.7.flat_9_.flat_16_) | copy-start | bytes 1376260
  50.4 10.0 %copy-start.1 = (bf16[8,7,16,256]{3,2,1,0:T(8,128)(2,1)}, bf16[8,7,16,256]{3,2,1,0:T(8,128)(2,1)S(1)}, u32[]{:S(2)}) copy-start(bf16[8,7,16,256]{3,2,1,0:T(8,128)(2,1)S(1)} %collective-permute-done.8.flat_10_.flat_17_) | copy-start | bytes 1376260
  60.4 0.8 %copy-start.2 = (bf16[8,7,16,256]{3,2,1,0:T(8,128)(2,1)}, bf16[8,7,16,256]{3,2,1,0:T(8,128)(2,1)S(1)}, u32[]{:S(2)}) copy-start(bf16[8,7,16,256]{3,2,1,0:T(8,128)(2,1)S(1)} %collective-permute-done.9.flat_11_.flat_18_) | copy-start | bytes 1376260

commit v2 on v1

v2 whole, which is shorter than its diff:
```python
import functools
import math

import jax
import jax.numpy as jnp
from jax import lax
from jax.experimental import pallas as pl
from jax.experimental.pallas import tpu as pltpu
from jax.sharding import PartitionSpec as P

H = 64
KVH = 8
HD = 128
FLOOR = -1e30
ANY = pl.BlockSpec(memory_space=pl.ANY)
SMEM = pl.BlockSpec(memory_space=pltpu.SMEM)
VMEM = pl.BlockSpec(memory_space=pltpu.VMEM)
LIMIT = 56 * 1024 * 1024


def divide(value, by):
    if by & (by - 1):
        return lax.div(value, by)
    return lax.shift_right_logical(value, by.bit_length() - 1)


def remainder(value, by):
    if by & (by - 1):
        return lax.rem(value, by)
    return value & (by - 1)


def live_pages(session, group, rank, hist_ref, owner_ref, groups, ways):
    step = groups * ways
    first = remainder(group - owner_ref[session] + groups, groups) * ways + rank
    return divide(hist_ref[session] - first + step - 1, step)


def place(session, group, rank, hist_ref, owner_ref, groups, ways):
    def add(s, total):
        n = live_pages(s, group, rank, hist_ref, owner_ref, groups, ways)
        return total + jnp.where(s < session, n, 0)

    offset = lax.fori_loop(0, groups, add, jnp.int32(0), unroll=groups <= 4)
    return offset, live_pages(session, group, rank, hist_ref, owner_ref, groups, ways)


def pack_kernel(dims, hist_ref, owner_ref, table_ref, pool_ref, new_ref, *refs):
    groups, ways, capacity, packed, page, width = dims
    outs, stage, sem = refs[:ways], refs[ways], refs[ways + 1]
    group, rank = lax.axis_index("grp"), lax.axis_index("tp")
    def each_session(s, at):
        first = remainder(group - owner_ref[s] + groups, groups) * ways + rank
        count = live_pages(s, group, rank, hist_ref, owner_ref, groups, ways)

        def each_page(j, at):
            slot = table_ref[s, j * groups * ways + first]
            pltpu.make_async_copy(pool_ref.at[slot], stage.at[at], sem.at[at]).start()
            return at + 1

        return lax.fori_loop(0, count, each_page, at)

    total = lax.fori_loop(0, groups, each_session, jnp.int32(0))
    repeat = ways // KVH

    def halves(shift):
        to = rank ^ shift
        key = pl.multiple_of(lax.div(to, repeat) * HD, HD)
        value = pl.multiple_of((KVH + lax.div(to, repeat)) * HD, HD)
        return to, key, value

    for shift in range(ways):
        to, key, value = halves(shift)
        outs[shift][packed, :, 0:HD] = new_ref[:, pl.ds(key, HD)]
        outs[shift][packed, :, HD:] = new_ref[:, pl.ds(value, HD)]
        columns = pl.multiple_of(to * width, width)
        outs[shift][packed + 1, :, 0:width] = new_ref[:, pl.ds(columns, width)]

    def blank(i, unused):
        stage[i] = jnp.zeros(stage.shape[1:], stage.dtype)
        return unused

    lax.fori_loop(total, packed, blank, 0)

    def drain(i, unused):
        pltpu.make_async_copy(pool_ref.at[0], stage.at[i], sem.at[i]).wait()
        return unused

    lax.fori_loop(0, total, drain, 0)

    for shift in range(ways):
        to, key, value = halves(shift)
        outs[shift][0:packed, :, 0:HD] = stage[:, :, pl.ds(key, HD)]
        outs[shift][0:packed, :, HD:] = stage[:, :, pl.ds(value, HD)]


def regroup_kernel(dims, shifts, hist_ref, owner_ref, *refs):
    groups, ways, capacity, packed = dims
    count = len(shifts)
    ins, outs, fresh = refs[:count], refs[-groups - 1:-1], refs[-1]
    group, rank = lax.axis_index("grp"), lax.axis_index("tp")
    for i, shift in enumerate(shifts):
        for far in range(groups):
            offset, unused = place(group ^ far, group, rank ^ shift, hist_ref, owner_ref, groups, ways)
            start = jnp.minimum(offset, packed + 2 - capacity)
            outs[far][i, 0:capacity] = ins[i][pl.ds(start, capacity)]
            outs[far][i, capacity] = ins[i][packed + 1]
        fresh[i] = ins[i][packed]


def attend_kernel(dims, refs, rounds, stages, number):
    groups, ways, capacity, packed, page, rows, heads, local_new, decode = dims
    first, last = number == 0, number == len(stages) - 1
    fresh_round = 0 if first else 1 if last else None
    hist_ref, owner_ref, query_ref = refs["hist"], refs["owner"], refs["query"]
    padded = -(-rows // 16) * 16
    group, rank = lax.axis_index("grp"), lax.axis_index("tp")
    stacked = refs["stacked"]

    homeward = []
    if last:
        sender = jnp.int32(0)
        for s in range(groups):
            sender = sender + jnp.where(owner_ref[s] == group, s, 0)
        for far in range(groups):
            home = [pltpu.make_async_copy(
                refs["parts"][r][far].at[i, capacity], refs["returned"].at[rank ^ shift], refs["home"].at[shift])
                for r, sources in enumerate(rounds) for i, shift in enumerate(sources)]
            homeward.append(((sender ^ group) == far, home))

            @pl.when(homeward[far][0])
            def start():
                for copy in homeward[far][1]:
                    copy.start()

    for head in range(heads):
        stacked[head * padded:head * padded + rows, :] = query_ref[:, head * HD:(head + 1) * HD]
        stacked[head * padded + rows:(head + 1) * padded, :] = jnp.zeros((padded - rows, HD), jnp.bfloat16)

    items = [(r, far, i) for r, far in stages[number] for i in range(len(rounds[r]))]
    many = -(-len(items) // -(-len(items) // 12))
    many = -(-many // 4) * 4
    chunks = [items[k:k + many] for k in range(0, len(items), many)]
    masks = []
    for chunk in chunks:
        lane = lax.broadcasted_iota(jnp.int32, (1, len(chunk) * capacity * page), 1)
        seen = lane < 0
        for n, (r, far, i) in enumerate(chunk):
            offset, live = place(group, group ^ far, rank ^ rounds[r][i], hist_ref, owner_ref, groups, ways)
            low = (n * capacity + offset - jnp.minimum(offset, packed + 2 - capacity)) * page
            seen = seen | ((lane >= low) & (lane < low + live * page))
        masks.append(jnp.where(seen, 0.0, FLOOR).astype(jnp.float32))

    fresh, fresh_bias = None, None
    if fresh_round is not None:
        fresh, shifts = refs["fresh"], rounds[fresh_round]
        units, known = fresh.shape[0], len(shifts)
        for unit in range(units):
            fresh[unit] = refs["rows"][unit] if unit < known else jnp.zeros(fresh.shape[1:], jnp.bfloat16)
        place_of = lax.broadcasted_iota(jnp.int32, (padded, units * page), 1)
        asker = lax.broadcasted_iota(jnp.int32, (padded, units * page), 0)
        inside = remainder(place_of, page)
        token = jnp.full_like(place_of, 2 * padded)
        for unit, shift in enumerate(shifts):
            here = (place_of >= unit * page) & (place_of < (unit + 1) * page) & (inside < local_new)
            token = jnp.where(here, (rank ^ shift) * local_new + inside, token)
        if first:
            mine = lax.div(rank, ways // KVH)
            fresh[known, :, 0:HD] = refs["decode"][:, pl.ds(pl.multiple_of(mine * HD, HD), HD)]
            fresh[known, :, HD:] = refs["decode"][:, pl.ds(pl.multiple_of((KVH + mine) * HD, HD), HD)]
            here = (place_of >= known * page) & (place_of < (known + 1) * page) & (inside < decode)
            token = jnp.where(here, ways * local_new + inside, token)
        fresh_bias = jnp.where(token <= asker, 0.0, FLOOR).astype(jnp.float32)

    slope = HD ** -0.5 * math.log2(math.e)
    block_heads = min(heads, 4)
    tall = block_heads * padded

    def fold(state, query, key, value, bias):
        total, top, mixed = state
        score = lax.dot_general(query, key, (((1,), (1,)), ((), ())), preferred_element_type=jnp.float32) + bias
        new_top = jnp.maximum(top, jnp.max(score, axis=1, keepdims=True))
        weight = jnp.exp2((score - new_top) * slope)
        upper = weight.astype(jnp.bfloat16)
        lower = (weight - upper.astype(jnp.float32)).astype(jnp.bfloat16)
        wide = jnp.concatenate([value, jnp.ones_like(value)], axis=1)
        product = jnp.dot(upper, wide, preferred_element_type=jnp.float32)
        product = product + jnp.dot(lower, wide, preferred_element_type=jnp.float32)
        shrink = jnp.exp2((top - new_top) * slope)
        return total * shrink + product[:, HD:], new_top, mixed * shrink + product[:, :HD]

    blocks = dict(zip(stages[number], refs["blocks"]))
    for b in range(heads // block_heads):
        at = pl.ds(b * tall, tall)
        query = stacked[at, :]
        if first:
            state = (jnp.zeros((tall, HD), jnp.float32), jnp.full((tall, 1), FLOOR, jnp.float32),
                     jnp.zeros((tall, HD), jnp.float32))
        else:
            both = refs["carry"][0][at, :]
            state = (both[:, HD // 2:HD // 2 + 1], both[:, :1], refs["carry"][1][at, :])
        for n, (chunk, mask) in enumerate(zip(chunks, masks)):
            def rows_of(low):
                rows_here = [blocks[r, far][i, 0:capacity, :, low:low + HD].reshape(capacity * page, HD) for r, far, i in chunk]
                if fresh is not None and n == 0:
                    rows_here.append(fresh[:, :, low:low + HD].reshape(units * page, HD))
                return jnp.concatenate(rows_here, axis=0)

            bias = mask
            if fresh is not None and n == 0:
                bias = jnp.concatenate([jnp.broadcast_to(mask, (padded, mask.shape[1])), fresh_bias], axis=1)
                bias = jnp.concatenate([bias] * block_heads, axis=0)
            state = fold(state, query, rows_of(0), rows_of(HD), bias)
        if last:
            result = (state[2] / state[0]).astype(jnp.bfloat16)
            for h in range(block_heads):
                head = b * block_heads + h
                refs["out"][:, head * HD:(head + 1) * HD] = result[h * padded:h * padded + rows, :]
        else:
            left = lax.broadcasted_iota(jnp.int32, (tall, HD), 1) < HD // 2
            refs["next"][0][at, :] = jnp.where(left, state[1], state[0])
            refs["next"][1][at, :] = state[2]

    for chosen, home in homeward:
        @pl.when(chosen)
        def finish():
            for copy in home:
                copy.wait()


def on_device(queries, new_kv, decode_kv, pool, hist_pages, owner, block_table):
    groups, ways = lax.axis_size("grp"), lax.axis_size("tp")
    slots, page, features = pool.shape
    capacity = slots // groups
    span = groups * ways
    rows = queries.shape[1]
    heads = H // ways
    local_new = new_kv.shape[1]
    decode = decode_kv.shape[1]
    width = features // ways
    pages_in_all = groups * block_table.shape[1] // 2
    packed = min(slots, (pages_in_all + groups * (span - 1) - ways * groups * (groups - 1) // 2) // span)
    rounds = [list(reversed(range(3 * ways // 4))), list(reversed(range(3 * ways // 4, ways)))]
    stages = [[(0, far) for far in range(groups // 2)], [(0, far) for far in range(groups // 2, groups)], [(1, far) for far in range(groups // 2, groups)] + [(1, far) for far in range(groups // 2)]]
    params = pltpu.CompilerParams(vmem_limit_bytes=LIMIT)
    cheap = pl.CostEstimate(flops=0, bytes_accessed=0, transcendentals=0)

    new_rows = new_kv[0]
    if local_new < page:
        new_rows = jnp.pad(new_rows, ((0, page - local_new), (0, 0)))
    decode_rows = jnp.pad(decode_kv[0], ((0, page - decode), (0, 0)))

    unit = (page, 2 * HD)
    cut = pl.pallas_call(
        functools.partial(pack_kernel, (groups, ways, capacity, packed, page, width)),
        out_shape=[jax.ShapeDtypeStruct((packed + 2,) + unit, jnp.bfloat16)] * ways,
        in_specs=[SMEM, SMEM, SMEM, ANY, VMEM],
        out_specs=[VMEM] * ways,
        scratch_shapes=[pltpu.VMEM((packed, page, features), jnp.bfloat16), pltpu.SemaphoreType.DMA((packed,))],
        compiler_params=params,
        cost_estimate=cheap,
    )(hist_pages, owner, block_table, pool, new_rows)
    def along_tp(shift):
        return lax.ppermute(cut[shift], "tp", [(i, i ^ shift) for i in range(ways)])

    arrived = {0: cut[0]}
    arrived.update({shift: along_tp(shift) for shift in sorted(rounds[0]) if shift})

    def sort(shifts, before):
        sent = pl.pallas_call(
            functools.partial(regroup_kernel, (groups, ways, capacity, packed), shifts),
            out_shape=[jax.ShapeDtypeStruct((len(shifts), capacity + 1) + unit, jnp.bfloat16)] * groups + [
                jax.ShapeDtypeStruct((len(shifts),) + unit, jnp.bfloat16)],
            in_specs=[SMEM, SMEM] + [VMEM] * len(shifts) + [ANY] * len(before),
            out_specs=[VMEM] * (groups + 1),
            compiler_params=params,
            cost_estimate=cheap,
        )(hist_pages, owner, *[arrived[shift] for shift in shifts], *before)
        got = {far: lax.ppermute(sent[far], "grp", [(i, i ^ far) for i in range(groups)])
               for far in reversed(range(1, groups))}
        return [sent[0]] + [got[far] for far in range(1, groups)], sent[groups]

    tall = heads * (-(-rows // 16) * 16)
    def attend(number, carry):
        stage = stages[number]
        first, last = number == 0, number == len(stages) - 1
        args = dict(hist=hist_pages, owner=owner, query=queries[0], blocks=[parts[r][far] for r, far in stage])
        specs = dict(hist=SMEM, owner=SMEM, query=VMEM, blocks=[VMEM] * len(stage))
        scratch = dict(stacked=pltpu.VMEM((tall, HD), jnp.bfloat16))
        if first:
            args["decode"], specs["decode"] = decode_rows, VMEM
        if carry is not None:
            args["carry"], specs["carry"] = list(carry), [VMEM] * 2
        if first or last:
            args["rows"], specs["rows"] = fresh_rows[0 if first else 1], VMEM
            scratch["fresh"] = pltpu.VMEM((-(-(len(rounds[0 if first else 1]) + 1) // 8) * 8,) + unit, jnp.bfloat16)
        if last:
            args["parts"], specs["parts"] = parts, [[ANY] * groups for unused in rounds]
            outs = dict(out=jax.ShapeDtypeStruct((rows, heads * HD), jnp.bfloat16),
                        returned=jax.ShapeDtypeStruct((ways,) + unit, jnp.bfloat16))
            out_specs = dict(out=VMEM, returned=VMEM)
            scratch["home"] = pltpu.SemaphoreType.DMA((ways,))
        else:
            outs = dict(next=[jax.ShapeDtypeStruct((tall, HD), jnp.float32)] * 2)
            out_specs = dict(next=[VMEM] * 2)
        flat_args, in_tree = jax.tree.flatten(args)
        flat_outs, out_tree = jax.tree.flatten(outs)
        flat_scratch, scratch_tree = jax.tree.flatten(scratch)

        def kernel(*flat, in_tree=in_tree, out_tree=out_tree, scratch_tree=scratch_tree, number=number):
            n, m = in_tree.num_leaves, out_tree.num_leaves
            refs = dict(jax.tree.unflatten(in_tree, flat[:n]))
            refs.update(jax.tree.unflatten(out_tree, flat[n:n + m]))
            refs.update(jax.tree.unflatten(scratch_tree, flat[n + m:]))
            dims = (groups, ways, capacity, packed, page, rows, heads, local_new, decode)
            attend_kernel(dims, refs, rounds, stages, number)

        flat = pl.pallas_call(
            kernel,
            out_shape=flat_outs,
            in_specs=jax.tree.leaves(specs),
            out_specs=jax.tree.leaves(out_specs),
            scratch_shapes=flat_scratch,
            compiler_params=params,
            cost_estimate=cheap,
        )(*flat_args)
        result = jax.tree.unflatten(out_tree, flat)
        return result

    (near_parts, near_fresh) = sort(rounds[0], [])
    arrived.update({shift: along_tp(shift) for shift in rounds[1]})
    parts, fresh_rows = [near_parts], [near_fresh]
    result = attend(0, None)
    (far_parts, far_fresh) = sort(rounds[1], [result["next"][0]])
    parts.append(far_parts)
    fresh_rows.append(far_fresh)
    for number in range(1, len(stages)):
        result = attend(number, result["next"])
    returned = result["returned"][:, :local_new, :width].reshape(1, ways * local_new, width)
    return result["out"][None], returned


def solution(mesh):
    return jax.shard_map(
        on_device,
        mesh=mesh,
        in_specs=(
            P("grp", None, "tp"),
            P("grp", "tp", None),
            P("grp", None, None),
            P(("grp", "tp"), None, None),
            P(),
            P(),
            P(),
        ),
        out_specs=(P("grp", None, "tp"), P("grp", None, "tp")),
        check_vma=False,
    )
```

time: 71.9 us -> 58.4 us (0.81)
  waiting for transfers between devices: 41.2 us -> 13.5 us
  Pallas kernels: 16.7 us -> 24.1 us
  starting transfers between devices: 10.9 us -> 15.5 us
  local copies, waits for them, and re-layouts: 2.03 us -> 4.23 us
    ppermute x10 -> x13, waiting for transfers between devices: 41.2 us -> 13.5 us  [the longest x7 13.5 us: along_tp(): return lax.ppermute(cut[shift], 'tp', [(i, i ^ shift) for i in range(ways)])]
    pallas_call x2 -> x5, Pallas kernels: 13.3 us -> 20.7 us  [the longest x3 16.3 us: attend(): pl.pallas_call(kernel, out_shape=flat_outs, in_specs=jax.tree.leaves(spec...]
    ppermute x10 -> x13, starting transfers between devices: 10.9 us -> 15.5 us  [the longest x7 8.4 us: along_tp(): return lax.ppermute(cut[shift], 'tp', [(i, i ^ shift) for i in range(ways)])]
    unnamed x22 -> x28, local copies, waits for them, and re-layouts: 1.4 us -> 3.59 us
  transfers between devices with their start and end apart: 10 -> 13, of which waited for: 7 -> 4; matrix products, arithmetic and copies ran while one was open for 1% -> 1% of each run, Pallas kernels for 0% -> 23%
where the time goes in v2:
time: 58.4 us; the launch traced here: 58 us
  Pallas kernels  24.1 us (41%)
  starting transfers between devices  15.5 us (27%)
  waiting for transfers between devices  13.5 us (23%)
  local copies, waits for them, and re-layouts  4.23 us (7%)
  between operations  0.74 us (1%)
    pallas_call x3, Pallas kernels, attend(): pl.pallas_call(kernel, out_shape=flat_outs, in_specs=jax.tree.leaves(spec...  16.3 us
    ppermute x7, waiting for transfers between devices, along_tp(): return lax.ppermute(cut[shift], 'tp', [(i, i ^ shift) for i in range(ways)])  13.5 us
    ppermute x7, starting transfers between devices, along_tp(): return lax.ppermute(cut[shift], 'tp', [(i, i ^ shift) for i in range(ways)])  8.4 us
    ppermute x6, starting transfers between devices, sort(): lax.ppermute(sent[far], 'grp', [(i, i ^ far) for i in range(groups)])  7.13 us
    pallas_call x2, Pallas kernels, sort(): pl.pallas_call(functools.partial(regroup_kernel, (groups, ways, capacity,...  4.33 us
    unnamed x28, local copies, waits for them, and re-layouts  3.59 us
    pallas_call x1, Pallas kernels, on_device(): pl.pallas_call(functools.partial(pack_kernel, (groups, ways, capacity, pa...  3.38 us
  transfers between devices with their start and end apart: 13, of which 4 were waited for; matrix products, arithmetic and copies ran while one was open for 1% of the time, Pallas kernels for 23%

profile of v2, /device:TPU:17, one launch (start us, length us, event | category | flops | bytes accessed | tf_op | source)
XLA Modules:
  0.0 58.0 jit_solution(12466663434023266212)
XLA Ops:
  0.6 3.4 %shard_map.86 = (bf16[16,16,256]{2,1,0:T(8,128)(2,1)}, bf16[16,16,256]{2,1,0:T(8,128)(2,1)}, bf16[16,16,256]{2,1,0:T(8,128)(2,1)}, bf16[16,16,256]{2,1,0:T(8,128...) custom-call(s32[4]{0:T(128)} %flat_6_.1, ...), custom_call_target="tpu_custom_call" | custom-call | tf_op jit(solution)/shard_map/pallas_call | solution.py:254
  4.0 1.1 %collective-permute-start.2 = (bf16[16,16,256]{2,1,0:T(8,128)(2,1)}, bf16[16,16,256]{2,1,0:T(8,128)(2,1)S(1)}, u32[]{:S(2)}, u32[]{:S(2)}) collective-permute-start(bf16[16,16,256]{2,1,0:T(8,128)(2,1)} %get-tuple-element.28), channel_id=1, source_target_pairs={{0,5},{1,4},{2,7},{3,6},{4,1},{5,0},{6,3},{7,2},{8,13},{9,12},{10,... | collective-permute-start | bytes 393224 | tf_op jit(solution)/shard_map/ppermute | solution.py:264
  5.1 2.3 %collective-permute-start.3 = (bf16[16,16,256]{2,1,0:T(8,128)(2,1)}, bf16[16,16,256]{2,1,0:T(8,128)(2,1)S(1)}, u32[]{:S(2)}, u32[]{:S(2)}) collective-permute-start(bf16[16,16,256]{2,1,0:T(8,128)(2,1)} %get-tuple-element.29), channel_id=1, source_target_pairs={{0,4},{1,5},{2,6},{3,7},{4,0},{5,1},{6,2},{7,3},{8,12},{9,13},{10,... | collective-permute-start | bytes 393224 | tf_op jit(solution)/shard_map/ppermute | solution.py:264
  7.4 1.3 %collective-permute-start.4 = (bf16[16,16,256]{2,1,0:T(8,128)(2,1)}, bf16[16,16,256]{2,1,0:T(8,128)(2,1)S(1)}, u32[]{:S(2)}, u32[]{:S(2)}) collective-permute-start(bf16[16,16,256]{2,1,0:T(8,128)(2,1)} %get-tuple-element.30), channel_id=1, source_target_pairs={{0,3},{1,2},{2,1},{3,0},{4,7},{5,6},{6,5},{7,4},{8,11},{9,10},{10,... | collective-permute-start | bytes 393224 | tf_op jit(solution)/shard_map/ppermute | solution.py:264
  8.7 0.2 collective-permute-start.5
  8.8 1.2 %collective-permute-start.6 = (bf16[16,16,256]{2,1,0:T(8,128)(2,1)}, bf16[16,16,256]{2,1,0:T(8,128)(2,1)S(1)}, u32[]{:S(2)}, u32[]{:S(2)}) collective-permute-start(bf16[16,16,256]{2,1,0:T(8,128)(2,1)} %get-tuple-element.32), channel_id=1, source_target_pairs={{0,1},{1,0},{2,3},{3,2},{4,5},{5,4},{6,7},{7,6},{8,9},{9,8},{10,11... | collective-permute-start | bytes 393224 | tf_op jit(solution)/shard_map/ppermute | solution.py:264
  10.0 2.4 %collective-permute-done.2.refs_0_ = bf16[16,16,256]{2,1,0:T(8,128)(2,1)S(1)} collective-permute-done((bf16[16,16,256]{2,1,0:T(8,128)(2,1)}, bf16[16,16,256]{2,1,0:T(8,128)(2,1)S(1)}, u32[]{:S(2)}, u32[]{:S(2)}) %collective-permute-start.2) | collective-permute-done | bytes 131104 | tf_op jit(solution)/shard_map/ppermute | solution.py:264
  12.5 3.6 %collective-permute-done.3.refs_1_ = bf16[16,16,256]{2,1,0:T(8,128)(2,1)S(1)} collective-permute-done((bf16[16,16,256]{2,1,0:T(8,128)(2,1)}, bf16[16,16,256]{2,1,0:T(8,128)(2,1)S(1)}, u32[]{:S(2)}, u32[]{:S(2)}) %collective-permute-start.3) | collective-permute-done | bytes 131104 | tf_op jit(solution)/shard_map/ppermute | solution.py:264
  16.1 2.1 %collective-permute-done.5.refs_3_ = bf16[16,16,256]{2,1,0:T(8,128)(2,1)S(1)} collective-permute-done((bf16[16,16,256]{2,1,0:T(8,128)(2,1)}, bf16[16,16,256]{2,1,0:T(8,128)(2,1)S(1)}, u32[]{:S(2)}, u32[]{:S(2)}) %collective-permute-start.5) | collective-permute-done | bytes 131104 | tf_op jit(solution)/shard_map/ppermute | solution.py:264
  18.3 0.6 %copy-done.9 = bf16[16,16,256]{2,1,0:T(8,128)(2,1)} copy-done((bf16[16,16,256]{2,1,0:T(8,128)(2,1)}, bf16[16,16,256]{2,1,0:T(8,128)(2,1)S(1)}, u32[]{:S(2)}) %copy-start.9) | copy-done | bytes 131096
  18.9 0.1 copy-done.10
  18.9 2.5 %shard_map.87 = (bf16[6,7,16,256]{3,2,1,0:T(8,128)(2,1)}, bf16[6,7,16,256]{3,2,1,0:T(8,128)(2,1)}, bf16[6,7,16,256]{3,2,1,0:T(8,128)(2,1)}, bf16[6,7,16,256]{3,2,1,0:T(8,128)(2,1)}, bf16[6,16,256]{2,1,0:T(8,128)(2,1)}) custom-call(s32[4]{0:T(128)} %flat_6_.1, s32[4]{0:T(128)} %flat_7_.1, bf16[16,16,256]{2,1,0:T(8,128)(2,1)} %copy-done.6, ...), custom_call_target="tpu_custom_call" | custom-call | tf_op jit(solution)/shard_map/pallas_call | solution.py:270
  21.4 2.8 %collective-permute-start.7 = (bf16[6,7,16,256]{3,2,1,0:T(8,128)(2,1)}, bf16[6,7,16,256]{3,2,1,0:T(8,128)(2,1)S(1)}, u32[]{:S(2)}, u32[]{:S(2)}) collective-permute-start(bf16[6,7,16,256]{3,2,1,0:T(8,128)(2,1)} %get-tuple-element.35), channel_id=1, source_target_pairs={{0,8},{8,0},{16,24},{24,16},{1,9},{9,1},{17,25},{25,17},{2,10},{10... | collective-permute-start | bytes 1032200 | tf_op jit(solution)/shard_map/ppermute | solution.py:279
  24.2 1.2 %collective-permute-start.11 = (bf16[6,7,16,256]{3,2,1,0:T(8,128)(2,1)}, bf16[6,7,16,256]{3,2,1,0:T(8,128)(2,1)S(1)}, u32[]{:S(2)}, u32[]{:S(2)}) collective-permute-start(bf16[6,7,16,256]{3,2,1,0:T(8,128)(2,1)} %get-tuple-element.42), channel_id=1, source_target_pairs={{0,16},{8,24},{16,0},{24,8},{1,17},{9,25},{17,1},{25,9},{2,18},{10... | collective-permute-start | bytes 1032200 | tf_op jit(solution)/shard_map/ppermute | solution.py:279
  25.5 0.5 collective-permute-start.12
  25.9 2.4 %collective-permute-start.1 = (bf16[16,16,256]{2,1,0:T(8,128)(2,1)}, bf16[16,16,256]{2,1,0:T(8,128)(2,1)S(1)}, u32[]{:S(2)}, u32[]{:S(2)}) collective-permute-start(bf16[16,16,256]{2,1,0:T(8,128)(2,1)} %get-tuple-element.27), channel_id=1, source_target_pairs={{0,6},{1,7},{2,4},{3,5},{4,2},{5,3},{6,0},{7,1},{8,14},{9,15},{10,... | collective-permute-start | bytes 393224 | tf_op jit(solution)/shard_map/ppermute | solution.py:264
  28.3 0.6 %pad.4.flat_2_ = bf16[16,2048]{1,0:T(8,128)(2,1)} pad(bf16[2,2048]{1,0:T(2,128)(2,1)S(1)} %bitcast.9, bf16[]{:T(256)} %constant.2.clone.1), padding=0_14x0_0 | pad | bytes 73730 | tf_op jit(solution)/shard_map/jit(_pad)/pad | solution.py:251
  29.0 0.7 %copy-done = bf16[6,7,16,256]{3,2,1,0:T(8,128)(2,1)} copy-done((bf16[6,7,16,256]{3,2,1,0:T(8,128)(2,1)}, bf16[6,7,16,256]{3,2,1,0:T(8,128)(2,1)S(1)}, u32[]{:S(2)}) %copy-start) | copy-done | bytes 344088
  29.7 5.5 %shard_map.88 = (f32[1152,128]{1,0:T(8,128)}, f32[1152,128]{1,0:T(8,128)}) custom-call(bf16[6,7,16,256]{3,2,1,0:T(8,128)(2,1)} %get-tuple-element.34.flat_0_.flat_8_, bf16[6,7,16,256]{3,2,1,0:T(8,128)(2,1)} %copy-done, bf16[16,2048]{1,0:T(8,128)(2,1)} %pad.4.flat_2_, s32[4]{0:T(128)} %flat_6_.1, s32[4]{0:T(128)} %flat_7_.1, bf16[130,1024]{1,0:T(8,128)(2,1)} %bitcast.5, ...), custom_call_target="tpu_custom_call" | custom-call | tf_op jit(solution)/shard_map/pallas_call | solution.py:318
  35.1 5.3 %collective-permute-done.1.refs_1_ = bf16[16,16,256]{2,1,0:T(8,128)(2,1)S(1)} collective-permute-done((bf16[16,16,256]{2,1,0:T(8,128)(2,1)}, bf16[16,16,256]{2,1,0:T(8,128)(2,1)S(1)}, u32[]{:S(2)}, u32[]{:S(2)}) %collective-permute-start.1) | collective-permute-done | bytes 131104 | tf_op jit(solution)/shard_map/ppermute | solution.py:264
  40.4 0.6 %copy-done.12 = bf16[16,16,256]{2,1,0:T(8,128)(2,1)} copy-done((bf16[16,16,256]{2,1,0:T(8,128)(2,1)}, bf16[16,16,256]{2,1,0:T(8,128)(2,1)S(1)}, u32[]{:S(2)}) %copy-start.12) | copy-done | bytes 131096
  41.1 1.8 %shard_map.89 = (bf16[2,7,16,256]{3,2,1,0:T(8,128)(2,1)}, bf16[2,7,16,256]{3,2,1,0:T(8,128)(2,1)}, bf16[2,7,16,256]{3,2,1,0:T(8,128)(2,1)}, bf16[2,7,16,256]{3,2,1,0:T(8,128)(2,1)}, bf16[2,16,256]{2,1,0:T(8,128)(2,1)}) custom-call(s32[4]{0:T(128)} %flat_6_.1, s32[4]{0:T(128)} %flat_7_.1, bf16[16,16,256]{2,1,0:T(8,128)(2,1)} %copy-done.11, ...), custom_call_target="tpu_custom_call" | custom-call | tf_op jit(solution)/shard_map/pallas_call | solution.py:270
  42.9 1.0 %collective-permute-start.10 = (bf16[2,7,16,256]{3,2,1,0:T(8,128)(2,1)}, bf16[2,7,16,256]{3,2,1,0:T(8,128)(2,1)S(1)}, u32[]{:S(2)}, u32[]{:S(2)}) collective-permute-start(bf16[2,7,16,256]{3,2,1,0:T(8,128)(2,1)} %get-tuple-element.41), channel_id=1, source_target_pairs={{0,8},{8,0},{16,24},{24,16},{1,9},{9,1},{17,25},{25,17},{2,10},{10... | collective-permute-start | bytes 344072 | tf_op jit(solution)/shard_map/ppermute | solution.py:279
  43.9 1.2 %collective-permute-start.8 = (bf16[2,7,16,256]{3,2,1,0:T(8,128)(2,1)}, bf16[2,7,16,256]{3,2,1,0:T(8,128)(2,1)S(1)}, u32[]{:S(2)}, u32[]{:S(2)}) collective-permute-start(bf16[2,7,16,256]{3,2,1,0:T(8,128)(2,1)} %get-tuple-element.38), channel_id=1, source_target_pairs={{0,16},{8,24},{16,0},{24,8},{1,17},{9,25},{17,1},{25,9},{2,18},{10... | collective-permute-start | bytes 344072 | tf_op jit(solution)/shard_map/ppermute | solution.py:279
  45.1 0.5 collective-permute-start.9
  45.6 0.7 %copy-done.1 = bf16[6,7,16,256]{3,2,1,0:T(8,128)(2,1)} copy-done((bf16[6,7,16,256]{3,2,1,0:T(8,128)(2,1)}, bf16[6,7,16,256]{3,2,1,0:T(8,128)(2,1)S(1)}, u32[]{:S(2)}) %copy-start.1) | copy-done | bytes 344088
  46.3 0.1 copy-done.2
  46.4 5.9 %shard_map.90 = (f32[1152,128]{1,0:T(8,128)}, f32[1152,128]{1,0:T(8,128)}) custom-call(bf16[6,7,16,256]{3,2,1,0:T(8,128)(2,1)} %copy-done.1, bf16[6,7,16,256]{3,2,1,0:T(8,128)(2,1)} %copy-done.2, f32[1152,128]{1,0:T(8,128)} %get-tuple-element.37.refs_2_.flat_2_, f32[1152,128]{1,0:T(8,128)} %get-tuple-element.44.flat_3_, s32[4]{0:T(128)} %flat_6_.1, ...), custom_call_target="tpu_custom_call" | custom-call | tf_op jit(solution)/shard_map/pallas_call | solution.py:318
  52.4 0.6 %copy-done.3 = bf16[2,7,16,256]{3,2,1,0:T(8,128)(2,1)} copy-done((bf16[2,7,16,256]{3,2,1,0:T(8,128)(2,1)}, bf16[2,7,16,256]{3,2,1,0:T(8,128)(2,1)S(1)}, u32[]{:S(2)}) %copy-start.3) | copy-done | bytes 114712
  53.0 0.0 copy-done.4
  53.0 0.0 copy-done.5
  53.0 5.0 %shard_map.91 = (bf16[130,1024]{1,0:T(8,128)(2,1)}, bf16[8,16,256]{2,1,0:T(8,128)(2,1)}) custom-call(bf16[2,7,16,256]{3,2,1,0:T(8,128)(2,1)} %copy-done.4, bf16[2,7,16,256]{3,2,1,0:T(8,128)(2,1)} %copy-done.5, bf16[2,7,16,256]{3,2,1,0:T(8,128)(2,1)} %get-tuple-element.40.flat_2_.flat_12_, bf16[2,7,16,256]{3,2,1,0:T(8,128)(2,1)} %copy-done.3, ...), custom_call_target="tpu_custom_call" | custom-call | tf_op jit(solution)/shard_map/pallas_call | solution.py:318
  (29 shorter events, 0.1 us)
Async XLA Ops:
  0.6 27.7 %copy-start.13 = (bf16[1,2,2048]{2,1,0:T(2,128)(2,1)S(1)}, bf16[1,2,2048]{2,1,0:T(2,128)(2,1)}, u32[]{:S(2)}) copy-start(bf16[1,2,2048]{2,1,0:T(2,128)(2,1)} %param.9) | copy-start | bytes 24580
  4.0 8.4 %collective-permute-start.2 = (bf16[16,16,256]{2,1,0:T(8,128)(2,1)}, bf16[16,16,256]{2,1,0:T(8,128)(2,1)S(1)}, u32[]{:S(2)}, u32[]{:S(2)}) collective-permute-start(bf16[16,16,256]{2,1,0:T(8,128)(2,1)} %get-tuple-element.28), channel_id=1, source_target_pairs={{0,5},{1,4},{2,7},{3,6},{4,1},{5,0},{6,3},{7,2},{8,13},{9,12},{10,... | collective-permute-start | bytes 393224 | tf_op jit(solution)/shard_map/ppermute | solution.py:264
  5.1 11.0 %collective-permute-start.3 = (bf16[16,16,256]{2,1,0:T(8,128)(2,1)}, bf16[16,16,256]{2,1,0:T(8,128)(2,1)S(1)}, u32[]{:S(2)}, u32[]{:S(2)}) collective-permute-start(bf16[16,16,256]{2,1,0:T(8,128)(2,1)} %get-tuple-element.29), channel_id=1, source_target_pairs={{0,4},{1,5},{2,6},{3,7},{4,0},{5,1},{6,2},{7,3},{8,12},{9,13},{10,... | collective-permute-start | bytes 393224 | tf_op jit(solution)/shard_map/ppermute | solution.py:264
  7.4 8.7 %collective-permute-start.4 = (bf16[16,16,256]{2,1,0:T(8,128)(2,1)}, bf16[16,16,256]{2,1,0:T(8,128)(2,1)S(1)}, u32[]{:S(2)}, u32[]{:S(2)}) collective-permute-start(bf16[16,16,256]{2,1,0:T(8,128)(2,1)} %get-tuple-element.30), channel_id=1, source_target_pairs={{0,3},{1,2},{2,1},{3,0},{4,7},{5,6},{6,5},{7,4},{8,11},{9,10},{10,... | collective-permute-start | bytes 393224 | tf_op jit(solution)/shard_map/ppermute | solution.py:264
  8.7 9.6 %collective-permute-start.5 = (bf16[16,16,256]{2,1,0:T(8,128)(2,1)}, bf16[16,16,256]{2,1,0:T(8,128)(2,1)S(1)}, u32[]{:S(2)}, u32[]{:S(2)}) collective-permute-start(bf16[16,16,256]{2,1,0:T(8,128)(2,1)} %get-tuple-element.31), channel_id=1, source_target_pairs={{0,2},{1,3},{2,0},{3,1},{4,6},{5,7},{6,4},{7,5},{8,10},{9,11},{10,... | collective-permute-start | bytes 393224 | tf_op jit(solution)/shard_map/ppermute | solution.py:264
  8.8 9.4 %collective-permute-start.6 = (bf16[16,16,256]{2,1,0:T(8,128)(2,1)}, bf16[16,16,256]{2,1,0:T(8,128)(2,1)S(1)}, u32[]{:S(2)}, u32[]{:S(2)}) collective-permute-start(bf16[16,16,256]{2,1,0:T(8,128)(2,1)} %get-tuple-element.32), channel_id=1, source_target_pairs={{0,1},{1,0},{2,3},{3,2},{4,5},{5,4},{6,7},{7,6},{8,9},{9,8},{10,11... | collective-permute-start | bytes 393224 | tf_op jit(solution)/shard_map/ppermute | solution.py:264
  12.5 5.8 %copy-start.6 = (bf16[16,16,256]{2,1,0:T(8,128)(2,1)}, bf16[16,16,256]{2,1,0:T(8,128)(2,1)S(1)}, u32[]{:S(2)}) copy-start(bf16[16,16,256]{2,1,0:T(8,128)(2,1)S(1)} %collective-permute-done.2.refs_0_) | copy-start | bytes 393220
  16.1 2.2 %copy-start.7 = (bf16[16,16,256]{2,1,0:T(8,128)(2,1)}, bf16[16,16,256]{2,1,0:T(8,128)(2,1)S(1)}, u32[]{:S(2)}) copy-start(bf16[16,16,256]{2,1,0:T(8,128)(2,1)S(1)} %collective-permute-done.3.refs_1_) | copy-start | bytes 393220
  16.1 2.2 %copy-start.8 = (bf16[16,16,256]{2,1,0:T(8,128)(2,1)}, bf16[16,16,256]{2,1,0:T(8,128)(2,1)S(1)}, u32[]{:S(2)}) copy-start(bf16[16,16,256]{2,1,0:T(8,128)(2,1)S(1)} %collective-permute-done.4.refs_2_) | copy-start | bytes 393220
  18.2 0.7 %copy-start.9 = (bf16[16,16,256]{2,1,0:T(8,128)(2,1)}, bf16[16,16,256]{2,1,0:T(8,128)(2,1)S(1)}, u32[]{:S(2)}) copy-start(bf16[16,16,256]{2,1,0:T(8,128)(2,1)S(1)} %collective-permute-done.5.refs_3_) | copy-start | bytes 393220
  18.2 0.7 %copy-start.10 = (bf16[16,16,256]{2,1,0:T(8,128)(2,1)}, bf16[16,16,256]{2,1,0:T(8,128)(2,1)S(1)}, u32[]{:S(2)}) copy-start(bf16[16,16,256]{2,1,0:T(8,128)(2,1)S(1)} %collective-permute-done.6.refs_4_) | copy-start | bytes 393220
  21.4 7.5 %collective-permute-start.7 = (bf16[6,7,16,256]{3,2,1,0:T(8,128)(2,1)}, bf16[6,7,16,256]{3,2,1,0:T(8,128)(2,1)S(1)}, u32[]{:S(2)}, u32[]{:S(2)}) collective-permute-start(bf16[6,7,16,256]{3,2,1,0:T(8,128)(2,1)} %get-tuple-element.35), channel_id=1, source_target_pairs={{0,8},{8,0},{16,24},{24,16},{1,9},{9,1},{17,25},{25,17},{2,10},{10... | collective-permute-start | bytes 1032200 | tf_op jit(solution)/shard_map/ppermute | solution.py:279
  24.2 21.3 %collective-permute-start.11 = (bf16[6,7,16,256]{3,2,1,0:T(8,128)(2,1)}, bf16[6,7,16,256]{3,2,1,0:T(8,128)(2,1)S(1)}, u32[]{:S(2)}, u32[]{:S(2)}) collective-permute-start(bf16[6,7,16,256]{3,2,1,0:T(8,128)(2,1)} %get-tuple-element.42), channel_id=1, source_target_pairs={{0,16},{8,24},{16,0},{24,8},{1,17},{9,25},{17,1},{25,9},{2,18},{10... | collective-permute-start | bytes 1032200 | tf_op jit(solution)/shard_map/ppermute | solution.py:279
  25.5 20.1 %collective-permute-start.12 = (bf16[6,7,16,256]{3,2,1,0:T(8,128)(2,1)}, bf16[6,7,16,256]{3,2,1,0:T(8,128)(2,1)S(1)}, u32[]{:S(2)}, u32[]{:S(2)}) collective-permute-start(bf16[6,7,16,256]{3,2,1,0:T(8,128)(2,1)} %get-tuple-element.43), channel_id=1, source_target_pairs={{0,24},{8,16},{16,8},{24,0},{1,25},{9,17},{17,9},{25,1},{2,26},{10... | collective-permute-start | bytes 1032200 | tf_op jit(solution)/shard_map/ppermute | solution.py:279
  25.9 9.2 %collective-permute-start = (bf16[16,16,256]{2,1,0:T(8,128)(2,1)}, bf16[16,16,256]{2,1,0:T(8,128)(2,1)S(1)}, u32[]{:S(2)}, u32[]{:S(2)}) collective-permute-start(bf16[16,16,256]{2,1,0:T(8,128)(2,1)} %get-tuple-element.26), channel_id=1, source_target_pairs={{0,7},{1,6},{2,5},{3,4},{4,3},{5,2},{6,1},{7,0},{8,15},{9,14},{10,... | collective-permute-start | bytes 393224 | tf_op jit(solution)/shard_map/ppermute | solution.py:264
  25.9 14.5 %collective-permute-start.1 = (bf16[16,16,256]{2,1,0:T(8,128)(2,1)}, bf16[16,16,256]{2,1,0:T(8,128)(2,1)S(1)}, u32[]{:S(2)}, u32[]{:S(2)}) collective-permute-start(bf16[16,16,256]{2,1,0:T(8,128)(2,1)} %get-tuple-element.27), channel_id=1, source_target_pairs={{0,6},{1,7},{2,4},{3,5},{4,2},{5,3},{6,0},{7,1},{8,14},{9,15},{10,... | collective-permute-start | bytes 393224 | tf_op jit(solution)/shard_map/ppermute | solution.py:264
  29.0 0.7 %copy-start = (bf16[6,7,16,256]{3,2,1,0:T(8,128)(2,1)}, bf16[6,7,16,256]{3,2,1,0:T(8,128)(2,1)S(1)}, u32[]{:S(2)}) copy-start(bf16[6,7,16,256]{3,2,1,0:T(8,128)(2,1)S(1)} %collective-permute-done.7.flat_1_.flat_9_) | copy-start | bytes 1032196
  35.1 5.3 %copy-start.11 = (bf16[16,16,256]{2,1,0:T(8,128)(2,1)}, bf16[16,16,256]{2,1,0:T(8,128)(2,1)S(1)}, u32[]{:S(2)}) copy-start(bf16[16,16,256]{2,1,0:T(8,128)(2,1)S(1)} %collective-permute-done.refs_0_) | copy-start | bytes 393220
  40.4 0.7 %copy-start.12 = (bf16[16,16,256]{2,1,0:T(8,128)(2,1)}, bf16[16,16,256]{2,1,0:T(8,128)(2,1)S(1)}, u32[]{:S(2)}) copy-start(bf16[16,16,256]{2,1,0:T(8,128)(2,1)S(1)} %collective-permute-done.1.refs_1_) | copy-start | bytes 393220
  42.9 9.4 %collective-permute-start.10 = (bf16[2,7,16,256]{3,2,1,0:T(8,128)(2,1)}, bf16[2,7,16,256]{3,2,1,0:T(8,128)(2,1)S(1)}, u32[]{:S(2)}, u32[]{:S(2)}) collective-permute-start(bf16[2,7,16,256]{3,2,1,0:T(8,128)(2,1)} %get-tuple-element.41), channel_id=1, source_target_pairs={{0,8},{8,0},{16,24},{24,16},{1,9},{9,1},{17,25},{25,17},{2,10},{10... | collective-permute-start | bytes 344072 | tf_op jit(solution)/shard_map/ppermute | solution.py:279
  43.9 8.4 %collective-permute-start.8 = (bf16[2,7,16,256]{3,2,1,0:T(8,128)(2,1)}, bf16[2,7,16,256]{3,2,1,0:T(8,128)(2,1)S(1)}, u32[]{:S(2)}, u32[]{:S(2)}) collective-permute-start(bf16[2,7,16,256]{3,2,1,0:T(8,128)(2,1)} %get-tuple-element.38), channel_id=1, source_target_pairs={{0,16},{8,24},{16,0},{24,8},{1,17},{9,25},{17,1},{25,9},{2,18},{10... | collective-permute-start | bytes 344072 | tf_op jit(solution)/shard_map/ppermute | solution.py:279
  45.1 7.2 %collective-permute-start.9 = (bf16[2,7,16,256]{3,2,1,0:T(8,128)(2,1)}, bf16[2,7,16,256]{3,2,1,0:T(8,128)(2,1)S(1)}, u32[]{:S(2)}, u32[]{:S(2)}) collective-permute-start(bf16[2,7,16,256]{3,2,1,0:T(8,128)(2,1)} %get-tuple-element.39), channel_id=1, source_target_pairs={{0,24},{8,16},{16,8},{24,0},{1,25},{9,17},{17,9},{25,1},{2,26},{10... | collective-permute-start | bytes 344072 | tf_op jit(solution)/shard_map/ppermute | solution.py:279
  45.6 0.7 %copy-start.1 = (bf16[6,7,16,256]{3,2,1,0:T(8,128)(2,1)}, bf16[6,7,16,256]{3,2,1,0:T(8,128)(2,1)S(1)}, u32[]{:S(2)}) copy-start(bf16[6,7,16,256]{3,2,1,0:T(8,128)(2,1)S(1)} %collective-permute-done.11.flat_0_.flat_10_) | copy-start | bytes 1032196
  45.6 0.8 %copy-start.2 = (bf16[6,7,16,256]{3,2,1,0:T(8,128)(2,1)}, bf16[6,7,16,256]{3,2,1,0:T(8,128)(2,1)S(1)}, u32[]{:S(2)}) copy-start(bf16[6,7,16,256]{3,2,1,0:T(8,128)(2,1)S(1)} %collective-permute-done.12.flat_1_.flat_11_) | copy-start | bytes 1032196
  52.3 0.6 %copy-start.3 = (bf16[2,7,16,256]{3,2,1,0:T(8,128)(2,1)}, bf16[2,7,16,256]{3,2,1,0:T(8,128)(2,1)S(1)}, u32[]{:S(2)}) copy-start(bf16[2,7,16,256]{3,2,1,0:T(8,128)(2,1)S(1)} %collective-permute-done.10.flat_3_.flat_13_) | copy-start | bytes 344068
  52.3 0.7 %copy-start.4 = (bf16[2,7,16,256]{3,2,1,0:T(8,128)(2,1)}, bf16[2,7,16,256]{3,2,1,0:T(8,128)(2,1)S(1)}, u32[]{:S(2)}) copy-start(bf16[2,7,16,256]{3,2,1,0:T(8,128)(2,1)S(1)} %collective-permute-done.8.flat_0_.flat_14_) | copy-start | bytes 344068
  52.4 0.7 %copy-start.5 = (bf16[2,7,16,256]{3,2,1,0:T(8,128)(2,1)}, bf16[2,7,16,256]{3,2,1,0:T(8,128)(2,1)S(1)}, u32[]{:S(2)}) copy-start(bf16[2,7,16,256]{3,2,1,0:T(8,128)(2,1)S(1)} %collective-permute-done.9.flat_1_.flat_15_) | copy-start | bytes 344068

commit v3 on v2

--- a/solution.py
+++ b/solution.py
@@ -15,7 +15,7 @@
 ANY = pl.BlockSpec(memory_space=pl.ANY)
 SMEM = pl.BlockSpec(memory_space=pltpu.SMEM)
 VMEM = pl.BlockSpec(memory_space=pltpu.VMEM)
-LIMIT = 56 * 1024 * 1024
+LIMIT = 32 * 1024 * 1024
 
 
 def divide(value, by):
@@ -241,7 +241,7 @@
     pages_in_all = groups * block_table.shape[1] // 2
     packed = min(slots, (pages_in_all + groups * (span - 1) - ways * groups * (groups - 1) // 2) // span)
     rounds = [list(reversed(range(3 * ways // 4))), list(reversed(range(3 * ways // 4, ways)))]
-    stages = [[(0, far) for far in range(groups // 2)], [(0, far) for far in range(groups // 2, groups)], [(1, far) for far in range(groups // 2, groups)] + [(1, far) for far in range(groups // 2)]]
+    stages = [[(0, far) for far in range(groups // 2)], [(0, far) for far in range(groups // 2, groups)] + [(1, far) for far in range(groups // 2)], [(1, far) for far in range(groups // 2, groups)]]
     params = pltpu.CompilerParams(vmem_limit_bytes=LIMIT)
     cheap = pl.CostEstimate(flops=0, bytes_accessed=0, transcendentals=0)
 
@@ -257,7 +257,7 @@
         in_specs=[SMEM, SMEM, SMEM, ANY, VMEM],
         out_specs=[VMEM] * ways,
         scratch_shapes=[pltpu.VMEM((packed, page, features), jnp.bfloat16), pltpu.SemaphoreType.DMA((packed,))],
-        compiler_params=params,
+        compiler_params=pltpu.CompilerParams(vmem_limit_bytes=56 * 1024 * 1024),
         cost_estimate=cheap,
     )(hist_pages, owner, block_table, pool, new_rows)
     def along_tp(shift):

time: 58.4 us -> 51.9 us (0.89)
  Pallas kernels: 24.1 us -> 17.3 us
  waiting for transfers between devices: 13.5 us -> 16.9 us
  local copies, waits for them, and re-layouts: 4.23 us -> 0.93 us
    pallas_call x3, Pallas kernels: 16.3 us -> 12.6 us  [attend(): pl.pallas_call(kernel, out_shape=flat_outs, in_specs=jax.tree.leaves(spec...]
    pallas_call x2, Pallas kernels: 4.33 us -> 1.35 us  [sort(): pl.pallas_call(functools.partial(regroup_kernel, (groups, ways, capacity,...]
    ppermute x7, waiting for transfers between devices: 13.5 us -> 16.4 us  [along_tp(): return lax.ppermute(cut[shift], 'tp', [(i, i ^ shift) for i in range(ways)])]
    unnamed x28 -> x10, local copies, waits for them, and re-layouts: 3.59 us -> 0.92 us
    pad x1, local copies, waits for them, and re-layouts: 0.64 us -> 0.01 us  [on_device(): decode_rows = jnp.pad(decode_kv[0], ((0, page - decode), (0, 0)))]
  transfers between devices with their start and end apart: 13 -> 13, of which waited for: 4 -> 5; matrix products, arithmetic and copies ran while one was open for 1% -> 0% of each run, Pallas kernels for 23% -> 19%
where the time goes in v3:
time: 51.9 us; the launch traced here: 51.6 us
  Pallas kernels  17.3 us (33%)
  waiting for transfers between devices  16.9 us (33%)
  starting transfers between devices  15.7 us (30%)
  local copies, waits for them, and re-layouts  0.93 us (2%)
  between operations  0.77 us (1%)
    ppermute x7, waiting for transfers between devices, along_tp(): return lax.ppermute(cut[shift], 'tp', [(i, i ^ shift) for i in range(ways)])  16.4 us
    pallas_call x3, Pallas kernels, attend(): pl.pallas_call(kernel, out_shape=flat_outs, in_specs=jax.tree.leaves(spec...  12.6 us
    ppermute x7, starting transfers between devices, along_tp(): return lax.ppermute(cut[shift], 'tp', [(i, i ^ shift) for i in range(ways)])  8.4 us
    ppermute x6, starting transfers between devices, sort(): lax.ppermute(sent[far], 'grp', [(i, i ^ far) for i in range(groups)])  7.32 us
    pallas_call x1, Pallas kernels, on_device(): pl.pallas_call(functools.partial(pack_kernel, (groups, ways, capacity, pa...  3.41 us
    pallas_call x2, Pallas kernels, sort(): pl.pallas_call(functools.partial(regroup_kernel, (groups, ways, capacity,...  1.35 us
  transfers between devices with their start and end apart: 13, of which 5 were waited for; matrix products, arithmetic and copies ran while one was open for 0% of the time, Pallas kernels for 19%

profile of v3, /device:TPU:17, one launch (start us, length us, event | category | flops | bytes accessed | tf_op | source)
XLA Modules:
  0.0 51.6 jit_solution(5518057013333584122)
XLA Ops:
  0.7 3.4 %shard_map.86 = (bf16[16,16,256]{2,1,0:T(8,128)(2,1)}, bf16[16,16,256]{2,1,0:T(8,128)(2,1)}, bf16[16,16,256]{2,1,0:T(8,128)(2,1)}, bf16[16,16,256]{2,1,0:T(8,128...) custom-call(s32[4]{0:T(128)} %flat_4_.3, ...), custom_call_target="tpu_custom_call" | custom-call | tf_op jit(solution)/shard_map/pallas_call | solution.py:254
  4.1 1.1 %collective-permute-start.2 = (bf16[16,16,256]{2,1,0:T(8,128)(2,1)}, bf16[16,16,256]{2,1,0:T(8,128)(2,1)S(1)}, u32[]{:S(2)}, u32[]{:S(2)}) collective-permute-start(bf16[16,16,256]{2,1,0:T(8,128)(2,1)} %get-tuple-element.28), channel_id=1, source_target_pairs={{0,5},{1,4},{2,7},{3,6},{4,1},{5,0},{6,3},{7,2},{8,13},{9,12},{10,... | collective-permute-start | bytes 393224 | tf_op jit(solution)/shard_map/ppermute | solution.py:264
  5.2 2.3 %collective-permute-start.3 = (bf16[16,16,256]{2,1,0:T(8,128)(2,1)}, bf16[16,16,256]{2,1,0:T(8,128)(2,1)S(1)}, u32[]{:S(2)}, u32[]{:S(2)}) collective-permute-start(bf16[16,16,256]{2,1,0:T(8,128)(2,1)} %get-tuple-element.29), channel_id=1, source_target_pairs={{0,4},{1,5},{2,6},{3,7},{4,0},{5,1},{6,2},{7,3},{8,12},{9,13},{10,... | collective-permute-start | bytes 393224 | tf_op jit(solution)/shard_map/ppermute | solution.py:264
  7.4 1.3 %collective-permute-start.4 = (bf16[16,16,256]{2,1,0:T(8,128)(2,1)}, bf16[16,16,256]{2,1,0:T(8,128)(2,1)S(1)}, u32[]{:S(2)}, u32[]{:S(2)}) collective-permute-start(bf16[16,16,256]{2,1,0:T(8,128)(2,1)} %get-tuple-element.30), channel_id=1, source_target_pairs={{0,3},{1,2},{2,1},{3,0},{4,7},{5,6},{6,5},{7,4},{8,11},{9,10},{10,... | collective-permute-start | bytes 393224 | tf_op jit(solution)/shard_map/ppermute | solution.py:264
  8.7 0.2 collective-permute-start.5
  8.9 1.2 %collective-permute-start.6 = (bf16[16,16,256]{2,1,0:T(8,128)(2,1)}, bf16[16,16,256]{2,1,0:T(8,128)(2,1)S(1)}, u32[]{:S(2)}, u32[]{:S(2)}) collective-permute-start(bf16[16,16,256]{2,1,0:T(8,128)(2,1)} %get-tuple-element.32), channel_id=1, source_target_pairs={{0,1},{1,0},{2,3},{3,2},{4,5},{5,4},{6,7},{7,6},{8,9},{9,8},{10,11... | collective-permute-start | bytes 393224 | tf_op jit(solution)/shard_map/ppermute | solution.py:264
  10.1 2.4 %collective-permute-done.2.refs_0_ = bf16[16,16,256]{2,1,0:T(8,128)(2,1)S(1)} collective-permute-done((bf16[16,16,256]{2,1,0:T(8,128)(2,1)}, bf16[16,16,256]{2,1,0:T(8,128)(2,1)S(1)}, u32[]{:S(2)}, u32[]{:S(2)}) %collective-permute-start.2) | collective-permute-done | bytes 131104 | tf_op jit(solution)/shard_map/ppermute | solution.py:264
  12.5 3.7 %collective-permute-done.3.refs_1_ = bf16[16,16,256]{2,1,0:T(8,128)(2,1)S(1)} collective-permute-done((bf16[16,16,256]{2,1,0:T(8,128)(2,1)}, bf16[16,16,256]{2,1,0:T(8,128)(2,1)S(1)}, u32[]{:S(2)}, u32[]{:S(2)}) %collective-permute-start.3) | collective-permute-done | bytes 131104 | tf_op jit(solution)/shard_map/ppermute | solution.py:264
  16.1 0.0 collective-permute-done.4.refs_2_
  16.1 2.1 %collective-permute-done.5.refs_3_ = bf16[16,16,256]{2,1,0:T(8,128)(2,1)S(1)} collective-permute-done((bf16[16,16,256]{2,1,0:T(8,128)(2,1)}, bf16[16,16,256]{2,1,0:T(8,128)(2,1)S(1)}, u32[]{:S(2)}, u32[]{:S(2)}) %collective-permute-start.5) | collective-permute-done | bytes 131104 | tf_op jit(solution)/shard_map/ppermute | solution.py:264
  18.3 0.0 collective-permute-done.6.refs_4_
  18.3 0.0 copy-start.1
  18.3 0.9 %copy-done.1 = bf16[16,16,256]{2,1,0:T(8,128)(2,1)S(1)} copy-done((bf16[16,16,256]{2,1,0:T(8,128)(2,1)S(1)}, bf16[16,16,256]{2,1,0:T(8,128)(2,1)}, u32[]{:S(2)}) %copy-start.1) | copy-done | bytes 131096
  19.2 0.7 %shard_map.87 = (bf16[6,7,16,256]{3,2,1,0:T(8,128)(2,1)S(1)}, bf16[6,7,16,256]{3,2,1,0:T(8,128)(2,1)S(1)}, bf16[6,7,16,256]{3,2,1,0:T(8,128)(2,1)S(1)}, bf16[6,7...) custom-call(s32[4]{0:T(128)S(1)} %copy-done.2, s32[4]{0:T(128)S(1)} %copy-done.3, ...), custom_call_target="tpu_custom_call" | custom-call | tf_op jit(solution)/shard_map/pallas_call | solution.py:270
  19.9 2.9 %collective-permute-start.7 = (bf16[6,7,16,256]{3,2,1,0:T(8,128)(2,1)S(1)}, bf16[6,7,16,256]{3,2,1,0:T(8,128)(2,1)S(1)}, u32[]{:S(2)}, u32[]{:S(2)}) collective-permute-start(bf16[6,7,16,256]{3,2,1,0:T(8,128)(2,1)S(1)} %get-tuple-element.35), channel_id=1, source_target_pairs={{0,8},{8,0},{16,24},{24,16},{1,9},{9,1},{17,25},{25,17},{2,10},{10... | collective-permute-start | bytes 1032200 | tf_op jit(solution)/shard_map/ppermute | solution.py:279
  22.8 1.3 %collective-permute-start.10 = (bf16[6,7,16,256]{3,2,1,0:T(8,128)(2,1)S(1)}, bf16[6,7,16,256]{3,2,1,0:T(8,128)(2,1)S(1)}, u32[]{:S(2)}, u32[]{:S(2)}) collective-permute-start(bf16[6,7,16,256]{3,2,1,0:T(8,128)(2,1)S(1)} %get-tuple-element.40), channel_id=1, source_target_pairs={{0,16},{8,24},{16,0},{24,8},{1,17},{9,25},{17,1},{25,9},{2,18},{10... | collective-permute-start | bytes 1032200 | tf_op jit(solution)/shard_map/ppermute | solution.py:279
  24.1 0.4 collective-permute-start.11
  24.5 2.4 %collective-permute-start.1 = (bf16[16,16,256]{2,1,0:T(8,128)(2,1)}, bf16[16,16,256]{2,1,0:T(8,128)(2,1)S(1)}, u32[]{:S(2)}, u32[]{:S(2)}) collective-permute-start(bf16[16,16,256]{2,1,0:T(8,128)(2,1)} %get-tuple-element.27), channel_id=1, source_target_pairs={{0,6},{1,7},{2,4},{3,5},{4,2},{5,3},{6,0},{7,1},{8,14},{9,15},{10,... | collective-permute-start | bytes 393224 | tf_op jit(solution)/shard_map/ppermute | solution.py:264
  26.9 0.0 collective-permute-done.7.flat_1_.flat_7_
  26.9 3.8 %shard_map.88 = (f32[1152,128]{1,0:T(8,128)S(1)}, f32[1152,128]{1,0:T(8,128)S(1)}) custom-call(bf16[6,7,16,256]{3,2,1,0:T(8,128)(2,1)S(1)} %get-tuple-element.34.flat_0_.flat_6_, bf16[6,7,16,256]{3,2,1,0:T(8,128)(2,1)S(1)} %collective-permute-done.7.flat_1_.flat_7_, bf16[16,2048]{1,0:T(8,128)(2,1)S(1)} %pad.4.flat_2_, s32[4]{0:T(128)S(1)} %copy-done.2, ...), custom_call_target="tpu_custom_call" | custom-call | tf_op jit(solution)/shard_map/pallas_call | solution.py:318
  30.8 0.0 collective-permute-done.refs_0_
  30.8 8.2 %collective-permute-done.1.refs_1_ = bf16[16,16,256]{2,1,0:T(8,128)(2,1)S(1)} collective-permute-done((bf16[16,16,256]{2,1,0:T(8,128)(2,1)}, bf16[16,16,256]{2,1,0:T(8,128)(2,1)S(1)}, u32[]{:S(2)}, u32[]{:S(2)}) %collective-permute-start.1) | collective-permute-done | bytes 131104 | tf_op jit(solution)/shard_map/ppermute | solution.py:264
  39.0 0.6 %shard_map.89 = (bf16[2,7,16,256]{3,2,1,0:T(8,128)(2,1)S(1)}, bf16[2,7,16,256]{3,2,1,0:T(8,128)(2,1)S(1)}, bf16[2,7,16,256]{3,2,1,0:T(8,128)(2,1)S(1)}, bf16[2,7...) custom-call(s32[4]{0:T(128)S(1)} %copy-done.2, s32[4]{0:T(128)S(1)} %copy-done.3, ...), custom_call_target="tpu_custom_call" | custom-call | tf_op jit(solution)/shard_map/pallas_call | solution.py:270
  39.6 1.0 %collective-permute-start.12 = (bf16[2,7,16,256]{3,2,1,0:T(8,128)(2,1)S(1)}, bf16[2,7,16,256]{3,2,1,0:T(8,128)(2,1)S(1)}, u32[]{:S(2)}, u32[]{:S(2)}) collective-permute-start(bf16[2,7,16,256]{3,2,1,0:T(8,128)(2,1)S(1)} %get-tuple-element.43), channel_id=1, source_target_pairs={{0,8},{8,0},{16,24},{24,16},{1,9},{9,1},{17,25},{25,17},{2,10},{10... | collective-permute-start | bytes 344072 | tf_op jit(solution)/shard_map/ppermute | solution.py:279
  40.7 1.3 %collective-permute-start.8 = (bf16[2,7,16,256]{3,2,1,0:T(8,128)(2,1)S(1)}, bf16[2,7,16,256]{3,2,1,0:T(8,128)(2,1)S(1)}, u32[]{:S(2)}, u32[]{:S(2)}) collective-permute-start(bf16[2,7,16,256]{3,2,1,0:T(8,128)(2,1)S(1)} %get-tuple-element.38), channel_id=1, source_target_pairs={{0,16},{8,24},{16,0},{24,8},{1,17},{9,25},{17,1},{25,9},{2,18},{10... | collective-permute-start | bytes 344072 | tf_op jit(solution)/shard_map/ppermute | solution.py:279
  41.9 0.4 collective-permute-start.9
  42.4 0.0 collective-permute-done.10.flat_0_.flat_8_
  42.4 0.0 collective-permute-done.11.flat_1_.flat_9_
  42.4 5.1 %shard_map.90 = (f32[1152,128]{1,0:T(8,128)S(1)}, f32[1152,128]{1,0:T(8,128)S(1)}) custom-call(bf16[6,7,16,256]{3,2,1,0:T(8,128)(2,1)S(1)} %collective-permute-done.10.flat_0_.flat_8_, bf16[6,7,16,256]{3,2,1,0:T(8,128)(2,1)S(1)} %collective-permute-done.11.flat_1_.flat_9_, bf16[2,7,16,256]{3,2,1,0:T(8,128)(2,1)S(1)} %get-tuple-element.42.flat_2_.flat_10_, ...), custom_call_target="tpu_custom_call" | custom-call | tf_op jit(solution)/shard_map/pallas_call | solution.py:318
  47.5 0.0 collective-permute-done.8.flat_0_.flat_12_
  47.6 0.5 collective-permute-done.9.flat_1_.flat_13_
  48.0 3.6 %shard_map.91 = (bf16[130,1024]{1,0:T(8,128)(2,1)}, bf16[8,16,256]{2,1,0:T(8,128)(2,1)}) custom-call(bf16[2,7,16,256]{3,2,1,0:T(8,128)(2,1)S(1)} %collective-permute-done.8.flat_0_.flat_12_, bf16[2,7,16,256]{3,2,1,0:T(8,128)(2,1)S(1)} %collective-permute-done.9.flat_1_.flat_13_, f32[1152,128]{1,0:T(8,128)S(1)} %get-tuple-element.45.flat_2_, ...), custom_call_target="tpu_custom_call" | custom-call | tf_op jit(solution)/shard_map/pallas_call | solution.py:318
  (11 shorter events, 0.0 us)
Async XLA Ops:
  0.6 17.6 %copy-start.3 = (s32[4]{0:T(128)S(1)}, s32[4]{0:T(128)}, u32[]{:S(2)}) copy-start(s32[4]{0:T(128)} %flat_5_.1) | copy-start | bytes 52
  0.6 17.6 %copy-start.2 = (s32[4]{0:T(128)S(1)}, s32[4]{0:T(128)}, u32[]{:S(2)}) copy-start(s32[4]{0:T(128)} %flat_4_.3) | copy-start | bytes 52
  0.7 26.2 %copy-start.4 = (bf16[1,2,2048]{2,1,0:T(2,128)(2,1)S(1)}, bf16[1,2,2048]{2,1,0:T(2,128)(2,1)}, u32[]{:S(2)}) copy-start(bf16[1,2,2048]{2,1,0:T(2,128)(2,1)} %param.9) | copy-start | bytes 24580
  0.7 26.3 %copy-start = (bf16[1,130,1024]{2,1,0:T(8,128)(2,1)S(1)}, bf16[1,130,1024]{2,1,0:T(8,128)(2,1)}, u32[]{:S(2)}) copy-start(bf16[1,130,1024]{2,1,0:T(8,128)(2,1)} %param.7) | copy-start | bytes 798724
  4.1 8.4 %collective-permute-start.2 = (bf16[16,16,256]{2,1,0:T(8,128)(2,1)}, bf16[16,16,256]{2,1,0:T(8,128)(2,1)S(1)}, u32[]{:S(2)}, u32[]{:S(2)}) collective-permute-start(bf16[16,16,256]{2,1,0:T(8,128)(2,1)} %get-tuple-element.28), channel_id=1, source_target_pairs={{0,5},{1,4},{2,7},{3,6},{4,1},{5,0},{6,3},{7,2},{8,13},{9,12},{10,... | collective-permute-start | bytes 393224 | tf_op jit(solution)/shard_map/ppermute | solution.py:264
  5.2 11.0 %collective-permute-start.3 = (bf16[16,16,256]{2,1,0:T(8,128)(2,1)}, bf16[16,16,256]{2,1,0:T(8,128)(2,1)S(1)}, u32[]{:S(2)}, u32[]{:S(2)}) collective-permute-start(bf16[16,16,256]{2,1,0:T(8,128)(2,1)} %get-tuple-element.29), channel_id=1, source_target_pairs={{0,4},{1,5},{2,6},{3,7},{4,0},{5,1},{6,2},{7,3},{8,12},{9,13},{10,... | collective-permute-start | bytes 393224 | tf_op jit(solution)/shard_map/ppermute | solution.py:264
  7.4 8.7 %collective-permute-start.4 = (bf16[16,16,256]{2,1,0:T(8,128)(2,1)}, bf16[16,16,256]{2,1,0:T(8,128)(2,1)S(1)}, u32[]{:S(2)}, u32[]{:S(2)}) collective-permute-start(bf16[16,16,256]{2,1,0:T(8,128)(2,1)} %get-tuple-element.30), channel_id=1, source_target_pairs={{0,3},{1,2},{2,1},{3,0},{4,7},{5,6},{6,5},{7,4},{8,11},{9,10},{10,... | collective-permute-start | bytes 393224 | tf_op jit(solution)/shard_map/ppermute | solution.py:264
  8.7 9.5 %collective-permute-start.5 = (bf16[16,16,256]{2,1,0:T(8,128)(2,1)}, bf16[16,16,256]{2,1,0:T(8,128)(2,1)S(1)}, u32[]{:S(2)}, u32[]{:S(2)}) collective-permute-start(bf16[16,16,256]{2,1,0:T(8,128)(2,1)} %get-tuple-element.31), channel_id=1, source_target_pairs={{0,2},{1,3},{2,0},{3,1},{4,6},{5,7},{6,4},{7,5},{8,10},{9,11},{10,... | collective-permute-start | bytes 393224 | tf_op jit(solution)/shard_map/ppermute | solution.py:264
  8.9 9.4 %collective-permute-start.6 = (bf16[16,16,256]{2,1,0:T(8,128)(2,1)}, bf16[16,16,256]{2,1,0:T(8,128)(2,1)S(1)}, u32[]{:S(2)}, u32[]{:S(2)}) collective-permute-start(bf16[16,16,256]{2,1,0:T(8,128)(2,1)} %get-tuple-element.32), channel_id=1, source_target_pairs={{0,1},{1,0},{2,3},{3,2},{4,5},{5,4},{6,7},{7,6},{8,9},{9,8},{10,11... | collective-permute-start | bytes 393224 | tf_op jit(solution)/shard_map/ppermute | solution.py:264
  18.3 0.9 %copy-start.1 = (bf16[16,16,256]{2,1,0:T(8,128)(2,1)S(1)}, bf16[16,16,256]{2,1,0:T(8,128)(2,1)}, u32[]{:S(2)}) copy-start(bf16[16,16,256]{2,1,0:T(8,128)(2,1)} %get-tuple-element.33.refs_5_) | copy-start | bytes 393220
  19.9 7.0 %collective-permute-start.7 = (bf16[6,7,16,256]{3,2,1,0:T(8,128)(2,1)S(1)}, bf16[6,7,16,256]{3,2,1,0:T(8,128)(2,1)S(1)}, u32[]{:S(2)}, u32[]{:S(2)}) collective-permute-start(bf16[6,7,16,256]{3,2,1,0:T(8,128)(2,1)S(1)} %get-tuple-element.35), channel_id=1, source_target_pairs={{0,8},{8,0},{16,24},{24,16},{1,9},{9,1},{17,25},{25,17},{2,10},{10... | collective-permute-start | bytes 1032200 | tf_op jit(solution)/shard_map/ppermute | solution.py:279
  22.8 19.6 %collective-permute-start.10 = (bf16[6,7,16,256]{3,2,1,0:T(8,128)(2,1)S(1)}, bf16[6,7,16,256]{3,2,1,0:T(8,128)(2,1)S(1)}, u32[]{:S(2)}, u32[]{:S(2)}) collective-permute-start(bf16[6,7,16,256]{3,2,1,0:T(8,128)(2,1)S(1)} %get-tuple-element.40), channel_id=1, source_target_pairs={{0,16},{8,24},{16,0},{24,8},{1,17},{9,25},{17,1},{25,9},{2,18},{10... | collective-permute-start | bytes 1032200 | tf_op jit(solution)/shard_map/ppermute | solution.py:279
  24.1 18.3 %collective-permute-start.11 = (bf16[6,7,16,256]{3,2,1,0:T(8,128)(2,1)S(1)}, bf16[6,7,16,256]{3,2,1,0:T(8,128)(2,1)S(1)}, u32[]{:S(2)}, u32[]{:S(2)}) collective-permute-start(bf16[6,7,16,256]{3,2,1,0:T(8,128)(2,1)S(1)} %get-tuple-element.41), channel_id=1, source_target_pairs={{0,24},{8,16},{16,8},{24,0},{1,25},{9,17},{17,9},{25,1},{2,26},{10... | collective-permute-start | bytes 1032200 | tf_op jit(solution)/shard_map/ppermute | solution.py:279
  24.5 6.3 %collective-permute-start = (bf16[16,16,256]{2,1,0:T(8,128)(2,1)}, bf16[16,16,256]{2,1,0:T(8,128)(2,1)S(1)}, u32[]{:S(2)}, u32[]{:S(2)}) collective-permute-start(bf16[16,16,256]{2,1,0:T(8,128)(2,1)} %get-tuple-element.26), channel_id=1, source_target_pairs={{0,7},{1,6},{2,5},{3,4},{4,3},{5,2},{6,1},{7,0},{8,15},{9,14},{10,... | collective-permute-start | bytes 393224 | tf_op jit(solution)/shard_map/ppermute | solution.py:264
  24.5 14.5 %collective-permute-start.1 = (bf16[16,16,256]{2,1,0:T(8,128)(2,1)}, bf16[16,16,256]{2,1,0:T(8,128)(2,1)S(1)}, u32[]{:S(2)}, u32[]{:S(2)}) collective-permute-start(bf16[16,16,256]{2,1,0:T(8,128)(2,1)} %get-tuple-element.27), channel_id=1, source_target_pairs={{0,6},{1,7},{2,4},{3,5},{4,2},{5,3},{6,0},{7,1},{8,14},{9,15},{10,... | collective-permute-start | bytes 393224 | tf_op jit(solution)/shard_map/ppermute | solution.py:264
  39.6 2.8 %collective-permute-start.12 = (bf16[2,7,16,256]{3,2,1,0:T(8,128)(2,1)S(1)}, bf16[2,7,16,256]{3,2,1,0:T(8,128)(2,1)S(1)}, u32[]{:S(2)}, u32[]{:S(2)}) collective-permute-start(bf16[2,7,16,256]{3,2,1,0:T(8,128)(2,1)S(1)} %get-tuple-element.43), channel_id=1, source_target_pairs={{0,8},{8,0},{16,24},{24,16},{1,9},{9,1},{17,25},{25,17},{2,10},{10... | collective-permute-start | bytes 344072 | tf_op jit(solution)/shard_map/ppermute | solution.py:279
  40.7 6.9 %collective-permute-start.8 = (bf16[2,7,16,256]{3,2,1,0:T(8,128)(2,1)S(1)}, bf16[2,7,16,256]{3,2,1,0:T(8,128)(2,1)S(1)}, u32[]{:S(2)}, u32[]{:S(2)}) collective-permute-start(bf16[2,7,16,256]{3,2,1,0:T(8,128)(2,1)S(1)} %get-tuple-element.38), channel_id=1, source_target_pairs={{0,16},{8,24},{16,0},{24,8},{1,17},{9,25},{17,1},{25,9},{2,18},{10... | collective-permute-start | bytes 344072 | tf_op jit(solution)/shard_map/ppermute | solution.py:279
  41.9 6.1 %collective-permute-start.9 = (bf16[2,7,16,256]{3,2,1,0:T(8,128)(2,1)S(1)}, bf16[2,7,16,256]{3,2,1,0:T(8,128)(2,1)S(1)}, u32[]{:S(2)}, u32[]{:S(2)}) collective-permute-start(bf16[2,7,16,256]{3,2,1,0:T(8,128)(2,1)S(1)} %get-tuple-element.39), channel_id=1, source_target_pairs={{0,24},{8,16},{16,8},{24,0},{1,25},{9,17},{17,9},{25,1},{2,26},{10... | collective-permute-start | bytes 344072 | tf_op jit(solution)/shard_map/ppermute | solution.py:279

commit v4 on v3

--- a/solution.py
+++ b/solution.py
@@ -111,9 +111,9 @@
 def attend_kernel(dims, refs, rounds, stages, number):
     groups, ways, capacity, packed, page, rows, heads, local_new, decode = dims
     first, last = number == 0, number == len(stages) - 1
-    fresh_round = 0 if first else 1 if last else None
+    fresh_rounds = rounds[:-1] if first else rounds[-1:] if number == 1 else []
     hist_ref, owner_ref, query_ref = refs["hist"], refs["owner"], refs["query"]
-    padded = -(-rows // 16) * 16
+    padded = -(-rows // 8) * 8
     group, rank = lax.axis_index("grp"), lax.axis_index("tp")
     stacked = refs["stacked"]
 
@@ -134,8 +134,8 @@
                     copy.start()
 
     for head in range(heads):
-        stacked[head * padded:head * padded + rows, :] = query_ref[:, head * HD:(head + 1) * HD]
-        stacked[head * padded + rows:(head + 1) * padded, :] = jnp.zeros((padded - rows, HD), jnp.bfloat16)
+        stacked[head * padded:head * padded + rows, :] = query_ref[:, head * HD:(head + 1) * HD].astype(jnp.float32)
+        stacked[head * padded + rows:(head + 1) * padded, :] = jnp.zeros((padded - rows, HD), jnp.float32)
 
     items = [(r, far, i) for r, far in stages[number] for i in range(len(rounds[r]))]
     many = -(-len(items) // -(-len(items) // 12))
@@ -152,11 +152,12 @@
         masks.append(jnp.where(seen, 0.0, FLOOR).astype(jnp.float32))
 
     fresh, fresh_bias = None, None
-    if fresh_round is not None:
-        fresh, shifts = refs["fresh"], rounds[fresh_round]
+    if fresh_rounds:
+        fresh, shifts = refs["fresh"], [shift for shifts in fresh_rounds for shift in shifts]
+        given = [ref.at[i] for shifts, ref in zip(fresh_rounds, refs["rows"]) for i in range(len(shifts))]
         units, known = fresh.shape[0], len(shifts)
         for unit in range(units):
-            fresh[unit] = refs["rows"][unit] if unit < known else jnp.zeros(fresh.shape[1:], jnp.bfloat16)
+            fresh[unit] = given[unit][...] if unit < known else jnp.zeros(fresh.shape[1:], jnp.bfloat16)
         place_of = lax.broadcasted_iota(jnp.int32, (padded, units * page), 1)
         asker = lax.broadcasted_iota(jnp.int32, (padded, units * page), 0)
         inside = remainder(place_of, page)
@@ -192,7 +193,7 @@
     blocks = dict(zip(stages[number], refs["blocks"]))
     for b in range(heads // block_heads):
         at = pl.ds(b * tall, tall)
-        query = stacked[at, :]
+        query = stacked[at, :].astype(jnp.bfloat16)
         if first:
             state = (jnp.zeros((tall, HD), jnp.float32), jnp.full((tall, 1), FLOOR, jnp.float32),
                      jnp.zeros((tall, HD), jnp.float32))
@@ -212,10 +213,10 @@
                 bias = jnp.concatenate([bias] * block_heads, axis=0)
             state = fold(state, query, rows_of(0), rows_of(HD), bias)
         if last:
-            result = (state[2] / state[0]).astype(jnp.bfloat16)
+            result = state[2] / state[0]
             for h in range(block_heads):
                 head = b * block_heads + h
-                refs["out"][:, head * HD:(head + 1) * HD] = result[h * padded:h * padded + rows, :]
+                refs["out"][:, head * HD:(head + 1) * HD] = result[h * padded:h * padded + rows, :].astype(jnp.bfloat16)
         else:
             left = lax.broadcasted_iota(jnp.int32, (tall, HD), 1) < HD // 2
             refs["next"][0][at, :] = jnp.where(left, state[1], state[0])
@@ -241,7 +242,10 @@
     pages_in_all = groups * block_table.shape[1] // 2
     packed = min(slots, (pages_in_all + groups * (span - 1) - ways * groups * (groups - 1) // 2) // span)
     rounds = [list(reversed(range(3 * ways // 4))), list(reversed(range(3 * ways // 4, ways)))]
-    stages = [[(0, far) for far in range(groups // 2)], [(0, far) for far in range(groups // 2, groups)] + [(1, far) for far in range(groups // 2)], [(1, far) for far in range(groups // 2, groups)]]
+    stages = [
+        [(r, far) for r in (0,) for far in range(groups // 2)],
+        [(r, far) for r in (0,) for far in range(groups // 2, groups)] + [(r, far) for r in (1,) for far in range(groups // 2)],
+        [(r, far) for r in (1,) for far in range(groups // 2, groups)]]
     params = pltpu.CompilerParams(vmem_limit_bytes=LIMIT)
     cheap = pl.CostEstimate(flops=0, bytes_accessed=0, transcendentals=0)
 
@@ -264,7 +268,6 @@
         return lax.ppermute(cut[shift], "tp", [(i, i ^ shift) for i in range(ways)])
 
     arrived = {0: cut[0]}
-    arrived.update({shift: along_tp(shift) for shift in sorted(rounds[0]) if shift})
 
     def sort(shifts, before):
         sent = pl.pallas_call(
@@ -280,20 +283,22 @@
                for far in reversed(range(1, groups))}
         return [sent[0]] + [got[far] for far in range(1, groups)], sent[groups]
 
-    tall = heads * (-(-rows // 16) * 16)
+    tall = heads * (-(-rows // 8) * 8)
     def attend(number, carry):
         stage = stages[number]
         first, last = number == 0, number == len(stages) - 1
         args = dict(hist=hist_pages, owner=owner, query=queries[0], blocks=[parts[r][far] for r, far in stage])
         specs = dict(hist=SMEM, owner=SMEM, query=VMEM, blocks=[VMEM] * len(stage))
-        scratch = dict(stacked=pltpu.VMEM((tall, HD), jnp.bfloat16))
+        scratch = dict(stacked=pltpu.VMEM((tall, HD), jnp.float32))
         if first:
             args["decode"], specs["decode"] = decode_rows, VMEM
         if carry is not None:
             args["carry"], specs["carry"] = list(carry), [VMEM] * 2
-        if first or last:
-            args["rows"], specs["rows"] = fresh_rows[0 if first else 1], VMEM
-            scratch["fresh"] = pltpu.VMEM((-(-(len(rounds[0 if first else 1]) + 1) // 8) * 8,) + unit, jnp.bfloat16)
+        if number < 2:
+            args["rows"] = list(fresh_rows) if first else fresh_rows[-1:]
+            specs["rows"] = [VMEM] * len(args["rows"])
+            some = sum(array.shape[0] for array in args["rows"])
+            scratch["fresh"] = pltpu.VMEM((-(-(some + 1) // 8) * 8,) + unit, jnp.bfloat16)
         if last:
             args["parts"], specs["parts"] = parts, [[ANY] * groups for unused in rounds]
             outs = dict(out=jax.ShapeDtypeStruct((rows, heads * HD), jnp.bfloat16),
@@ -327,13 +332,14 @@
         result = jax.tree.unflatten(out_tree, flat)
         return result
 
-    (near_parts, near_fresh) = sort(rounds[0], [])
-    arrived.update({shift: along_tp(shift) for shift in rounds[1]})
-    parts, fresh_rows = [near_parts], [near_fresh]
-    result = attend(0, None)
-    (far_parts, far_fresh) = sort(rounds[1], [result["next"][0]])
-    parts.append(far_parts)
-    fresh_rows.append(far_fresh)
+    parts, fresh_rows, result = [], [], None
+    for shifts in rounds:
+        arrived.update({shift: along_tp(shift) for shift in sorted(shifts) if shift})
+        if shifts == rounds[-1]:
+            result = attend(0, None)
+        sorted_pages, sorted_rows = sort(shifts, [] if result is None else [result["next"][0]])
+        parts.append(sorted_pages)
+        fresh_rows.append(sorted_rows)
     for number in range(1, len(stages)):
         result = attend(number, result["next"])
     returned = result["returned"][:, :local_new, :width].reshape(1, ways * local_new, width)

time: 51.9 us -> 51.4 us (level)
  no operation moved by 1% of the time
where the time goes in v4:
time: 51.4 us; the launch traced here: 51.1 us
  waiting for transfers between devices  16.9 us (33%)
  Pallas kernels  16.8 us (33%)
  starting transfers between devices  15.8 us (31%)
  local copies, waits for them, and re-layouts  0.93 us (2%)
  between operations  0.77 us (1%)
    ppermute x7, waiting for transfers between devices, along_tp(): return lax.ppermute(cut[shift], 'tp', [(i, i ^ shift) for i in range(ways)])  16.5 us
    pallas_call x3, Pallas kernels, attend(): pl.pallas_call(kernel, out_shape=flat_outs, in_specs=jax.tree.leaves(spec...  12.1 us
    ppermute x7, starting transfers between devices, along_tp(): return lax.ppermute(cut[shift], 'tp', [(i, i ^ shift) for i in range(ways)])  8.4 us
    ppermute x6, starting transfers between devices, sort(): lax.ppermute(sent[far], 'grp', [(i, i ^ far) for i in range(groups)])  7.37 us
    pallas_call x1, Pallas kernels, on_device(): pl.pallas_call(functools.partial(pack_kernel, (groups, ways, capacity, pa...  3.41 us
    pallas_call x2, Pallas kernels, sort(): pl.pallas_call(functools.partial(regroup_kernel, (groups, ways, capacity,...  1.35 us
  transfers between devices with their start and end apart: 13, of which 5 were waited for; matrix products, arithmetic and copies ran while one was open for 0% of the time, Pallas kernels for 19%

profile of v4, /device:TPU:17, one launch (start us, length us, event | category | flops | bytes accessed | tf_op | source)
XLA Modules:
  0.0 51.1 jit_solution(9931066602470048082)
XLA Ops:
  0.7 3.4 %shard_map.86 = (bf16[16,16,256]{2,1,0:T(8,128)(2,1)}, bf16[16,16,256]{2,1,0:T(8,128)(2,1)}, bf16[16,16,256]{2,1,0:T(8,128)(2,1)}, bf16[16,16,256]{2,1,0:T(8,128...) custom-call(s32[4]{0:T(128)} %flat_4_.3, ...), custom_call_target="tpu_custom_call" | custom-call | tf_op jit(solution)/shard_map/pallas_call | solution.py:258
  4.1 1.0 %collective-permute-start.2 = (bf16[16,16,256]{2,1,0:T(8,128)(2,1)}, bf16[16,16,256]{2,1,0:T(8,128)(2,1)S(1)}, u32[]{:S(2)}, u32[]{:S(2)}) collective-permute-start(bf16[16,16,256]{2,1,0:T(8,128)(2,1)} %get-tuple-element.28), channel_id=1, source_target_pairs={{0,5},{1,4},{2,7},{3,6},{4,1},{5,0},{6,3},{7,2},{8,13},{9,12},{10,... | collective-permute-start | bytes 393224 | tf_op jit(solution)/shard_map/ppermute | solution.py:268
  5.1 2.3 %collective-permute-start.3 = (bf16[16,16,256]{2,1,0:T(8,128)(2,1)}, bf16[16,16,256]{2,1,0:T(8,128)(2,1)S(1)}, u32[]{:S(2)}, u32[]{:S(2)}) collective-permute-start(bf16[16,16,256]{2,1,0:T(8,128)(2,1)} %get-tuple-element.29), channel_id=1, source_target_pairs={{0,4},{1,5},{2,6},{3,7},{4,0},{5,1},{6,2},{7,3},{8,12},{9,13},{10,... | collective-permute-start | bytes 393224 | tf_op jit(solution)/shard_map/ppermute | solution.py:268
  7.4 1.3 %collective-permute-start.4 = (bf16[16,16,256]{2,1,0:T(8,128)(2,1)}, bf16[16,16,256]{2,1,0:T(8,128)(2,1)S(1)}, u32[]{:S(2)}, u32[]{:S(2)}) collective-permute-start(bf16[16,16,256]{2,1,0:T(8,128)(2,1)} %get-tuple-element.30), channel_id=1, source_target_pairs={{0,3},{1,2},{2,1},{3,0},{4,7},{5,6},{6,5},{7,4},{8,11},{9,10},{10,... | collective-permute-start | bytes 393224 | tf_op jit(solution)/shard_map/ppermute | solution.py:268
  8.7 0.2 collective-permute-start.5
  8.9 1.2 %collective-permute-start.6 = (bf16[16,16,256]{2,1,0:T(8,128)(2,1)}, bf16[16,16,256]{2,1,0:T(8,128)(2,1)S(1)}, u32[]{:S(2)}, u32[]{:S(2)}) collective-permute-start(bf16[16,16,256]{2,1,0:T(8,128)(2,1)} %get-tuple-element.32), channel_id=1, source_target_pairs={{0,1},{1,0},{2,3},{3,2},{4,5},{5,4},{6,7},{7,6},{8,9},{9,8},{10,11... | collective-permute-start | bytes 393224 | tf_op jit(solution)/shard_map/ppermute | solution.py:268
  10.1 2.3 %collective-permute-done.2.refs_0_ = bf16[16,16,256]{2,1,0:T(8,128)(2,1)S(1)} collective-permute-done((bf16[16,16,256]{2,1,0:T(8,128)(2,1)}, bf16[16,16,256]{2,1,0:T(8,128)(2,1)S(1)}, u32[]{:S(2)}, u32[]{:S(2)}) %collective-permute-start.2) | collective-permute-done | bytes 131104 | tf_op jit(solution)/shard_map/ppermute | solution.py:268
  12.4 3.7 %collective-permute-done.3.refs_1_ = bf16[16,16,256]{2,1,0:T(8,128)(2,1)S(1)} collective-permute-done((bf16[16,16,256]{2,1,0:T(8,128)(2,1)}, bf16[16,16,256]{2,1,0:T(8,128)(2,1)S(1)}, u32[]{:S(2)}, u32[]{:S(2)}) %collective-permute-start.3) | collective-permute-done | bytes 131104 | tf_op jit(solution)/shard_map/ppermute | solution.py:268
  16.1 0.0 collective-permute-done.4.refs_2_
  16.1 2.1 %collective-permute-done.5.refs_3_ = bf16[16,16,256]{2,1,0:T(8,128)(2,1)S(1)} collective-permute-done((bf16[16,16,256]{2,1,0:T(8,128)(2,1)}, bf16[16,16,256]{2,1,0:T(8,128)(2,1)S(1)}, u32[]{:S(2)}, u32[]{:S(2)}) %collective-permute-start.5) | collective-permute-done | bytes 131104 | tf_op jit(solution)/shard_map/ppermute | solution.py:268
  18.2 0.0 collective-permute-done.6.refs_4_
  18.2 0.0 copy-start.1
  18.2 0.9 %copy-done.1 = bf16[16,16,256]{2,1,0:T(8,128)(2,1)S(1)} copy-done((bf16[16,16,256]{2,1,0:T(8,128)(2,1)S(1)}, bf16[16,16,256]{2,1,0:T(8,128)(2,1)}, u32[]{:S(2)}) %copy-start.1) | copy-done | bytes 131096
  19.1 0.7 %shard_map.87 = (bf16[6,7,16,256]{3,2,1,0:T(8,128)(2,1)S(1)}, bf16[6,7,16,256]{3,2,1,0:T(8,128)(2,1)S(1)}, bf16[6,7,16,256]{3,2,1,0:T(8,128)(2,1)S(1)}, bf16[6,7...) custom-call(s32[4]{0:T(128)S(1)} %copy-done.2, s32[4]{0:T(128)S(1)} %copy-done.3, ...), custom_call_target="tpu_custom_call" | custom-call | tf_op jit(solution)/shard_map/pallas_call | solution.py:273
  19.9 2.9 %collective-permute-start.7 = (bf16[6,7,16,256]{3,2,1,0:T(8,128)(2,1)S(1)}, bf16[6,7,16,256]{3,2,1,0:T(8,128)(2,1)S(1)}, u32[]{:S(2)}, u32[]{:S(2)}) collective-permute-start(bf16[6,7,16,256]{3,2,1,0:T(8,128)(2,1)S(1)} %get-tuple-element.35), channel_id=1, source_target_pairs={{0,8},{8,0},{16,24},{24,16},{1,9},{9,1},{17,25},{25,17},{2,10},{10... | collective-permute-start | bytes 1032200 | tf_op jit(solution)/shard_map/ppermute | solution.py:282
  22.8 1.3 %collective-permute-start.10 = (bf16[6,7,16,256]{3,2,1,0:T(8,128)(2,1)S(1)}, bf16[6,7,16,256]{3,2,1,0:T(8,128)(2,1)S(1)}, u32[]{:S(2)}, u32[]{:S(2)}) collective-permute-start(bf16[6,7,16,256]{3,2,1,0:T(8,128)(2,1)S(1)} %get-tuple-element.40), channel_id=1, source_target_pairs={{0,16},{8,24},{16,0},{24,8},{1,17},{9,25},{17,1},{25,9},{2,18},{10... | collective-permute-start | bytes 1032200 | tf_op jit(solution)/shard_map/ppermute | solution.py:282
  24.1 0.4 collective-permute-start.11
  24.5 0.0 collective-permute-start
  24.5 2.4 %collective-permute-start.1 = (bf16[16,16,256]{2,1,0:T(8,128)(2,1)}, bf16[16,16,256]{2,1,0:T(8,128)(2,1)S(1)}, u32[]{:S(2)}, u32[]{:S(2)}) collective-permute-start(bf16[16,16,256]{2,1,0:T(8,128)(2,1)} %get-tuple-element.27), channel_id=1, source_target_pairs={{0,6},{1,7},{2,4},{3,5},{4,2},{5,3},{6,0},{7,1},{8,14},{9,15},{10,... | collective-permute-start | bytes 393224 | tf_op jit(solution)/shard_map/ppermute | solution.py:268
  26.9 0.0 collective-permute-done.7.flat_1_.flat_7_
  26.9 3.7 %shard_map.88 = (f32[1088,128]{1,0:T(8,128)S(1)}, f32[1088,128]{1,0:T(8,128)S(1)}) custom-call(bf16[6,7,16,256]{3,2,1,0:T(8,128)(2,1)S(1)} %get-tuple-element.34.flat_0_.flat_6_, bf16[6,7,16,256]{3,2,1,0:T(8,128)(2,1)S(1)} %collective-permute-done.7.flat_1_.flat_7_, bf16[16,2048]{1,0:T(8,128)(2,1)S(1)} %pad.4.flat_2_, s32[4]{0:T(128)S(1)} %copy-done.2, ...), custom_call_target="tpu_custom_call" | custom-call | tf_op jit(solution)/shard_map/pallas_call | solution.py:323
  30.6 0.0 collective-permute-done.refs_0_
  30.6 8.4 %collective-permute-done.1.refs_1_ = bf16[16,16,256]{2,1,0:T(8,128)(2,1)S(1)} collective-permute-done((bf16[16,16,256]{2,1,0:T(8,128)(2,1)}, bf16[16,16,256]{2,1,0:T(8,128)(2,1)S(1)}, u32[]{:S(2)}, u32[]{:S(2)}) %collective-permute-start.1) | collective-permute-done | bytes 131104 | tf_op jit(solution)/shard_map/ppermute | solution.py:268
  39.0 0.6 %shard_map.89 = (bf16[2,7,16,256]{3,2,1,0:T(8,128)(2,1)S(1)}, bf16[2,7,16,256]{3,2,1,0:T(8,128)(2,1)S(1)}, bf16[2,7,16,256]{3,2,1,0:T(8,128)(2,1)S(1)}, bf16[2,7...) custom-call(s32[4]{0:T(128)S(1)} %copy-done.2, s32[4]{0:T(128)S(1)} %copy-done.3, ...), custom_call_target="tpu_custom_call" | custom-call | tf_op jit(solution)/shard_map/pallas_call | solution.py:273
  39.6 1.0 %collective-permute-start.12 = (bf16[2,7,16,256]{3,2,1,0:T(8,128)(2,1)S(1)}, bf16[2,7,16,256]{3,2,1,0:T(8,128)(2,1)S(1)}, u32[]{:S(2)}, u32[]{:S(2)}) collective-permute-start(bf16[2,7,16,256]{3,2,1,0:T(8,128)(2,1)S(1)} %get-tuple-element.43), channel_id=1, source_target_pairs={{0,8},{8,0},{16,24},{24,16},{1,9},{9,1},{17,25},{25,17},{2,10},{10... | collective-permute-start | bytes 344072 | tf_op jit(solution)/shard_map/ppermute | solution.py:282
  40.7 1.3 %collective-permute-start.8 = (bf16[2,7,16,256]{3,2,1,0:T(8,128)(2,1)S(1)}, bf16[2,7,16,256]{3,2,1,0:T(8,128)(2,1)S(1)}, u32[]{:S(2)}, u32[]{:S(2)}) collective-permute-start(bf16[2,7,16,256]{3,2,1,0:T(8,128)(2,1)S(1)} %get-tuple-element.38), channel_id=1, source_target_pairs={{0,16},{8,24},{16,0},{24,8},{1,17},{9,25},{17,1},{25,9},{2,18},{10... | collective-permute-start | bytes 344072 | tf_op jit(solution)/shard_map/ppermute | solution.py:282
  41.9 0.4 collective-permute-start.9
  42.4 0.0 collective-permute-done.10.flat_0_.flat_8_
  42.4 5.3 %shard_map.90 = (f32[1088,128]{1,0:T(8,128)S(1)}, f32[1088,128]{1,0:T(8,128)S(1)}) custom-call(bf16[6,7,16,256]{3,2,1,0:T(8,128)(2,1)S(1)} %collective-permute-done.10.flat_0_.flat_8_, bf16[6,7,16,256]{3,2,1,0:T(8,128)(2,1)S(1)} %collective-permute-done.11.flat_1_.flat_9_, bf16[2,7,16,256]{3,2,1,0:T(8,128)(2,1)S(1)} %get-tuple-element.42.flat_2_.flat_10_, ...), custom_call_target="tpu_custom_call" | custom-call | tf_op jit(solution)/shard_map/pallas_call | solution.py:323
  47.7 0.0 collective-permute-done.8.flat_0_.flat_12_
  47.7 0.3 collective-permute-done.9.flat_1_.flat_13_
  48.0 3.1 %shard_map.91 = (bf16[130,1024]{1,0:T(8,128)(2,1)}, bf16[8,16,256]{2,1,0:T(8,128)(2,1)}) custom-call(bf16[2,7,16,256]{3,2,1,0:T(8,128)(2,1)S(1)} %collective-permute-done.8.flat_0_.flat_12_, bf16[2,7,16,256]{3,2,1,0:T(8,128)(2,1)S(1)} %collective-permute-done.9.flat_1_.flat_13_, f32[1088,128]{1,0:T(8,128)S(1)} %get-tuple-element.46.flat_2_, ...), custom_call_target="tpu_custom_call" | custom-call | tf_op jit(solution)/shard_map/pallas_call | solution.py:323
  (11 shorter events, 0.0 us)
Async XLA Ops:
  0.6 17.6 %copy-start.3 = (s32[4]{0:T(128)S(1)}, s32[4]{0:T(128)}, u32[]{:S(2)}) copy-start(s32[4]{0:T(128)} %flat_5_.1) | copy-start | bytes 52
  0.6 17.6 %copy-start.2 = (s32[4]{0:T(128)S(1)}, s32[4]{0:T(128)}, u32[]{:S(2)}) copy-start(s32[4]{0:T(128)} %flat_4_.3) | copy-start | bytes 52
  0.7 26.2 %copy-start.4 = (bf16[1,2,2048]{2,1,0:T(2,128)(2,1)S(1)}, bf16[1,2,2048]{2,1,0:T(2,128)(2,1)}, u32[]{:S(2)}) copy-start(bf16[1,2,2048]{2,1,0:T(2,128)(2,1)} %param.9) | copy-start | bytes 24580
  0.7 26.3 %copy-start = (bf16[1,130,1024]{2,1,0:T(8,128)(2,1)S(1)}, bf16[1,130,1024]{2,1,0:T(8,128)(2,1)}, u32[]{:S(2)}) copy-start(bf16[1,130,1024]{2,1,0:T(8,128)(2,1)} %param.7) | copy-start | bytes 798724
  4.1 8.3 %collective-permute-start.2 = (bf16[16,16,256]{2,1,0:T(8,128)(2,1)}, bf16[16,16,256]{2,1,0:T(8,128)(2,1)S(1)}, u32[]{:S(2)}, u32[]{:S(2)}) collective-permute-start(bf16[16,16,256]{2,1,0:T(8,128)(2,1)} %get-tuple-element.28), channel_id=1, source_target_pairs={{0,5},{1,4},{2,7},{3,6},{4,1},{5,0},{6,3},{7,2},{8,13},{9,12},{10,... | collective-permute-start | bytes 393224 | tf_op jit(solution)/shard_map/ppermute | solution.py:268
  5.1 11.0 %collective-permute-start.3 = (bf16[16,16,256]{2,1,0:T(8,128)(2,1)}, bf16[16,16,256]{2,1,0:T(8,128)(2,1)S(1)}, u32[]{:S(2)}, u32[]{:S(2)}) collective-permute-start(bf16[16,16,256]{2,1,0:T(8,128)(2,1)} %get-tuple-element.29), channel_id=1, source_target_pairs={{0,4},{1,5},{2,6},{3,7},{4,0},{5,1},{6,2},{7,3},{8,12},{9,13},{10,... | collective-permute-start | bytes 393224 | tf_op jit(solution)/shard_map/ppermute | solution.py:268
  7.4 8.7 %collective-permute-start.4 = (bf16[16,16,256]{2,1,0:T(8,128)(2,1)}, bf16[16,16,256]{2,1,0:T(8,128)(2,1)S(1)}, u32[]{:S(2)}, u32[]{:S(2)}) collective-permute-start(bf16[16,16,256]{2,1,0:T(8,128)(2,1)} %get-tuple-element.30), channel_id=1, source_target_pairs={{0,3},{1,2},{2,1},{3,0},{4,7},{5,6},{6,5},{7,4},{8,11},{9,10},{10,... | collective-permute-start | bytes 393224 | tf_op jit(solution)/shard_map/ppermute | solution.py:268
  8.7 9.5 %collective-permute-start.5 = (bf16[16,16,256]{2,1,0:T(8,128)(2,1)}, bf16[16,16,256]{2,1,0:T(8,128)(2,1)S(1)}, u32[]{:S(2)}, u32[]{:S(2)}) collective-permute-start(bf16[16,16,256]{2,1,0:T(8,128)(2,1)} %get-tuple-element.31), channel_id=1, source_target_pairs={{0,2},{1,3},{2,0},{3,1},{4,6},{5,7},{6,4},{7,5},{8,10},{9,11},{10,... | collective-permute-start | bytes 393224 | tf_op jit(solution)/shard_map/ppermute | solution.py:268
  8.9 9.3 %collective-permute-start.6 = (bf16[16,16,256]{2,1,0:T(8,128)(2,1)}, bf16[16,16,256]{2,1,0:T(8,128)(2,1)S(1)}, u32[]{:S(2)}, u32[]{:S(2)}) collective-permute-start(bf16[16,16,256]{2,1,0:T(8,128)(2,1)} %get-tuple-element.32), channel_id=1, source_target_pairs={{0,1},{1,0},{2,3},{3,2},{4,5},{5,4},{6,7},{7,6},{8,9},{9,8},{10,11... | collective-permute-start | bytes 393224 | tf_op jit(solution)/shard_map/ppermute | solution.py:268
  18.2 0.9 %copy-start.1 = (bf16[16,16,256]{2,1,0:T(8,128)(2,1)S(1)}, bf16[16,16,256]{2,1,0:T(8,128)(2,1)}, u32[]{:S(2)}) copy-start(bf16[16,16,256]{2,1,0:T(8,128)(2,1)} %get-tuple-element.33.refs_5_) | copy-start | bytes 393220
  19.9 7.0 %collective-permute-start.7 = (bf16[6,7,16,256]{3,2,1,0:T(8,128)(2,1)S(1)}, bf16[6,7,16,256]{3,2,1,0:T(8,128)(2,1)S(1)}, u32[]{:S(2)}, u32[]{:S(2)}) collective-permute-start(bf16[6,7,16,256]{3,2,1,0:T(8,128)(2,1)S(1)} %get-tuple-element.35), channel_id=1, source_target_pairs={{0,8},{8,0},{16,24},{24,16},{1,9},{9,1},{17,25},{25,17},{2,10},{10... | collective-permute-start | bytes 1032200 | tf_op jit(solution)/shard_map/ppermute | solution.py:282
  22.8 19.6 %collective-permute-start.10 = (bf16[6,7,16,256]{3,2,1,0:T(8,128)(2,1)S(1)}, bf16[6,7,16,256]{3,2,1,0:T(8,128)(2,1)S(1)}, u32[]{:S(2)}, u32[]{:S(2)}) collective-permute-start(bf16[6,7,16,256]{3,2,1,0:T(8,128)(2,1)S(1)} %get-tuple-element.40), channel_id=1, source_target_pairs={{0,16},{8,24},{16,0},{24,8},{1,17},{9,25},{17,1},{25,9},{2,18},{10... | collective-permute-start | bytes 1032200 | tf_op jit(solution)/shard_map/ppermute | solution.py:282
  24.1 18.3 %collective-permute-start.11 = (bf16[6,7,16,256]{3,2,1,0:T(8,128)(2,1)S(1)}, bf16[6,7,16,256]{3,2,1,0:T(8,128)(2,1)S(1)}, u32[]{:S(2)}, u32[]{:S(2)}) collective-permute-start(bf16[6,7,16,256]{3,2,1,0:T(8,128)(2,1)S(1)} %get-tuple-element.41), channel_id=1, source_target_pairs={{0,24},{8,16},{16,8},{24,0},{1,25},{9,17},{17,9},{25,1},{2,26},{10... | collective-permute-start | bytes 1032200 | tf_op jit(solution)/shard_map/ppermute | solution.py:282
  24.5 6.1 %collective-permute-start = (bf16[16,16,256]{2,1,0:T(8,128)(2,1)}, bf16[16,16,256]{2,1,0:T(8,128)(2,1)S(1)}, u32[]{:S(2)}, u32[]{:S(2)}) collective-permute-start(bf16[16,16,256]{2,1,0:T(8,128)(2,1)} %get-tuple-element.26), channel_id=1, source_target_pairs={{0,7},{1,6},{2,5},{3,4},{4,3},{5,2},{6,1},{7,0},{8,15},{9,14},{10,... | collective-permute-start | bytes 393224 | tf_op jit(solution)/shard_map/ppermute | solution.py:268
  24.5 14.5 %collective-permute-start.1 = (bf16[16,16,256]{2,1,0:T(8,128)(2,1)}, bf16[16,16,256]{2,1,0:T(8,128)(2,1)S(1)}, u32[]{:S(2)}, u32[]{:S(2)}) collective-permute-start(bf16[16,16,256]{2,1,0:T(8,128)(2,1)} %get-tuple-element.27), channel_id=1, source_target_pairs={{0,6},{1,7},{2,4},{3,5},{4,2},{5,3},{6,0},{7,1},{8,14},{9,15},{10,... | collective-permute-start | bytes 393224 | tf_op jit(solution)/shard_map/ppermute | solution.py:268
  39.6 2.8 %collective-permute-start.12 = (bf16[2,7,16,256]{3,2,1,0:T(8,128)(2,1)S(1)}, bf16[2,7,16,256]{3,2,1,0:T(8,128)(2,1)S(1)}, u32[]{:S(2)}, u32[]{:S(2)}) collective-permute-start(bf16[2,7,16,256]{3,2,1,0:T(8,128)(2,1)S(1)} %get-tuple-element.43), channel_id=1, source_target_pairs={{0,8},{8,0},{16,24},{24,16},{1,9},{9,1},{17,25},{25,17},{2,10},{10... | collective-permute-start | bytes 344072 | tf_op jit(solution)/shard_map/ppermute | solution.py:282
  40.7 7.0 %collective-permute-start.8 = (bf16[2,7,16,256]{3,2,1,0:T(8,128)(2,1)S(1)}, bf16[2,7,16,256]{3,2,1,0:T(8,128)(2,1)S(1)}, u32[]{:S(2)}, u32[]{:S(2)}) collective-permute-start(bf16[2,7,16,256]{3,2,1,0:T(8,128)(2,1)S(1)} %get-tuple-element.38), channel_id=1, source_target_pairs={{0,16},{8,24},{16,0},{24,8},{1,17},{9,25},{17,1},{25,9},{2,18},{10... | collective-permute-start | bytes 344072 | tf_op jit(solution)/shard_map/ppermute | solution.py:282
  41.9 6.1 %collective-permute-start.9 = (bf16[2,7,16,256]{3,2,1,0:T(8,128)(2,1)S(1)}, bf16[2,7,16,256]{3,2,1,0:T(8,128)(2,1)S(1)}, u32[]{:S(2)}, u32[]{:S(2)}) collective-permute-start(bf16[2,7,16,256]{3,2,1,0:T(8,128)(2,1)S(1)} %get-tuple-element.39), channel_id=1, source_target_pairs={{0,24},{8,16},{16,8},{24,0},{1,25},{9,17},{17,9},{25,1},{2,26},{10... | collective-permute-start | bytes 344072 | tf_op jit(solution)/shard_map/ppermute | solution.py:282

commit v5 on v4

--- a/solution.py
+++ b/solution.py
@@ -92,6 +92,10 @@
         to, key, value = halves(shift)
         outs[shift][0:packed, :, 0:HD] = stage[:, :, pl.ds(key, HD)]
         outs[shift][0:packed, :, HD:] = stage[:, :, pl.ds(value, HD)]
+
+
+def hold_kernel(own_ref, other_ref, out_ref, same_ref):
+    out_ref[...] = own_ref[...]
 
 
 def regroup_kernel(dims, shifts, hist_ref, owner_ref, *refs):
@@ -243,9 +247,9 @@
     packed = min(slots, (pages_in_all + groups * (span - 1) - ways * groups * (groups - 1) // 2) // span)
     rounds = [list(reversed(range(3 * ways // 4))), list(reversed(range(3 * ways // 4, ways)))]
     stages = [
-        [(r, far) for r in (0,) for far in range(groups // 2)],
-        [(r, far) for r in (0,) for far in range(groups // 2, groups)] + [(r, far) for r in (1,) for far in range(groups // 2)],
-        [(r, far) for r in (1,) for far in range(groups // 2, groups)]]
+        [(0, far) for far in range(groups // 2)],
+        [(0, far) for far in range(groups // 2, groups)],
+        [(1, far) for far in range(groups // 2, groups)] + [(1, far) for far in range(groups // 2)]]
     params = pltpu.CompilerParams(vmem_limit_bytes=LIMIT)
     cheap = pl.CostEstimate(flops=0, bytes_accessed=0, transcendentals=0)
 
@@ -264,6 +268,12 @@
         compiler_params=pltpu.CompilerParams(vmem_limit_bytes=56 * 1024 * 1024),
         cost_estimate=cheap,
     )(hist_pages, owner, block_table, pool, new_rows)
+    cut = list(cut)
+    part = jax.ShapeDtypeStruct((packed + 2,) + unit, jnp.bfloat16)
+    cut[0], cut[1] = pl.pallas_call(
+        hold_kernel, out_shape=[part, part], in_specs=[VMEM, ANY], out_specs=[VMEM, ANY],
+        input_output_aliases={1: 1}, compiler_params=params)(cut[0], cut[1])
+
     def along_tp(shift):
         return lax.ppermute(cut[shift], "tp", [(i, i ^ shift) for i in range(ways)])
 

time: 51.4 us -> 50.4 us (0.981)
  waiting for transfers between devices: 16.9 us -> 15.3 us
  local copies, waits for them, and re-layouts: 0.93 us -> 1.83 us
    ppermute x7, waiting for transfers between devices: 16.5 us -> 14.7 us  [along_tp(): return lax.ppermute(cut[shift], 'tp', [(i, i ^ shift) for i in range(ways)])]
    unnamed x10 -> x12, local copies, waits for them, and re-layouts: 0.92 us -> 1.82 us
  transfers between devices with their start and end apart: 13 -> 13, of which waited for: 5 -> 5; matrix products, arithmetic and copies ran while one was open for 0% -> 0% of each run, Pallas kernels for 19% -> 17%
where the time goes in v5:
time: 50.4 us; the launch traced here: 50.2 us
  Pallas kernels  16.6 us (33%)
  starting transfers between devices  15.6 us (31%)
  waiting for transfers between devices  15.3 us (30%)
  local copies, waits for them, and re-layouts  1.83 us (4%)
  between operations  0.76 us (2%)
    ppermute x7, waiting for transfers between devices, along_tp(): return lax.ppermute(cut[shift], 'tp', [(i, i ^ shift) for i in range(ways)])  14.7 us
    pallas_call x3, Pallas kernels, attend(): pl.pallas_call(kernel, out_shape=flat_outs, in_specs=jax.tree.leaves(spec...  11.8 us
    ppermute x7, starting transfers between devices, along_tp(): return lax.ppermute(cut[shift], 'tp', [(i, i ^ shift) for i in range(ways)])  8.46 us
    ppermute x6, starting transfers between devices, sort(): lax.ppermute(sent[far], 'grp', [(i, i ^ far) for i in range(groups)])  7.17 us
    pallas_call x1, Pallas kernels, on_device(): pl.pallas_call(functools.partial(pack_kernel, (groups, ways, capacity, pa...  3.46 us
    unnamed x12, local copies, waits for them, and re-layouts  1.82 us
    pallas_call x2, Pallas kernels, sort(): pl.pallas_call(functools.partial(regroup_kernel, (groups, ways, capacity,...  1.36 us
  transfers between devices with their start and end apart: 13, of which 5 were waited for; matrix products, arithmetic and copies ran while one was open for 0% of the time, Pallas kernels for 17%

profile of v5, /device:TPU:17, one launch (start us, length us, event | category | flops | bytes accessed | tf_op | source)
XLA Modules:
  0.0 50.2 jit_solution(13990418554466381641)
XLA Ops:
  0.7 3.5 %shard_map.86 = (bf16[16,16,256]{2,1,0:T(8,128)(2,1)}, bf16[16,16,256]{2,1,0:T(8,128)(2,1)}, bf16[16,16,256]{2,1,0:T(8,128)(2,1)}, bf16[16,16,256]{2,1,0:T(8,128...) custom-call(s32[4]{0:T(128)} %flat_6_.1, ...), custom_call_target="tpu_custom_call" | custom-call | tf_op jit(solution)/shard_map/pallas_call | solution.py:262
  4.1 1.0 %collective-permute-start.2 = (bf16[16,16,256]{2,1,0:T(8,128)(2,1)}, bf16[16,16,256]{2,1,0:T(8,128)(2,1)S(1)}, u32[]{:S(2)}, u32[]{:S(2)}) collective-permute-start(bf16[16,16,256]{2,1,0:T(8,128)(2,1)} %get-tuple-element.30), channel_id=1, source_target_pairs={{0,5},{1,4},{2,7},{3,6},{4,1},{5,0},{6,3},{7,2},{8,13},{9,12},{10,... | collective-permute-start | bytes 393224 | tf_op jit(solution)/shard_map/ppermute | solution.py:278
  5.2 2.3 %collective-permute-start.3 = (bf16[16,16,256]{2,1,0:T(8,128)(2,1)}, bf16[16,16,256]{2,1,0:T(8,128)(2,1)S(1)}, u32[]{:S(2)}, u32[]{:S(2)}) collective-permute-start(bf16[16,16,256]{2,1,0:T(8,128)(2,1)} %get-tuple-element.31), channel_id=1, source_target_pairs={{0,4},{1,5},{2,6},{3,7},{4,0},{5,1},{6,2},{7,3},{8,12},{9,13},{10,... | collective-permute-start | bytes 393224 | tf_op jit(solution)/shard_map/ppermute | solution.py:278
  7.5 1.2 %collective-permute-start.4 = (bf16[16,16,256]{2,1,0:T(8,128)(2,1)}, bf16[16,16,256]{2,1,0:T(8,128)(2,1)S(1)}, u32[]{:S(2)}, u32[]{:S(2)}) collective-permute-start(bf16[16,16,256]{2,1,0:T(8,128)(2,1)} %get-tuple-element.32), channel_id=1, source_target_pairs={{0,3},{1,2},{2,1},{3,0},{4,7},{5,6},{6,5},{7,4},{8,11},{9,10},{10,... | collective-permute-start | bytes 393224 | tf_op jit(solution)/shard_map/ppermute | solution.py:278
  8.7 0.2 collective-permute-start.5
  8.9 0.9 %copy-done.1 = bf16[16,16,256]{2,1,0:T(8,128)(2,1)S(1)} copy-done((bf16[16,16,256]{2,1,0:T(8,128)(2,1)S(1)}, bf16[16,16,256]{2,1,0:T(8,128)(2,1)}, u32[]{:S(2)}) %copy-start.1) | copy-done | bytes 131096
  9.8 0.9 %copy-done.2 = bf16[16,16,256]{2,1,0:T(8,128)(2,1)S(1)} copy-done((bf16[16,16,256]{2,1,0:T(8,128)(2,1)S(1)}, bf16[16,16,256]{2,1,0:T(8,128)(2,1)}, u32[]{:S(2)}) %copy-start.2) | copy-done | bytes 131096
  10.8 1.3 %collective-permute-start.6 = (bf16[16,16,256]{2,1,0:T(8,128)(2,1)S(1)}, bf16[16,16,256]{2,1,0:T(8,128)(2,1)S(1)}, u32[]{:S(2)}, u32[]{:S(2)}) collective-permute-start(bf16[16,16,256]{2,1,0:T(8,128)(2,1)S(1)} %get-tuple-element.36), channel_id=1, source_target_pairs={{0,1},{1,0},{2,3},{3,2},{4,5},{5,4},{6,7},{7,6},{8,9},{9,8},{10,11... | collective-permute-start | bytes 393224 | tf_op jit(solution)/shard_map/ppermute | solution.py:278
  12.0 0.5 %collective-permute-done.2.refs_0_ = bf16[16,16,256]{2,1,0:T(8,128)(2,1)S(1)} collective-permute-done((bf16[16,16,256]{2,1,0:T(8,128)(2,1)}, bf16[16,16,256]{2,1,0:T(8,128)(2,1)S(1)}, u32[]{:S(2)}, u32[]{:S(2)}) %collective-permute-start.2) | collective-permute-done | bytes 131104 | tf_op jit(solution)/shard_map/ppermute | solution.py:278
  12.5 3.6 %collective-permute-done.3.refs_1_ = bf16[16,16,256]{2,1,0:T(8,128)(2,1)S(1)} collective-permute-done((bf16[16,16,256]{2,1,0:T(8,128)(2,1)}, bf16[16,16,256]{2,1,0:T(8,128)(2,1)S(1)}, u32[]{:S(2)}, u32[]{:S(2)}) %collective-permute-start.3) | collective-permute-done | bytes 131104 | tf_op jit(solution)/shard_map/ppermute | solution.py:278
  16.2 0.0 collective-permute-done.4.refs_2_
  16.2 2.2 %collective-permute-done.5.refs_3_ = bf16[16,16,256]{2,1,0:T(8,128)(2,1)S(1)} collective-permute-done((bf16[16,16,256]{2,1,0:T(8,128)(2,1)}, bf16[16,16,256]{2,1,0:T(8,128)(2,1)S(1)}, u32[]{:S(2)}, u32[]{:S(2)}) %collective-permute-start.5) | collective-permute-done | bytes 131104 | tf_op jit(solution)/shard_map/ppermute | solution.py:278
  18.4 0.7 %shard_map.88 = (bf16[6,7,16,256]{3,2,1,0:T(8,128)(2,1)S(1)}, bf16[6,7,16,256]{3,2,1,0:T(8,128)(2,1)S(1)}, bf16[6,7,16,256]{3,2,1,0:T(8,128)(2,1)S(1)}, bf16[6,7...) custom-call(s32[4]{0:T(128)S(1)} %copy-done.3, s32[4]{0:T(128)S(1)} %copy-done.4, ...), custom_call_target="tpu_custom_call" | custom-call | tf_op jit(solution)/shard_map/pallas_call | solution.py:283
  19.1 2.8 %collective-permute-start.7 = (bf16[6,7,16,256]{3,2,1,0:T(8,128)(2,1)S(1)}, bf16[6,7,16,256]{3,2,1,0:T(8,128)(2,1)S(1)}, u32[]{:S(2)}, u32[]{:S(2)}) collective-permute-start(bf16[6,7,16,256]{3,2,1,0:T(8,128)(2,1)S(1)} %get-tuple-element.39), channel_id=1, source_target_pairs={{0,8},{8,0},{16,24},{24,16},{1,9},{9,1},{17,25},{25,17},{2,10},{10... | collective-permute-start | bytes 1032200 | tf_op jit(solution)/shard_map/ppermute | solution.py:292
  21.9 1.2 %collective-permute-start.11 = (bf16[6,7,16,256]{3,2,1,0:T(8,128)(2,1)S(1)}, bf16[6,7,16,256]{3,2,1,0:T(8,128)(2,1)S(1)}, u32[]{:S(2)}, u32[]{:S(2)}) collective-permute-start(bf16[6,7,16,256]{3,2,1,0:T(8,128)(2,1)S(1)} %get-tuple-element.46), channel_id=1, source_target_pairs={{0,16},{8,24},{16,0},{24,8},{1,17},{9,25},{17,1},{25,9},{2,18},{10... | collective-permute-start | bytes 1032200 | tf_op jit(solution)/shard_map/ppermute | solution.py:292
  23.1 0.5 collective-permute-start.12
  23.6 0.0 collective-permute-start
  23.6 2.4 %collective-permute-start.1 = (bf16[16,16,256]{2,1,0:T(8,128)(2,1)}, bf16[16,16,256]{2,1,0:T(8,128)(2,1)S(1)}, u32[]{:S(2)}, u32[]{:S(2)}) collective-permute-start(bf16[16,16,256]{2,1,0:T(8,128)(2,1)} %get-tuple-element.29), channel_id=1, source_target_pairs={{0,6},{1,7},{2,4},{3,5},{4,2},{5,3},{6,0},{7,1},{8,14},{9,15},{10,... | collective-permute-start | bytes 393224 | tf_op jit(solution)/shard_map/ppermute | solution.py:278
  26.0 0.0 collective-permute-done.7.flat_1_.flat_9_
  26.1 3.7 %shard_map.89 = (f32[1088,128]{1,0:T(8,128)S(1)}, f32[1088,128]{1,0:T(8,128)S(1)}) custom-call(bf16[6,7,16,256]{3,2,1,0:T(8,128)(2,1)S(1)} %get-tuple-element.38.flat_0_.flat_8_, bf16[6,7,16,256]{3,2,1,0:T(8,128)(2,1)S(1)} %collective-permute-done.7.flat_1_.flat_9_, bf16[16,2048]{1,0:T(8,128)(2,1)S(1)} %pad.4.flat_2_, s32[4]{0:T(128)S(1)} %copy-done.3, ...), custom_call_target="tpu_custom_call" | custom-call | tf_op jit(solution)/shard_map/pallas_call | solution.py:333
  29.7 0.0 collective-permute-done.refs_0_
  29.7 8.4 %collective-permute-done.1.refs_1_ = bf16[16,16,256]{2,1,0:T(8,128)(2,1)S(1)} collective-permute-done((bf16[16,16,256]{2,1,0:T(8,128)(2,1)}, bf16[16,16,256]{2,1,0:T(8,128)(2,1)S(1)}, u32[]{:S(2)}, u32[]{:S(2)}) %collective-permute-start.1) | collective-permute-done | bytes 131104 | tf_op jit(solution)/shard_map/ppermute | solution.py:278
  38.1 0.6 %shard_map.90 = (bf16[2,7,16,256]{3,2,1,0:T(8,128)(2,1)S(1)}, bf16[2,7,16,256]{3,2,1,0:T(8,128)(2,1)S(1)}, bf16[2,7,16,256]{3,2,1,0:T(8,128)(2,1)S(1)}, bf16[2,7...) custom-call(s32[4]{0:T(128)S(1)} %copy-done.3, s32[4]{0:T(128)S(1)} %copy-done.4, ...), custom_call_target="tpu_custom_call" | custom-call | tf_op jit(solution)/shard_map/pallas_call | solution.py:283
  38.8 1.3 %collective-permute-start.8 = (bf16[2,7,16,256]{3,2,1,0:T(8,128)(2,1)S(1)}, bf16[2,7,16,256]{3,2,1,0:T(8,128)(2,1)S(1)}, u32[]{:S(2)}, u32[]{:S(2)}) collective-permute-start(bf16[2,7,16,256]{3,2,1,0:T(8,128)(2,1)S(1)} %get-tuple-element.42), channel_id=1, source_target_pairs={{0,16},{8,24},{16,0},{24,8},{1,17},{9,25},{17,1},{25,9},{2,18},{10... | collective-permute-start | bytes 344072 | tf_op jit(solution)/shard_map/ppermute | solution.py:292
  40.0 1.4 %collective-permute-start.9 = (bf16[2,7,16,256]{3,2,1,0:T(8,128)(2,1)S(1)}, bf16[2,7,16,256]{3,2,1,0:T(8,128)(2,1)S(1)}, u32[]{:S(2)}, u32[]{:S(2)}) collective-permute-start(bf16[2,7,16,256]{3,2,1,0:T(8,128)(2,1)S(1)} %get-tuple-element.43), channel_id=1, source_target_pairs={{0,24},{8,16},{16,8},{24,0},{1,25},{9,17},{17,9},{25,1},{2,26},{10... | collective-permute-start | bytes 344072 | tf_op jit(solution)/shard_map/ppermute | solution.py:292
  41.4 0.0 collective-permute-start.10
  41.4 0.0 collective-permute-done.11.flat_0_.flat_10_
  41.4 0.0 collective-permute-done.12.flat_1_.flat_11_
  41.4 4.3 %shard_map.91 = (f32[1088,128]{1,0:T(8,128)S(1)}, f32[1088,128]{1,0:T(8,128)S(1)}) custom-call(bf16[6,7,16,256]{3,2,1,0:T(8,128)(2,1)S(1)} %collective-permute-done.11.flat_0_.flat_10_, bf16[6,7,16,256]{3,2,1,0:T(8,128)(2,1)S(1)} %collective-permute-done.12.flat_1_.flat_11_, f32[1088,128]{1,0:T(8,128)S(1)} %get-tuple-element.41.refs_2_.flat_2_, ...), custom_call_target="tpu_custom_call" | custom-call | tf_op jit(solution)/shard_map/pallas_call | solution.py:333
  45.7 0.0 collective-permute-done.8.flat_0_.flat_14_
  45.7 0.6 %collective-permute-done.9.flat_1_.flat_15_ = bf16[2,7,16,256]{3,2,1,0:T(8,128)(2,1)S(1)} collective-permute-done((bf16[2,7,16,256]{3,2,1,0:T(8,128)(2,1)S(1)}, bf16[2,7,16,256]{3,2,1,0:T(8,128)(2,1)S(1)}, u32[]{:S(2)}, u32[]{:S(2)}) %collective-permute-start.9) | collective-permute-done | bytes 114720 | tf_op jit(solution)/shard_map/ppermute | solution.py:292
  46.4 3.9 %shard_map.92 = (bf16[130,1024]{1,0:T(8,128)(2,1)}, bf16[8,16,256]{2,1,0:T(8,128)(2,1)}) custom-call(bf16[2,7,16,256]{3,2,1,0:T(8,128)(2,1)S(1)} %collective-permute-done.8.flat_0_.flat_14_, bf16[2,7,16,256]{3,2,1,0:T(8,128)(2,1)S(1)} %collective-permute-done.9.flat_1_.flat_15_, bf16[2,7,16,256]{3,2,1,0:T(8,128)(2,1)S(1)} %get-tuple-element.44.flat_2_.flat_12_, ...), custom_call_target="tpu_custom_call" | custom-call | tf_op jit(solution)/shard_map/pallas_call | solution.py:333
  (14 shorter events, 0.0 us)
Async XLA Ops:
  0.6 17.7 %copy-start.4 = (s32[4]{0:T(128)S(1)}, s32[4]{0:T(128)}, u32[]{:S(2)}) copy-start(s32[4]{0:T(128)} %flat_7_.1) | copy-start | bytes 52
  0.6 17.7 %copy-start.3 = (s32[4]{0:T(128)S(1)}, s32[4]{0:T(128)}, u32[]{:S(2)}) copy-start(s32[4]{0:T(128)} %flat_6_.1) | copy-start | bytes 52
  0.7 25.4 %copy-start.5 = (bf16[1,2,2048]{2,1,0:T(2,128)(2,1)S(1)}, bf16[1,2,2048]{2,1,0:T(2,128)(2,1)}, u32[]{:S(2)}) copy-start(bf16[1,2,2048]{2,1,0:T(2,128)(2,1)} %param.9) | copy-start | bytes 24580
  0.7 25.4 %copy-start = (bf16[1,130,1024]{2,1,0:T(8,128)(2,1)S(1)}, bf16[1,130,1024]{2,1,0:T(8,128)(2,1)}, u32[]{:S(2)}) copy-start(bf16[1,130,1024]{2,1,0:T(8,128)(2,1)} %param.7) | copy-start | bytes 798724
  4.1 8.4 %collective-permute-start.2 = (bf16[16,16,256]{2,1,0:T(8,128)(2,1)}, bf16[16,16,256]{2,1,0:T(8,128)(2,1)S(1)}, u32[]{:S(2)}, u32[]{:S(2)}) collective-permute-start(bf16[16,16,256]{2,1,0:T(8,128)(2,1)} %get-tuple-element.30), channel_id=1, source_target_pairs={{0,5},{1,4},{2,7},{3,6},{4,1},{5,0},{6,3},{7,2},{8,13},{9,12},{10,... | collective-permute-start | bytes 393224 | tf_op jit(solution)/shard_map/ppermute | solution.py:278
  5.2 11.0 %collective-permute-start.3 = (bf16[16,16,256]{2,1,0:T(8,128)(2,1)}, bf16[16,16,256]{2,1,0:T(8,128)(2,1)S(1)}, u32[]{:S(2)}, u32[]{:S(2)}) collective-permute-start(bf16[16,16,256]{2,1,0:T(8,128)(2,1)} %get-tuple-element.31), channel_id=1, source_target_pairs={{0,4},{1,5},{2,6},{3,7},{4,0},{5,1},{6,2},{7,3},{8,12},{9,13},{10,... | collective-permute-start | bytes 393224 | tf_op jit(solution)/shard_map/ppermute | solution.py:278
  7.5 8.7 %collective-permute-start.4 = (bf16[16,16,256]{2,1,0:T(8,128)(2,1)}, bf16[16,16,256]{2,1,0:T(8,128)(2,1)S(1)}, u32[]{:S(2)}, u32[]{:S(2)}) collective-permute-start(bf16[16,16,256]{2,1,0:T(8,128)(2,1)} %get-tuple-element.32), channel_id=1, source_target_pairs={{0,3},{1,2},{2,1},{3,0},{4,7},{5,6},{6,5},{7,4},{8,11},{9,10},{10,... | collective-permute-start | bytes 393224 | tf_op jit(solution)/shard_map/ppermute | solution.py:278
  8.7 9.6 %collective-permute-start.5 = (bf16[16,16,256]{2,1,0:T(8,128)(2,1)}, bf16[16,16,256]{2,1,0:T(8,128)(2,1)S(1)}, u32[]{:S(2)}, u32[]{:S(2)}) collective-permute-start(bf16[16,16,256]{2,1,0:T(8,128)(2,1)} %get-tuple-element.33), channel_id=1, source_target_pairs={{0,2},{1,3},{2,0},{3,1},{4,6},{5,7},{6,4},{7,5},{8,10},{9,11},{10,... | collective-permute-start | bytes 393224 | tf_op jit(solution)/shard_map/ppermute | solution.py:278
  8.9 0.9 %copy-start.1 = (bf16[16,16,256]{2,1,0:T(8,128)(2,1)S(1)}, bf16[16,16,256]{2,1,0:T(8,128)(2,1)}, u32[]{:S(2)}) copy-start(bf16[16,16,256]{2,1,0:T(8,128)(2,1)} %get-tuple-element.34.own_ref) | copy-start | bytes 393220
  9.8 0.9 %copy-start.2 = (bf16[16,16,256]{2,1,0:T(8,128)(2,1)S(1)}, bf16[16,16,256]{2,1,0:T(8,128)(2,1)}, u32[]{:S(2)}) copy-start(bf16[16,16,256]{2,1,0:T(8,128)(2,1)} %get-tuple-element.35.other_ref) | copy-start | bytes 393220
  10.8 7.6 %collective-permute-start.6 = (bf16[16,16,256]{2,1,0:T(8,128)(2,1)S(1)}, bf16[16,16,256]{2,1,0:T(8,128)(2,1)S(1)}, u32[]{:S(2)}, u32[]{:S(2)}) collective-permute-start(bf16[16,16,256]{2,1,0:T(8,128)(2,1)S(1)} %get-tuple-element.36), channel_id=1, source_target_pairs={{0,1},{1,0},{2,3},{3,2},{4,5},{5,4},{6,7},{7,6},{8,9},{9,8},{10,11... | collective-permute-start | bytes 393224 | tf_op jit(solution)/shard_map/ppermute | solution.py:278
  19.1 6.9 %collective-permute-start.7 = (bf16[6,7,16,256]{3,2,1,0:T(8,128)(2,1)S(1)}, bf16[6,7,16,256]{3,2,1,0:T(8,128)(2,1)S(1)}, u32[]{:S(2)}, u32[]{:S(2)}) collective-permute-start(bf16[6,7,16,256]{3,2,1,0:T(8,128)(2,1)S(1)} %get-tuple-element.39), channel_id=1, source_target_pairs={{0,8},{8,0},{16,24},{24,16},{1,9},{9,1},{17,25},{25,17},{2,10},{10... | collective-permute-start | bytes 1032200 | tf_op jit(solution)/shard_map/ppermute | solution.py:292
  21.9 19.5 %collective-permute-start.11 = (bf16[6,7,16,256]{3,2,1,0:T(8,128)(2,1)S(1)}, bf16[6,7,16,256]{3,2,1,0:T(8,128)(2,1)S(1)}, u32[]{:S(2)}, u32[]{:S(2)}) collective-permute-start(bf16[6,7,16,256]{3,2,1,0:T(8,128)(2,1)S(1)} %get-tuple-element.46), channel_id=1, source_target_pairs={{0,16},{8,24},{16,0},{24,8},{1,17},{9,25},{17,1},{25,9},{2,18},{10... | collective-permute-start | bytes 1032200 | tf_op jit(solution)/shard_map/ppermute | solution.py:292
  23.1 18.3 %collective-permute-start.12 = (bf16[6,7,16,256]{3,2,1,0:T(8,128)(2,1)S(1)}, bf16[6,7,16,256]{3,2,1,0:T(8,128)(2,1)S(1)}, u32[]{:S(2)}, u32[]{:S(2)}) collective-permute-start(bf16[6,7,16,256]{3,2,1,0:T(8,128)(2,1)S(1)} %get-tuple-element.47), channel_id=1, source_target_pairs={{0,24},{8,16},{16,8},{24,0},{1,25},{9,17},{17,9},{25,1},{2,26},{10... | collective-permute-start | bytes 1032200 | tf_op jit(solution)/shard_map/ppermute | solution.py:292
  23.6 6.1 %collective-permute-start = (bf16[16,16,256]{2,1,0:T(8,128)(2,1)}, bf16[16,16,256]{2,1,0:T(8,128)(2,1)S(1)}, u32[]{:S(2)}, u32[]{:S(2)}) collective-permute-start(bf16[16,16,256]{2,1,0:T(8,128)(2,1)} %get-tuple-element.28), channel_id=1, source_target_pairs={{0,7},{1,6},{2,5},{3,4},{4,3},{5,2},{6,1},{7,0},{8,15},{9,14},{10,... | collective-permute-start | bytes 393224 | tf_op jit(solution)/shard_map/ppermute | solution.py:278
  23.6 14.5 %collective-permute-start.1 = (bf16[16,16,256]{2,1,0:T(8,128)(2,1)}, bf16[16,16,256]{2,1,0:T(8,128)(2,1)S(1)}, u32[]{:S(2)}, u32[]{:S(2)}) collective-permute-start(bf16[16,16,256]{2,1,0:T(8,128)(2,1)} %get-tuple-element.29), channel_id=1, source_target_pairs={{0,6},{1,7},{2,4},{3,5},{4,2},{5,3},{6,0},{7,1},{8,14},{9,15},{10,... | collective-permute-start | bytes 393224 | tf_op jit(solution)/shard_map/ppermute | solution.py:278
  38.8 7.0 %collective-permute-start.8 = (bf16[2,7,16,256]{3,2,1,0:T(8,128)(2,1)S(1)}, bf16[2,7,16,256]{3,2,1,0:T(8,128)(2,1)S(1)}, u32[]{:S(2)}, u32[]{:S(2)}) collective-permute-start(bf16[2,7,16,256]{3,2,1,0:T(8,128)(2,1)S(1)} %get-tuple-element.42), channel_id=1, source_target_pairs={{0,16},{8,24},{16,0},{24,8},{1,17},{9,25},{17,1},{25,9},{2,18},{10... | collective-permute-start | bytes 344072 | tf_op jit(solution)/shard_map/ppermute | solution.py:292
  40.0 6.3 %collective-permute-start.9 = (bf16[2,7,16,256]{3,2,1,0:T(8,128)(2,1)S(1)}, bf16[2,7,16,256]{3,2,1,0:T(8,128)(2,1)S(1)}, u32[]{:S(2)}, u32[]{:S(2)}) collective-permute-start(bf16[2,7,16,256]{3,2,1,0:T(8,128)(2,1)S(1)} %get-tuple-element.43), channel_id=1, source_target_pairs={{0,24},{8,16},{16,8},{24,0},{1,25},{9,17},{17,9},{25,1},{2,26},{10... | collective-permute-start | bytes 344072 | tf_op jit(solution)/shard_map/ppermute | solution.py:292
  41.4 4.9 %collective-permute-start.10 = (bf16[2,7,16,256]{3,2,1,0:T(8,128)(2,1)S(1)}, bf16[2,7,16,256]{3,2,1,0:T(8,128)(2,1)S(1)}, u32[]{:S(2)}, u32[]{:S(2)}) collective-permute-start(bf16[2,7,16,256]{3,2,1,0:T(8,128)(2,1)S(1)} %get-tuple-element.45), channel_id=1, source_target_pairs={{0,8},{8,0},{16,24},{24,16},{1,9},{9,1},{17,25},{25,17},{2,10},{10... | collective-permute-start | bytes 344072 | tf_op jit(solution)/shard_map/ppermute | solution.py:292

commit v6 on v5

--- a/solution.py
+++ b/solution.py
@@ -137,9 +137,9 @@
                 for copy in homeward[far][1]:
                     copy.start()
 
+    stacked[...] = jnp.zeros_like(stacked)
     for head in range(heads):
         stacked[head * padded:head * padded + rows, :] = query_ref[:, head * HD:(head + 1) * HD].astype(jnp.float32)
-        stacked[head * padded + rows:(head + 1) * padded, :] = jnp.zeros((padded - rows, HD), jnp.float32)
 
     items = [(r, far, i) for r, far in stages[number] for i in range(len(rounds[r]))]
     many = -(-len(items) // -(-len(items) // 12))
@@ -299,7 +299,7 @@
         first, last = number == 0, number == len(stages) - 1
         args = dict(hist=hist_pages, owner=owner, query=queries[0], blocks=[parts[r][far] for r, far in stage])
         specs = dict(hist=SMEM, owner=SMEM, query=VMEM, blocks=[VMEM] * len(stage))
-        scratch = dict(stacked=pltpu.VMEM((tall, HD), jnp.float32))
+        scratch = dict(stacked=pltpu.VMEM((tall + 16, HD), jnp.float32))
         if first:
             args["decode"], specs["decode"] = decode_rows, VMEM
         if carry is not None:

time: 50.4 us -> 50.4 us (level)
  no operation moved by 1% of the time
where the time goes in v6:
time: 50.4 us; the launch traced here: 50.2 us
  Pallas kernels  16.6 us (33%)
  starting transfers between devices  15.7 us (31%)
  waiting for transfers between devices  15.3 us (30%)
  local copies, waits for them, and re-layouts  1.83 us (4%)
  between operations  0.76 us (2%)
    ppermute x7, waiting for transfers between devices, along_tp(): return lax.ppermute(cut[shift], 'tp', [(i, i ^ shift) for i in range(ways)])  14.7 us
    pallas_call x3, Pallas kernels, attend(): pl.pallas_call(kernel, out_shape=flat_outs, in_specs=jax.tree.leaves(spec...  11.8 us
    ppermute x7, starting transfers between devices, along_tp(): return lax.ppermute(cut[shift], 'tp', [(i, i ^ shift) for i in range(ways)])  8.46 us
    ppermute x6, starting transfers between devices, sort(): lax.ppermute(sent[far], 'grp', [(i, i ^ far) for i in range(groups)])  7.21 us
    pallas_call x1, Pallas kernels, on_device(): pl.pallas_call(functools.partial(pack_kernel, (groups, ways, capacity, pa...  3.43 us
    unnamed x12, local copies, waits for them, and re-layouts  1.82 us
    pallas_call x2, Pallas kernels, sort(): pl.pallas_call(functools.partial(regroup_kernel, (groups, ways, capacity,...  1.36 us
  transfers between devices with their start and end apart: 13, of which 5 were waited for; matrix products, arithmetic and copies ran while one was open for 0% of the time, Pallas kernels for 17%

profile of v6, /device:TPU:17, one launch (start us, length us, event | category | flops | bytes accessed | tf_op | source)
XLA Modules:
  0.0 50.2 jit_solution(879461398137773132)
XLA Ops:
  0.7 3.4 %shard_map.86 = (bf16[16,16,256]{2,1,0:T(8,128)(2,1)}, bf16[16,16,256]{2,1,0:T(8,128)(2,1)}, bf16[16,16,256]{2,1,0:T(8,128)(2,1)}, bf16[16,16,256]{2,1,0:T(8,128...) custom-call(s32[4]{0:T(128)} %flat_6_.1, ...), custom_call_target="tpu_custom_call" | custom-call | tf_op jit(solution)/shard_map/pallas_call | solution.py:262
  4.1 1.1 %collective-permute-start.2 = (bf16[16,16,256]{2,1,0:T(8,128)(2,1)}, bf16[16,16,256]{2,1,0:T(8,128)(2,1)S(1)}, u32[]{:S(2)}, u32[]{:S(2)}) collective-permute-start(bf16[16,16,256]{2,1,0:T(8,128)(2,1)} %get-tuple-element.30), channel_id=1, source_target_pairs={{0,5},{1,4},{2,7},{3,6},{4,1},{5,0},{6,3},{7,2},{8,13},{9,12},{10,... | collective-permute-start | bytes 393224 | tf_op jit(solution)/shard_map/ppermute | solution.py:278
  5.2 2.3 %collective-permute-start.3 = (bf16[16,16,256]{2,1,0:T(8,128)(2,1)}, bf16[16,16,256]{2,1,0:T(8,128)(2,1)S(1)}, u32[]{:S(2)}, u32[]{:S(2)}) collective-permute-start(bf16[16,16,256]{2,1,0:T(8,128)(2,1)} %get-tuple-element.31), channel_id=1, source_target_pairs={{0,4},{1,5},{2,6},{3,7},{4,0},{5,1},{6,2},{7,3},{8,12},{9,13},{10,... | collective-permute-start | bytes 393224 | tf_op jit(solution)/shard_map/ppermute | solution.py:278
  7.5 1.3 %collective-permute-start.4 = (bf16[16,16,256]{2,1,0:T(8,128)(2,1)}, bf16[16,16,256]{2,1,0:T(8,128)(2,1)S(1)}, u32[]{:S(2)}, u32[]{:S(2)}) collective-permute-start(bf16[16,16,256]{2,1,0:T(8,128)(2,1)} %get-tuple-element.32), channel_id=1, source_target_pairs={{0,3},{1,2},{2,1},{3,0},{4,7},{5,6},{6,5},{7,4},{8,11},{9,10},{10,... | collective-permute-start | bytes 393224 | tf_op jit(solution)/shard_map/ppermute | solution.py:278
  8.7 0.2 collective-permute-start.5
  8.9 0.9 %copy-done.1 = bf16[16,16,256]{2,1,0:T(8,128)(2,1)S(1)} copy-done((bf16[16,16,256]{2,1,0:T(8,128)(2,1)S(1)}, bf16[16,16,256]{2,1,0:T(8,128)(2,1)}, u32[]{:S(2)}) %copy-start.1) | copy-done | bytes 131096
  9.8 0.9 %copy-done.2 = bf16[16,16,256]{2,1,0:T(8,128)(2,1)S(1)} copy-done((bf16[16,16,256]{2,1,0:T(8,128)(2,1)S(1)}, bf16[16,16,256]{2,1,0:T(8,128)(2,1)}, u32[]{:S(2)}) %copy-start.2) | copy-done | bytes 131096
  10.7 1.3 %collective-permute-start.6 = (bf16[16,16,256]{2,1,0:T(8,128)(2,1)S(1)}, bf16[16,16,256]{2,1,0:T(8,128)(2,1)S(1)}, u32[]{:S(2)}, u32[]{:S(2)}) collective-permute-start(bf16[16,16,256]{2,1,0:T(8,128)(2,1)S(1)} %get-tuple-element.36), channel_id=1, source_target_pairs={{0,1},{1,0},{2,3},{3,2},{4,5},{5,4},{6,7},{7,6},{8,9},{9,8},{10,11... | collective-permute-start | bytes 393224 | tf_op jit(solution)/shard_map/ppermute | solution.py:278
  12.0 0.5 collective-permute-done.2.refs_0_
  12.5 3.7 %collective-permute-done.3.refs_1_ = bf16[16,16,256]{2,1,0:T(8,128)(2,1)S(1)} collective-permute-done((bf16[16,16,256]{2,1,0:T(8,128)(2,1)}, bf16[16,16,256]{2,1,0:T(8,128)(2,1)S(1)}, u32[]{:S(2)}, u32[]{:S(2)}) %collective-permute-start.3) | collective-permute-done | bytes 131104 | tf_op jit(solution)/shard_map/ppermute | solution.py:278
  16.2 0.0 collective-permute-done.4.refs_2_
  16.2 2.2 %collective-permute-done.5.refs_3_ = bf16[16,16,256]{2,1,0:T(8,128)(2,1)S(1)} collective-permute-done((bf16[16,16,256]{2,1,0:T(8,128)(2,1)}, bf16[16,16,256]{2,1,0:T(8,128)(2,1)S(1)}, u32[]{:S(2)}, u32[]{:S(2)}) %collective-permute-start.5) | collective-permute-done | bytes 131104 | tf_op jit(solution)/shard_map/ppermute | solution.py:278
  18.3 0.0 collective-permute-done.6.refs_4_
  18.3 0.7 %shard_map.88 = (bf16[6,7,16,256]{3,2,1,0:T(8,128)(2,1)S(1)}, bf16[6,7,16,256]{3,2,1,0:T(8,128)(2,1)S(1)}, bf16[6,7,16,256]{3,2,1,0:T(8,128)(2,1)S(1)}, bf16[6,7...) custom-call(s32[4]{0:T(128)S(1)} %copy-done.3, s32[4]{0:T(128)S(1)} %copy-done.4, ...), custom_call_target="tpu_custom_call" | custom-call | tf_op jit(solution)/shard_map/pallas_call | solution.py:283
  19.1 2.8 %collective-permute-start.7 = (bf16[6,7,16,256]{3,2,1,0:T(8,128)(2,1)S(1)}, bf16[6,7,16,256]{3,2,1,0:T(8,128)(2,1)S(1)}, u32[]{:S(2)}, u32[]{:S(2)}) collective-permute-start(bf16[6,7,16,256]{3,2,1,0:T(8,128)(2,1)S(1)} %get-tuple-element.39), channel_id=1, source_target_pairs={{0,8},{8,0},{16,24},{24,16},{1,9},{9,1},{17,25},{25,17},{2,10},{10... | collective-permute-start | bytes 1032200 | tf_op jit(solution)/shard_map/ppermute | solution.py:292
  21.9 1.3 %collective-permute-start.11 = (bf16[6,7,16,256]{3,2,1,0:T(8,128)(2,1)S(1)}, bf16[6,7,16,256]{3,2,1,0:T(8,128)(2,1)S(1)}, u32[]{:S(2)}, u32[]{:S(2)}) collective-permute-start(bf16[6,7,16,256]{3,2,1,0:T(8,128)(2,1)S(1)} %get-tuple-element.46), channel_id=1, source_target_pairs={{0,16},{8,24},{16,0},{24,8},{1,17},{9,25},{17,1},{25,9},{2,18},{10... | collective-permute-start | bytes 1032200 | tf_op jit(solution)/shard_map/ppermute | solution.py:292
  23.2 0.5 collective-permute-start.12
  23.6 0.0 collective-permute-start
  23.6 2.4 %collective-permute-start.1 = (bf16[16,16,256]{2,1,0:T(8,128)(2,1)}, bf16[16,16,256]{2,1,0:T(8,128)(2,1)S(1)}, u32[]{:S(2)}, u32[]{:S(2)}) collective-permute-start(bf16[16,16,256]{2,1,0:T(8,128)(2,1)} %get-tuple-element.29), channel_id=1, source_target_pairs={{0,6},{1,7},{2,4},{3,5},{4,2},{5,3},{6,0},{7,1},{8,14},{9,15},{10,... | collective-permute-start | bytes 393224 | tf_op jit(solution)/shard_map/ppermute | solution.py:278
  26.0 0.0 collective-permute-done.7.flat_1_.flat_9_
  26.0 3.7 %shard_map.89 = (f32[1088,128]{1,0:T(8,128)S(1)}, f32[1088,128]{1,0:T(8,128)S(1)}) custom-call(bf16[6,7,16,256]{3,2,1,0:T(8,128)(2,1)S(1)} %get-tuple-element.38.flat_0_.flat_8_, bf16[6,7,16,256]{3,2,1,0:T(8,128)(2,1)S(1)} %collective-permute-done.7.flat_1_.flat_9_, bf16[16,2048]{1,0:T(8,128)(2,1)S(1)} %pad.4.flat_2_, s32[4]{0:T(128)S(1)} %copy-done.3, ...), custom_call_target="tpu_custom_call" | custom-call | tf_op jit(solution)/shard_map/pallas_call | solution.py:333
  29.7 8.4 %collective-permute-done.1.refs_1_ = bf16[16,16,256]{2,1,0:T(8,128)(2,1)S(1)} collective-permute-done((bf16[16,16,256]{2,1,0:T(8,128)(2,1)}, bf16[16,16,256]{2,1,0:T(8,128)(2,1)S(1)}, u32[]{:S(2)}, u32[]{:S(2)}) %collective-permute-start.1) | collective-permute-done | bytes 131104 | tf_op jit(solution)/shard_map/ppermute | solution.py:278
  38.1 0.6 %shard_map.90 = (bf16[2,7,16,256]{3,2,1,0:T(8,128)(2,1)S(1)}, bf16[2,7,16,256]{3,2,1,0:T(8,128)(2,1)S(1)}, bf16[2,7,16,256]{3,2,1,0:T(8,128)(2,1)S(1)}, bf16[2,7...) custom-call(s32[4]{0:T(128)S(1)} %copy-done.3, s32[4]{0:T(128)S(1)} %copy-done.4, ...), custom_call_target="tpu_custom_call" | custom-call | tf_op jit(solution)/shard_map/pallas_call | solution.py:283
  38.8 1.3 %collective-permute-start.8 = (bf16[2,7,16,256]{3,2,1,0:T(8,128)(2,1)S(1)}, bf16[2,7,16,256]{3,2,1,0:T(8,128)(2,1)S(1)}, u32[]{:S(2)}, u32[]{:S(2)}) collective-permute-start(bf16[2,7,16,256]{3,2,1,0:T(8,128)(2,1)S(1)} %get-tuple-element.42), channel_id=1, source_target_pairs={{0,16},{8,24},{16,0},{24,8},{1,17},{9,25},{17,1},{25,9},{2,18},{10... | collective-permute-start | bytes 344072 | tf_op jit(solution)/shard_map/ppermute | solution.py:292
  40.1 1.4 %collective-permute-start.9 = (bf16[2,7,16,256]{3,2,1,0:T(8,128)(2,1)S(1)}, bf16[2,7,16,256]{3,2,1,0:T(8,128)(2,1)S(1)}, u32[]{:S(2)}, u32[]{:S(2)}) collective-permute-start(bf16[2,7,16,256]{3,2,1,0:T(8,128)(2,1)S(1)} %get-tuple-element.43), channel_id=1, source_target_pairs={{0,24},{8,16},{16,8},{24,0},{1,25},{9,17},{17,9},{25,1},{2,26},{10... | collective-permute-start | bytes 344072 | tf_op jit(solution)/shard_map/ppermute | solution.py:292
  41.4 0.0 collective-permute-start.10
  41.4 0.0 collective-permute-done.11.flat_0_.flat_10_
  41.4 0.0 collective-permute-done.12.flat_1_.flat_11_
  41.4 4.3 %shard_map.91 = (f32[1088,128]{1,0:T(8,128)S(1)}, f32[1088,128]{1,0:T(8,128)S(1)}) custom-call(bf16[6,7,16,256]{3,2,1,0:T(8,128)(2,1)S(1)} %collective-permute-done.11.flat_0_.flat_10_, bf16[6,7,16,256]{3,2,1,0:T(8,128)(2,1)S(1)} %collective-permute-done.12.flat_1_.flat_11_, f32[1088,128]{1,0:T(8,128)S(1)} %get-tuple-element.41.refs_2_.flat_2_, ...), custom_call_target="tpu_custom_call" | custom-call | tf_op jit(solution)/shard_map/pallas_call | solution.py:333
  45.7 0.0 collective-permute-done.8.flat_0_.flat_14_
  45.7 0.6 %collective-permute-done.9.flat_1_.flat_15_ = bf16[2,7,16,256]{3,2,1,0:T(8,128)(2,1)S(1)} collective-permute-done((bf16[2,7,16,256]{3,2,1,0:T(8,128)(2,1)S(1)}, bf16[2,7,16,256]{3,2,1,0:T(8,128)(2,1)S(1)}, u32[]{:S(2)}, u32[]{:S(2)}) %collective-permute-start.9) | collective-permute-done | bytes 114720 | tf_op jit(solution)/shard_map/ppermute | solution.py:292
  46.4 3.8 %shard_map.92 = (bf16[130,1024]{1,0:T(8,128)(2,1)}, bf16[8,16,256]{2,1,0:T(8,128)(2,1)}) custom-call(bf16[2,7,16,256]{3,2,1,0:T(8,128)(2,1)S(1)} %collective-permute-done.8.flat_0_.flat_14_, bf16[2,7,16,256]{3,2,1,0:T(8,128)(2,1)S(1)} %collective-permute-done.9.flat_1_.flat_15_, bf16[2,7,16,256]{3,2,1,0:T(8,128)(2,1)S(1)} %get-tuple-element.44.flat_2_.flat_12_, ...), custom_call_target="tpu_custom_call" | custom-call | tf_op jit(solution)/shard_map/pallas_call | solution.py:333
  (14 shorter events, 0.0 us)
Async XLA Ops:
  0.6 17.7 %copy-start.4 = (s32[4]{0:T(128)S(1)}, s32[4]{0:T(128)}, u32[]{:S(2)}) copy-start(s32[4]{0:T(128)} %flat_7_.1) | copy-start | bytes 52
  0.6 17.7 %copy-start.3 = (s32[4]{0:T(128)S(1)}, s32[4]{0:T(128)}, u32[]{:S(2)}) copy-start(s32[4]{0:T(128)} %flat_6_.1) | copy-start | bytes 52
  0.7 25.4 %copy-start.5 = (bf16[1,2,2048]{2,1,0:T(2,128)(2,1)S(1)}, bf16[1,2,2048]{2,1,0:T(2,128)(2,1)}, u32[]{:S(2)}) copy-start(bf16[1,2,2048]{2,1,0:T(2,128)(2,1)} %param.9) | copy-start | bytes 24580
  0.7 25.4 %copy-start = (bf16[1,130,1024]{2,1,0:T(8,128)(2,1)S(1)}, bf16[1,130,1024]{2,1,0:T(8,128)(2,1)}, u32[]{:S(2)}) copy-start(bf16[1,130,1024]{2,1,0:T(8,128)(2,1)} %param.7) | copy-start | bytes 798724
  4.1 8.4 %collective-permute-start.2 = (bf16[16,16,256]{2,1,0:T(8,128)(2,1)}, bf16[16,16,256]{2,1,0:T(8,128)(2,1)S(1)}, u32[]{:S(2)}, u32[]{:S(2)}) collective-permute-start(bf16[16,16,256]{2,1,0:T(8,128)(2,1)} %get-tuple-element.30), channel_id=1, source_target_pairs={{0,5},{1,4},{2,7},{3,6},{4,1},{5,0},{6,3},{7,2},{8,13},{9,12},{10,... | collective-permute-start | bytes 393224 | tf_op jit(solution)/shard_map/ppermute | solution.py:278
  5.2 11.0 %collective-permute-start.3 = (bf16[16,16,256]{2,1,0:T(8,128)(2,1)}, bf16[16,16,256]{2,1,0:T(8,128)(2,1)S(1)}, u32[]{:S(2)}, u32[]{:S(2)}) collective-permute-start(bf16[16,16,256]{2,1,0:T(8,128)(2,1)} %get-tuple-element.31), channel_id=1, source_target_pairs={{0,4},{1,5},{2,6},{3,7},{4,0},{5,1},{6,2},{7,3},{8,12},{9,13},{10,... | collective-permute-start | bytes 393224 | tf_op jit(solution)/shard_map/ppermute | solution.py:278
  7.5 8.7 %collective-permute-start.4 = (bf16[16,16,256]{2,1,0:T(8,128)(2,1)}, bf16[16,16,256]{2,1,0:T(8,128)(2,1)S(1)}, u32[]{:S(2)}, u32[]{:S(2)}) collective-permute-start(bf16[16,16,256]{2,1,0:T(8,128)(2,1)} %get-tuple-element.32), channel_id=1, source_target_pairs={{0,3},{1,2},{2,1},{3,0},{4,7},{5,6},{6,5},{7,4},{8,11},{9,10},{10,... | collective-permute-start | bytes 393224 | tf_op jit(solution)/shard_map/ppermute | solution.py:278
  8.7 9.6 %collective-permute-start.5 = (bf16[16,16,256]{2,1,0:T(8,128)(2,1)}, bf16[16,16,256]{2,1,0:T(8,128)(2,1)S(1)}, u32[]{:S(2)}, u32[]{:S(2)}) collective-permute-start(bf16[16,16,256]{2,1,0:T(8,128)(2,1)} %get-tuple-element.33), channel_id=1, source_target_pairs={{0,2},{1,3},{2,0},{3,1},{4,6},{5,7},{6,4},{7,5},{8,10},{9,11},{10,... | collective-permute-start | bytes 393224 | tf_op jit(solution)/shard_map/ppermute | solution.py:278
  8.9 0.9 %copy-start.1 = (bf16[16,16,256]{2,1,0:T(8,128)(2,1)S(1)}, bf16[16,16,256]{2,1,0:T(8,128)(2,1)}, u32[]{:S(2)}) copy-start(bf16[16,16,256]{2,1,0:T(8,128)(2,1)} %get-tuple-element.34.own_ref) | copy-start | bytes 393220
  9.8 0.9 %copy-start.2 = (bf16[16,16,256]{2,1,0:T(8,128)(2,1)S(1)}, bf16[16,16,256]{2,1,0:T(8,128)(2,1)}, u32[]{:S(2)}) copy-start(bf16[16,16,256]{2,1,0:T(8,128)(2,1)} %get-tuple-element.35.other_ref) | copy-start | bytes 393220
  10.7 7.6 %collective-permute-start.6 = (bf16[16,16,256]{2,1,0:T(8,128)(2,1)S(1)}, bf16[16,16,256]{2,1,0:T(8,128)(2,1)S(1)}, u32[]{:S(2)}, u32[]{:S(2)}) collective-permute-start(bf16[16,16,256]{2,1,0:T(8,128)(2,1)S(1)} %get-tuple-element.36), channel_id=1, source_target_pairs={{0,1},{1,0},{2,3},{3,2},{4,5},{5,4},{6,7},{7,6},{8,9},{9,8},{10,11... | collective-permute-start | bytes 393224 | tf_op jit(solution)/shard_map/ppermute | solution.py:278
  19.1 7.0 %collective-permute-start.7 = (bf16[6,7,16,256]{3,2,1,0:T(8,128)(2,1)S(1)}, bf16[6,7,16,256]{3,2,1,0:T(8,128)(2,1)S(1)}, u32[]{:S(2)}, u32[]{:S(2)}) collective-permute-start(bf16[6,7,16,256]{3,2,1,0:T(8,128)(2,1)S(1)} %get-tuple-element.39), channel_id=1, source_target_pairs={{0,8},{8,0},{16,24},{24,16},{1,9},{9,1},{17,25},{25,17},{2,10},{10... | collective-permute-start | bytes 1032200 | tf_op jit(solution)/shard_map/ppermute | solution.py:292
  21.9 19.5 %collective-permute-start.11 = (bf16[6,7,16,256]{3,2,1,0:T(8,128)(2,1)S(1)}, bf16[6,7,16,256]{3,2,1,0:T(8,128)(2,1)S(1)}, u32[]{:S(2)}, u32[]{:S(2)}) collective-permute-start(bf16[6,7,16,256]{3,2,1,0:T(8,128)(2,1)S(1)} %get-tuple-element.46), channel_id=1, source_target_pairs={{0,16},{8,24},{16,0},{24,8},{1,17},{9,25},{17,1},{25,9},{2,18},{10... | collective-permute-start | bytes 1032200 | tf_op jit(solution)/shard_map/ppermute | solution.py:292
  23.2 18.3 %collective-permute-start.12 = (bf16[6,7,16,256]{3,2,1,0:T(8,128)(2,1)S(1)}, bf16[6,7,16,256]{3,2,1,0:T(8,128)(2,1)S(1)}, u32[]{:S(2)}, u32[]{:S(2)}) collective-permute-start(bf16[6,7,16,256]{3,2,1,0:T(8,128)(2,1)S(1)} %get-tuple-element.47), channel_id=1, source_target_pairs={{0,24},{8,16},{16,8},{24,0},{1,25},{9,17},{17,9},{25,1},{2,26},{10... | collective-permute-start | bytes 1032200 | tf_op jit(solution)/shard_map/ppermute | solution.py:292
  23.6 6.1 %collective-permute-start = (bf16[16,16,256]{2,1,0:T(8,128)(2,1)}, bf16[16,16,256]{2,1,0:T(8,128)(2,1)S(1)}, u32[]{:S(2)}, u32[]{:S(2)}) collective-permute-start(bf16[16,16,256]{2,1,0:T(8,128)(2,1)} %get-tuple-element.28), channel_id=1, source_target_pairs={{0,7},{1,6},{2,5},{3,4},{4,3},{5,2},{6,1},{7,0},{8,15},{9,14},{10,... | collective-permute-start | bytes 393224 | tf_op jit(solution)/shard_map/ppermute | solution.py:278
  23.6 14.5 %collective-permute-start.1 = (bf16[16,16,256]{2,1,0:T(8,128)(2,1)}, bf16[16,16,256]{2,1,0:T(8,128)(2,1)S(1)}, u32[]{:S(2)}, u32[]{:S(2)}) collective-permute-start(bf16[16,16,256]{2,1,0:T(8,128)(2,1)} %get-tuple-element.29), channel_id=1, source_target_pairs={{0,6},{1,7},{2,4},{3,5},{4,2},{5,3},{6,0},{7,1},{8,14},{9,15},{10,... | collective-permute-start | bytes 393224 | tf_op jit(solution)/shard_map/ppermute | solution.py:278
  38.8 7.0 %collective-permute-start.8 = (bf16[2,7,16,256]{3,2,1,0:T(8,128)(2,1)S(1)}, bf16[2,7,16,256]{3,2,1,0:T(8,128)(2,1)S(1)}, u32[]{:S(2)}, u32[]{:S(2)}) collective-permute-start(bf16[2,7,16,256]{3,2,1,0:T(8,128)(2,1)S(1)} %get-tuple-element.42), channel_id=1, source_target_pairs={{0,16},{8,24},{16,0},{24,8},{1,17},{9,25},{17,1},{25,9},{2,18},{10... | collective-permute-start | bytes 344072 | tf_op jit(solution)/shard_map/ppermute | solution.py:292
  40.1 6.3 %collective-permute-start.9 = (bf16[2,7,16,256]{3,2,1,0:T(8,128)(2,1)S(1)}, bf16[2,7,16,256]{3,2,1,0:T(8,128)(2,1)S(1)}, u32[]{:S(2)}, u32[]{:S(2)}) collective-permute-start(bf16[2,7,16,256]{3,2,1,0:T(8,128)(2,1)S(1)} %get-tuple-element.43), channel_id=1, source_target_pairs={{0,24},{8,16},{16,8},{24,0},{1,25},{9,17},{17,9},{25,1},{2,26},{10... | collective-permute-start | bytes 344072 | tf_op jit(solution)/shard_map/ppermute | solution.py:292
  41.4 4.9 %collective-permute-start.10 = (bf16[2,7,16,256]{3,2,1,0:T(8,128)(2,1)S(1)}, bf16[2,7,16,256]{3,2,1,0:T(8,128)(2,1)S(1)}, u32[]{:S(2)}, u32[]{:S(2)}) collective-permute-start(bf16[2,7,16,256]{3,2,1,0:T(8,128)(2,1)S(1)} %get-tuple-element.45), channel_id=1, source_target_pairs={{0,8},{8,0},{16,24},{24,16},{1,9},{9,1},{17,25},{25,17},{2,10},{10... | collective-permute-start | bytes 344072 | tf_op jit(solution)/shard_map/ppermute | solution.py:292
